TPU v7x, 32 devices: a whole 2x2x4 slice. The times are simulated.
32 devices in a mesh: stream: 4 (over y, x), seq: 8 (over z, core).
Axes of the slice: x: 2, y: 2, z: 4, core: 2. Of those that a mesh axis runs over, the one named last changes fastest.
Arguments:
- tokens: bfloat16 [4, 8192, 768], P('stream', 'seq'), may hold values from -6 to 6
- global_states: bfloat16 [4, 256, 768], P('stream', 'seq'), may hold values from -6 to 6
- cotangent: bfloat16 [4, 8192, 768], P('stream', 'seq'), may hold values from -6 to 6
- w_qkv: bfloat16 [768, 2304], replicated, may hold values from -0.21875 to 0.21875
- w_out: bfloat16 [768, 768], replicated, may hold values from -1.75 to 1.75
- w_up: bfloat16 [768, 3072], replicated, may hold values from -0.21875 to 0.21875
- w_down: bfloat16 [3072, 768], replicated, may hold values from -0.109375 to 0.109375
- first_gain: float32 [768], replicated, may hold values from 0.5 to 1.5
- first_shift: float32 [768], replicated, may hold values from -3 to 3
- second_gain: float32 [768], replicated, may hold values from 0.5 to 1.5
- second_shift: float32 [768], replicated, may hold values from -3 to 3
- rich_query: float32 [4, 768], replicated, may hold values from -0.75 to 0.75
- rich_key: float32 [4, 768], replicated, may hold values from -0.75 to 0.75
- rich_bias: float32 [4, 12], replicated, may hold values from 0.5 to 3.5
- rich_theta: float32 [2, 12], replicated, may hold values from 0.3 to 0.8
- bucket_units: int32 [4, 4], P('stream'), may hold values from 1 to 4, as said below
- form_lengths: int32 [4, 4], P('stream'), may hold values from 128 to 4608, as said below
- coords: int32 [4, 2, 8192], P('stream'), may hold values from 0 to 99
- glob_owner: int32 [4, 256], P('stream'), may hold values from 0 to 3, as said below
Outputs:
- layer_out: bfloat16 [4, 8192, 768], P('stream', 'seq')
- tokens_grad: bfloat16 [4, 8192, 768], P('stream', 'seq')
- glob_grad: bfloat16 [4, 256, 768], P('stream', 'seq')
- w_qkv_grad: float32 [768, 2304], P('seq')
- w_out_grad: float32 [768, 768], P('seq')
- w_up_grad: float32 [768, 3072], P('seq')
- w_down_grad: float32 [3072, 768], P('seq')
- first_gain_grad: float32 [768], P('seq')
- first_shift_grad: float32 [768], P('seq')
- second_gain_grad: float32 [768], P('seq')
- second_shift_grad: float32 [768], P('seq')
- rich_query_grad: float32 [4, 768], P(None, 'seq')
- rich_key_grad: float32 [4, 768], P(None, 'seq')
- rich_bias_grad: float32 [4, 12], replicated
- rich_theta_grad: float32 [2, 12], replicated
Inputs may be any that keep to these rules, and one draw needn't show every extreme that they name: `bucket_units`: per stream the 4 values sum to 8; each stream has one value 4. form_lengths[s, f] is at most the size of bucket f of stream s (steps' starts[f+1] - starts[f], the last one ending at 8192) and at least that size minus 1024 // 2 plus 128. `glob_owner`: every form of a stream owns exactly 64 of that stream's global tokens.
All inputs are finite; a program needn't handle non-finite values.
Results may differ from a plain program's by a relative error of at most 0.019.
Values may be sent and summed in bfloat16 or wider, within the bound.
No kernel may reach another device: no remote copies, remote signals or barrier semaphores. Data moves between devices by JAX's collectives and lax.ppermute only.
A program may use at most 256 MiB of HBM per device.

v0:
```python
from functools import partial

import jax
import jax.numpy as jnp
from jax import lax
from jax.sharding import PartitionSpec as P

RADIUS = 128
GLOB_FORM = 64
QBLOCK = 512
TOK_DEV = 1024


EPSILON = 1e-06
NEGATIVE = -1e30
HIGHEST = lax.Precision.HIGHEST


def padded(shard, sides, width):
    for axis, dim in sides:
        peers, length = (lax.axis_size(axis), shard.shape[dim])
        up = [(i, (i + 1) % peers) for i in range(peers - 1)]
        down = [(j, i) for i, j in up]
        last = lax.slice_in_dim(shard, length - width, length, axis=dim)
        first = lax.slice_in_dim(shard, 0, width, axis=dim)
        before = lax.ppermute(last, axis, up)
        after = lax.ppermute(first, axis, down)
        shard = jnp.concatenate([before, shard, after], axis=dim)
    return shard


def layer_norm(values, norm_gain, norm_shift):
    centre = jnp.mean(values, axis=-1, keepdims=True)
    centred = values - centre
    spread = jnp.mean(centred * centred, axis=-1, keepdims=True)
    return centred * lax.rsqrt(spread + EPSILON) * norm_gain + norm_shift


def gelu_exact(values):
    return jax.nn.gelu(values, approximate=False)


def bucket_starts(unit_counts):
    position = jnp.arange(unit_counts.shape[0], dtype=jnp.int32)
    before = jnp.cumsum(unit_counts) - unit_counts
    return jnp.where(position == 0, 0, TOK_DEV // 2 + TOK_DEV * before)


def locate(position, starts, lengths, stream_len):
    form_count = starts.shape[0]
    form_index = jnp.sum((position[:, None] >= starts[None, 1:]).astype(jnp.int32), axis=1)
    chosen = form_index[:, None] == jnp.arange(form_count, dtype=jnp.int32)[None, :]
    first_row = jnp.sum(jnp.where(chosen, starts[None, :], 0), axis=1)
    live_rows = jnp.sum(jnp.where(chosen, lengths[None, :], 0), axis=1)
    is_live = (position >= 0) & (position < stream_len) & (position - first_row < live_rows)
    return (form_index, is_live)


def geometry(coord_query, coord_key):
    ahead_sign = jnp.where(coord_key[:, None, :] > coord_query[:, :, None], 1.0, -1.0).astype(
        jnp.float32
    )
    log_apart = jnp.log1p(
        jnp.abs(coord_query[:, :, None] - coord_key[:, None, :]).astype(jnp.float32)
    )
    return (ahead_sign[0], ahead_sign[1], log_apart[0], log_apart[1])


def rich_terms(query_rich, key_rich, rich_shift, rich_width, pair_geometry):
    sign_x, sign_y, dist_x, dist_y = pair_geometry

    def summed(column):
        return query_rich[column][:, None] + key_rich[column][None, :] + rich_shift[column]

    ordered = -jax.nn.softplus(-sign_x * summed(0)) - jax.nn.softplus(-sign_y * summed(1))
    gap_x = dist_x - summed(2)
    gap_y = dist_y - summed(3)
    return (
        ordered
        - 0.5 * rich_width[0] * rich_width[0] * gap_x * gap_x
        - 0.5 * rich_width[1] * rich_width[1] * gap_y * gap_y
    )


def head_scores(
    query_head,
    key_head,
    glob_key_head,
    query_rich,
    key_rich,
    rich_shift,
    rich_width,
    pair_geometry,
    near_mask,
    far_mask,
):
    near_part = (
        jnp.einsum("qe,ke->qk", query_head, key_head, preferred_element_type=jnp.float32) * 0.125
    )
    near_part = near_part + rich_terms(query_rich, key_rich, rich_shift, rich_width, pair_geometry)
    far_part = (
        jnp.einsum("qe,ge->qg", query_head, glob_key_head, preferred_element_type=jnp.float32)
        * 0.125
    )
    return jnp.concatenate(
        [jnp.where(near_mask, near_part, NEGATIVE), jnp.where(far_mask, far_part, NEGATIVE)], axis=1
    )


def body(
    tokens,
    global_states,
    cotangent,
    w_qkv,
    w_out,
    w_up,
    w_down,
    first_gain,
    first_shift,
    second_gain,
    second_shift,
    rich_query,
    rich_key,
    rich_bias,
    rich_theta,
    bucket_units,
    form_lengths,
    coords,
    glob_owner,
):
    row_count = tokens.shape[1]
    model_width = tokens.shape[2]
    head_count = rich_bias.shape[1]
    head_dim = model_width // head_count
    stream_len = row_count * lax.axis_size("seq")
    offset = lax.axis_index("seq") * row_count
    band_span = QBLOCK + 2 * RADIUS
    block_count = row_count // QBLOCK
    starts = bucket_starts(bucket_units[0])
    lengths = form_lengths[0]
    coord_pad = jnp.pad(coords[0], ((0, 0), (RADIUS, RADIUS)))
    glob_order = jnp.argsort(glob_owner[0], stable=True)
    glob_count = glob_order.shape[0]

    def split_heads(block_rows):
        return block_rows.reshape(block_rows.shape[0], head_count, head_dim).transpose(1, 0, 2)

    def join_heads(stacked):
        return stacked.transpose(1, 0, 2).reshape(stacked.shape[1], model_width)

    inputs = tokens[0].astype(jnp.float32)
    norm_first, pull_first = jax.vjp(layer_norm, inputs, first_gain, first_shift)
    hidden_one = norm_first.astype(jnp.bfloat16)
    projected = jnp.dot(hidden_one, w_qkv, preferred_element_type=jnp.float32).astype(jnp.bfloat16)
    queries = projected[:, :model_width]
    stacked_pairs = jnp.stack(
        [projected[:, model_width : 2 * model_width], projected[:, 2 * model_width :]]
    )
    padded_pairs = padded(stacked_pairs, (("seq", 1),), RADIUS)
    key_pad = padded_pairs[0]
    value_pad = padded_pairs[1]
    glob_norm, pull_glob = jax.vjp(
        layer_norm, global_states[0].astype(jnp.float32), first_gain, first_shift
    )
    glob_hidden = glob_norm.astype(jnp.bfloat16)
    w_pair = w_qkv[:, model_width:]
    local_pairs = jnp.dot(glob_hidden, w_pair, preferred_element_type=jnp.float32).astype(
        jnp.bfloat16
    )
    glob_pairs = lax.all_gather(local_pairs, "seq", axis=0, tiled=True)
    glob_keys = glob_pairs[:, :model_width]
    glob_values = glob_pairs[:, model_width:]
    query_float = queries.astype(jnp.float32)
    key_float = key_pad.astype(jnp.float32)
    query_vectors = rich_query.reshape(4, head_count, head_dim)
    key_vectors = rich_key.reshape(4, head_count, head_dim)
    query_rich_all = jnp.einsum(
        "she,che->chs",
        query_float.reshape(row_count, head_count, head_dim),
        query_vectors,
        precision=HIGHEST,
    )
    key_rich_all = jnp.einsum(
        "she,che->chs",
        key_float.reshape(row_count + 2 * RADIUS, head_count, head_dim),
        key_vectors,
        precision=HIGHEST,
    )
    shift_heads = rich_bias.T
    width_heads = rich_theta.T

    def block_inputs(block_index):
        first_row = block_index * QBLOCK
        pos_query = offset + first_row + jnp.arange(QBLOCK, dtype=jnp.int32)
        pos_key = offset + first_row - RADIUS + jnp.arange(band_span, dtype=jnp.int32)
        form_query = locate(pos_query, starts, lengths, stream_len)[0]
        form_key, live_key = locate(pos_key, starts, lengths, stream_len)
        near_mask = (
            live_key[None, :]
            & (form_key[None, :] == form_query[:, None])
            & (jnp.abs(pos_query[:, None] - pos_key[None, :]) <= RADIUS)
        )
        coord_query = lax.dynamic_slice_in_dim(coord_pad, offset + first_row + RADIUS, QBLOCK, 1)
        coord_key = lax.dynamic_slice_in_dim(coord_pad, offset + first_row, band_span, 1)
        pair_geometry = geometry(coord_query, coord_key)
        form_low = form_query[0]
        form_high = form_query[QBLOCK - 1]
        picked = jnp.concatenate(
            [
                lax.dynamic_slice_in_dim(glob_order, form_low * GLOB_FORM, GLOB_FORM),
                lax.dynamic_slice_in_dim(glob_order, form_high * GLOB_FORM, GLOB_FORM),
            ]
        )
        low_side = jnp.broadcast_to((form_query == form_low)[:, None], (QBLOCK, GLOB_FORM))
        high_side = jnp.broadcast_to(
            ((form_query == form_high) & (form_high != form_low))[:, None], (QBLOCK, GLOB_FORM)
        )
        far_mask = jnp.concatenate([low_side, high_side], axis=1)
        head_items = (
            split_heads(lax.dynamic_slice_in_dim(queries, first_row, QBLOCK, 0)),
            split_heads(lax.dynamic_slice_in_dim(key_pad, first_row, band_span, 0)),
            split_heads(lax.dynamic_slice_in_dim(value_pad, first_row, band_span, 0)),
            split_heads(jnp.take(glob_keys, picked, axis=0)),
            split_heads(jnp.take(glob_values, picked, axis=0)),
            lax.dynamic_slice_in_dim(query_rich_all, first_row, QBLOCK, 2).transpose(1, 0, 2),
            lax.dynamic_slice_in_dim(key_rich_all, first_row, band_span, 2).transpose(1, 0, 2),
            shift_heads,
            width_heads,
        )
        return (head_items, (pair_geometry, near_mask, far_mask), picked, first_row)

    def forward_block(block_index):
        head_items, shared, picked, first_row = block_inputs(block_index)

        def forward_one_head(items):
            (
                query_head,
                key_head,
                value_head,
                glob_key_head,
                glob_value_head,
                query_rich,
                key_rich,
                rich_shift,
                rich_width,
            ) = items
            scores = head_scores(
                query_head,
                key_head,
                glob_key_head,
                query_rich,
                key_rich,
                rich_shift,
                rich_width,
                shared[0],
                shared[1],
                shared[2],
            )
            row_max = jnp.max(scores, axis=1, keepdims=True)
            exp_scores = jnp.exp(scores - row_max)
            row_total = jnp.sum(exp_scores, axis=1, keepdims=True)
            attn_probs = (exp_scores / row_total).astype(jnp.bfloat16)
            context = jnp.einsum(
                "qk,ke->qe",
                attn_probs[:, :band_span],
                value_head,
                preferred_element_type=jnp.float32,
            ) + jnp.einsum(
                "qg,ge->qe",
                attn_probs[:, band_span:],
                glob_value_head,
                preferred_element_type=jnp.float32,
            )
            return (context, row_max[:, 0] + jnp.log(row_total[:, 0]))

        contexts, log_totals = lax.map(forward_one_head, head_items)
        return (join_heads(contexts), log_totals)

    contexts, log_totals = lax.map(forward_block, jnp.arange(block_count, dtype=jnp.int32))
    context_low = contexts.reshape(row_count, model_width).astype(jnp.bfloat16)
    middle = inputs + jnp.dot(context_low, w_out, preferred_element_type=jnp.float32)
    norm_second, pull_second = jax.vjp(layer_norm, middle, second_gain, second_shift)
    hidden_two = norm_second.astype(jnp.bfloat16)
    pre_act = jnp.dot(hidden_two, w_up, preferred_element_type=jnp.float32)
    activated, pull_gelu = jax.vjp(gelu_exact, pre_act)
    act_low = activated.astype(jnp.bfloat16)
    layer_out = (middle + jnp.dot(act_low, w_down, preferred_element_type=jnp.float32)).astype(
        jnp.bfloat16
    )
    grad_branch = cotangent[0]
    grad_w_down = jnp.einsum("nf,nd->fd", act_low, grad_branch, preferred_element_type=jnp.float32)
    grad_act = jnp.einsum("nd,fd->nf", grad_branch, w_down, preferred_element_type=jnp.float32)
    grad_pre = pull_gelu(grad_act)[0].astype(jnp.bfloat16)
    grad_w_up = jnp.einsum("nd,nf->df", hidden_two, grad_pre, preferred_element_type=jnp.float32)
    grad_hidden_two = jnp.einsum("nf,df->nd", grad_pre, w_up, preferred_element_type=jnp.float32)
    grad_middle_norm, grad_second_gain, grad_second_shift = pull_second(grad_hidden_two)
    grad_middle = grad_branch.astype(jnp.float32) + grad_middle_norm
    grad_attn = grad_middle.astype(jnp.bfloat16)
    grad_w_out = jnp.einsum("nd,ne->de", context_low, grad_attn, preferred_element_type=jnp.float32)
    grad_context = jnp.einsum(
        "ne,de->nd", grad_attn, w_out, preferred_element_type=jnp.float32
    ).astype(jnp.bfloat16)

    def backward_block(carry, block_index):
        (
            grad_key_pad,
            grad_value_pad,
            grad_glob_key,
            grad_glob_value,
            grad_query_vec,
            grad_key_vec,
            grad_shift,
            grad_width,
        ) = carry
        head_items, shared, picked, first_row = block_inputs(block_index)
        extra_items = (
            split_heads(lax.dynamic_slice_in_dim(query_float, first_row, QBLOCK, 0)),
            split_heads(lax.dynamic_slice_in_dim(key_float, first_row, band_span, 0)),
            query_vectors.transpose(1, 0, 2),
            key_vectors.transpose(1, 0, 2),
            split_heads(lax.dynamic_slice_in_dim(grad_context, first_row, QBLOCK, 0)),
            log_totals[block_index],
        )

        def backward_one_head(items):
            (
                query_head,
                key_head,
                value_head,
                glob_key_head,
                glob_value_head,
                query_rich,
                key_rich,
                rich_shift,
                rich_width,
                query_exact,
                key_exact,
                query_vec,
                key_vec,
                grad_head,
                log_total,
            ) = items
            scores = head_scores(
                query_head,
                key_head,
                glob_key_head,
                query_rich,
                key_rich,
                rich_shift,
                rich_width,
                shared[0],
                shared[1],
                shared[2],
            )
            attn_probs = jnp.exp(scores - log_total[:, None])
            grad_probs = jnp.concatenate(
                [
                    jnp.einsum(
                        "qe,ke->qk", grad_head, value_head, preferred_element_type=jnp.float32
                    ),
                    jnp.einsum(
                        "qe,ge->qg", grad_head, glob_value_head, preferred_element_type=jnp.float32
                    ),
                ],
                axis=1,
            )
            row_dot = jnp.sum(attn_probs * grad_probs, axis=1, keepdims=True)
            grad_scores = (attn_probs * (grad_probs - row_dot)).astype(jnp.bfloat16)
            probs_low = attn_probs.astype(jnp.bfloat16)
            near_grad = grad_scores[:, :band_span]
            far_grad = grad_scores[:, band_span:]
            grad_value = jnp.einsum(
                "qk,qe->ke", probs_low[:, :band_span], grad_head, preferred_element_type=jnp.float32
            )
            grad_glob_value_head = jnp.einsum(
                "qg,qe->ge", probs_low[:, band_span:], grad_head, preferred_element_type=jnp.float32
            )
            grad_query = (
                jnp.einsum("qk,ke->qe", near_grad, key_head, preferred_element_type=jnp.float32)
                + jnp.einsum(
                    "qg,ge->qe", far_grad, glob_key_head, preferred_element_type=jnp.float32
                )
            ) * 0.125
            grad_key = (
                jnp.einsum("qk,qe->ke", near_grad, query_head, preferred_element_type=jnp.float32)
                * 0.125
            )
            grad_glob_key_head = (
                jnp.einsum("qg,qe->ge", far_grad, query_head, preferred_element_type=jnp.float32)
                * 0.125
            )
            rich_pull = jax.vjp(
                partial(rich_terms, pair_geometry=shared[0]),
                query_rich,
                key_rich,
                rich_shift,
                rich_width,
            )[1]
            grad_query_rich, grad_key_rich, grad_shift_head, grad_width_head = rich_pull(
                near_grad.astype(jnp.float32)
            )
            grad_query = grad_query + jnp.dot(grad_query_rich.T, query_vec, precision=HIGHEST)
            grad_key = grad_key + jnp.dot(grad_key_rich.T, key_vec, precision=HIGHEST)
            return (
                grad_query,
                grad_key,
                grad_value,
                grad_glob_key_head,
                grad_glob_value_head,
                jnp.dot(grad_query_rich, query_exact, precision=HIGHEST),
                jnp.dot(grad_key_rich, key_exact, precision=HIGHEST),
                grad_shift_head,
                grad_width_head,
            )

        results = lax.map(backward_one_head, head_items + extra_items)
        key_now = lax.dynamic_slice_in_dim(grad_key_pad, first_row, band_span, 0)
        grad_key_pad = lax.dynamic_update_slice_in_dim(
            grad_key_pad, key_now + join_heads(results[1]), first_row, 0
        )
        value_now = lax.dynamic_slice_in_dim(grad_value_pad, first_row, band_span, 0)
        grad_value_pad = lax.dynamic_update_slice_in_dim(
            grad_value_pad, value_now + join_heads(results[2]), first_row, 0
        )
        grad_glob_key = grad_glob_key.at[picked].add(join_heads(results[3]))
        grad_glob_value = grad_glob_value.at[picked].add(join_heads(results[4]))
        carry = (
            grad_key_pad,
            grad_value_pad,
            grad_glob_key,
            grad_glob_value,
            grad_query_vec + results[5],
            grad_key_vec + results[6],
            grad_shift + results[7],
            grad_width + results[8],
        )
        return (carry, join_heads(results[0]))

    start_carry = (
        jnp.zeros((row_count + 2 * RADIUS, model_width), jnp.float32),
        jnp.zeros((row_count + 2 * RADIUS, model_width), jnp.float32),
        jnp.zeros((glob_count, model_width), jnp.float32),
        jnp.zeros((glob_count, model_width), jnp.float32),
        jnp.zeros((head_count, 4, head_dim), jnp.float32),
        jnp.zeros((head_count, 4, head_dim), jnp.float32),
        jnp.zeros((head_count, 4), jnp.float32),
        jnp.zeros((head_count, 2), jnp.float32),
    )
    final_carry, query_grads = lax.scan(
        backward_block, start_carry, jnp.arange(block_count, dtype=jnp.int32)
    )
    (
        grad_key_pad,
        grad_value_pad,
        grad_glob_key,
        grad_glob_value,
        grad_query_vec,
        grad_key_vec,
        grad_shift,
        grad_width,
    ) = final_carry
    grad_pads = jnp.stack([grad_key_pad, grad_value_pad])
    rim_send = jnp.concatenate([grad_pads[:, :RADIUS], grad_pads[:, row_count + RADIUS :]], axis=1)
    rim_back = padded(rim_send.astype(jnp.bfloat16), (("seq", 1),), RADIUS).astype(rim_send.dtype)
    own_pairs = grad_pads[:, RADIUS : RADIUS + row_count]
    own_pairs = own_pairs.at[:, :RADIUS].add(rim_back[:, :RADIUS])
    own_pairs = own_pairs.at[:, row_count - RADIUS :].add(rim_back[:, 3 * RADIUS :])
    grad_projected = jnp.concatenate(
        [query_grads.reshape(row_count, model_width), own_pairs[0], own_pairs[1]], axis=1
    ).astype(jnp.bfloat16)
    glob_grad_all = jnp.concatenate([grad_glob_key, grad_glob_value], axis=1)
    w_pair_float = w_pair.astype(jnp.float32)
    glob_grad_own = lax.psum_scatter(
        glob_grad_all.astype(jnp.bfloat16), "seq", scatter_dimension=0, tiled=True
    ).astype(jnp.float32)
    grad_w_pair = jnp.dot(glob_hidden.astype(jnp.float32).T, glob_grad_own, precision=HIGHEST)
    grad_glob_hidden = jnp.dot(glob_grad_own, w_pair_float.T, precision=HIGHEST)
    grad_w_qkv = jnp.einsum(
        "nd,ne->de", hidden_one, grad_projected, preferred_element_type=jnp.float32
    )
    grad_w_qkv = jnp.concatenate(
        [grad_w_qkv[:, :model_width], grad_w_qkv[:, model_width:] + grad_w_pair], axis=1
    )
    grad_hidden_one = jnp.einsum(
        "ne,de->nd", grad_projected, w_qkv, preferred_element_type=jnp.float32
    )
    grad_inputs_norm, grad_gain_tokens, grad_shift_tokens = pull_first(grad_hidden_one)
    grad_glob_in, grad_gain_globals, grad_shift_globals = pull_glob(grad_glob_hidden)
    tokens_grad = (grad_middle + grad_inputs_norm).astype(jnp.bfloat16)
    glob_grad = grad_glob_in.astype(jnp.bfloat16)
    grad_first_gain = grad_gain_tokens + grad_gain_globals
    grad_first_shift = grad_shift_tokens + grad_shift_globals
    rich_query_grad = grad_query_vec.transpose(1, 0, 2).reshape(4, model_width)
    rich_key_grad = grad_key_vec.transpose(1, 0, 2).reshape(4, model_width)
    every_share = (
        lax.psum_scatter(
            grad_w_up.astype(jnp.bfloat16), "seq", scatter_dimension=0, tiled=True
        ).astype(jnp.float32),
        lax.psum_scatter(
            grad_w_down.astype(jnp.bfloat16), "seq", scatter_dimension=0, tiled=True
        ).astype(jnp.float32),
        lax.psum_scatter(
            grad_second_gain.astype(jnp.bfloat16), "seq", scatter_dimension=0, tiled=True
        ).astype(jnp.float32),
        lax.psum_scatter(
            grad_second_shift.astype(jnp.bfloat16), "seq", scatter_dimension=0, tiled=True
        ).astype(jnp.float32),
        lax.psum_scatter(
            grad_w_qkv.astype(jnp.bfloat16), "seq", scatter_dimension=0, tiled=True
        ).astype(jnp.float32),
        lax.psum_scatter(
            grad_w_out.astype(jnp.bfloat16), "seq", scatter_dimension=0, tiled=True
        ).astype(jnp.float32),
        lax.psum_scatter(
            grad_first_gain.astype(jnp.bfloat16), "seq", scatter_dimension=0, tiled=True
        ).astype(jnp.float32),
        lax.psum_scatter(
            grad_first_shift.astype(jnp.bfloat16), "seq", scatter_dimension=0, tiled=True
        ).astype(jnp.float32),
        lax.psum_scatter(
            rich_query_grad.astype(jnp.bfloat16), "seq", scatter_dimension=1, tiled=True
        ).astype(jnp.float32),
        lax.psum_scatter(
            rich_key_grad.astype(jnp.bfloat16), "seq", scatter_dimension=1, tiled=True
        ).astype(jnp.float32),
    )
    every_share = (
        lax.psum(every_share[0].astype(jnp.bfloat16), "stream").astype(jnp.float32),
        lax.psum(every_share[1].astype(jnp.bfloat16), "stream").astype(jnp.float32),
        lax.psum(every_share[2].astype(jnp.bfloat16), "stream").astype(jnp.float32),
        lax.psum(every_share[3].astype(jnp.bfloat16), "stream").astype(jnp.float32),
        lax.psum(every_share[4].astype(jnp.bfloat16), "stream").astype(jnp.float32),
        lax.psum(every_share[5].astype(jnp.bfloat16), "stream").astype(jnp.float32),
        lax.psum(every_share[6].astype(jnp.bfloat16), "stream").astype(jnp.float32),
        lax.psum(every_share[7].astype(jnp.bfloat16), "stream").astype(jnp.float32),
        lax.psum(every_share[8].astype(jnp.bfloat16), "stream").astype(jnp.float32),
        lax.psum(every_share[9].astype(jnp.bfloat16), "stream").astype(jnp.float32),
    )
    ffn_shares = every_share[:4]
    attn_shares = every_share[4:]
    small_sums = lax.psum((grad_shift.T, grad_width.T), ("stream", "seq"))
    return (
        layer_out[None],
        tokens_grad[None],
        glob_grad[None],
        attn_shares[0],
        attn_shares[1],
        ffn_shares[0],
        ffn_shares[1],
        attn_shares[2],
        attn_shares[3],
        ffn_shares[2],
        ffn_shares[3],
        attn_shares[4],
        attn_shares[5],
        small_sums[0],
        small_sums[1],
    )


def solution(mesh):
    return jax.shard_map(
        body,
        mesh=mesh,
        in_specs=(
            P("stream", "seq", None),
            P("stream", "seq", None),
            P("stream", "seq", None),
            P(),
            P(),
            P(),
            P(),
            P(),
            P(),
            P(),
            P(),
            P(),
            P(),
            P(),
            P(),
            P("stream", None),
            P("stream", None),
            P("stream", None, None),
            P("stream", None),
        ),
        out_specs=(
            P("stream", "seq", None),
            P("stream", "seq", None),
            P("stream", "seq", None),
            P("seq", None),
            P("seq", None),
            P("seq", None),
            P("seq", None),
            P("seq"),
            P("seq"),
            P("seq"),
            P("seq"),
            P(None, "seq"),
            P(None, "seq"),
            P(),
            P(),
        ),
        check_vma=False,
    )
```

profile of v0, /device:TPU:0, one launch (start us, length us, event | category | flops | bytes accessed | tf_op | source)
XLA Modules:
  0.0 2726.8 jit_solution(17832418818424959782)
XLA Ops:
  31.1 18.4 all_gather.3
  81.9 573.7 %while.138 = (s32[]{:T(128)}, bf16[2,512,768]{2,1,0:T(8,128)(2,1)}, f32[2,12,512]{2,1,0:T(8,128)}, s32[2]{0:T(128)S(1)}, bf16[1024,768]{0,1:T(8,128)(2,1)}, /*in...) while((s32[]{:T(128)}, bf16[2,512,768]{2,1,0:T(8,128)(2,1)}, ...), condition=%wide.region_16.18_spmd.clone, body=%wide.region_6.17_spmd.sunk.clone | while | flops 142410656 | bytes 48024660 | solution.py:279
  105.7 259.5 %while.137 = (s32[]{:T(128)}, bf16[12,512,64]{1,2,0:T(8,128)(2,1)}, f32[12,512]{1,0:T(8,128)}, bf16[12,512,64]{1,2,0:T(8,128)(2,1)}, bf16[12,768,64]{1,2,0:T(8,1...) while((s32[]{:T(128)}, bf16[12,512,64]{1,2,0:T(8,128)(2,1)}, ...), condition=%wide.region_15.16_spmd.clone, body=%wide.region_11.15_spmd.clone.sunk | while | flops 137395712 | bytes 14558689 | solution.py:276
  135.4 9.2 fusion.382
  157.1 9.2 fusion.382
  178.7 9.2 fusion.382
  200.3 9.2 fusion.382
  221.9 9.2 fusion.382
  243.6 9.2 fusion.382
  265.2 9.2 fusion.382
  286.8 9.2 fusion.382
  392.3 259.5 %while.137 = (s32[]{:T(128)}, bf16[12,512,64]{1,2,0:T(8,128)(2,1)}, f32[12,512]{1,0:T(8,128)}, bf16[12,512,64]{1,2,0:T(8,128)(2,1)}, bf16[12,768,64]{1,2,0:T(8,1...) while((s32[]{:T(128)}, bf16[12,512,64]{1,2,0:T(8,128)(2,1)}, ...), condition=%wide.region_15.16_spmd.clone, body=%wide.region_11.15_spmd.clone.sunk | while | flops 137395712 | bytes 14558689 | solution.py:276
  465.3 9.2 fusion.382
  486.9 9.2 fusion.382
  508.6 9.2 fusion.382
  616.7 9.2 fusion.382
  638.3 9.2 fusion.382
  660.0 35.6 %multiply_convert_fusion.1 = (bf16[1024,3072]{1,0:T(8,128)(2,1)}, f32[1024,3072]{1,0:T(8,128)}, f32[1024,3072]{1,0:T(8,128)}) fusion(bf16[768,3072]{1,0:T(8,128)(2,1)S(1)} %bitcast.744, f32[1024,768]{0,1:T(8,128)S(1)} %get-tuple-element.2419, f32[768]{0:T(1024)S(1)} %copy-done.98, f32[768]{0:T(1024)S(1)} %copy-done.83, f32[1024]{0:T(1024)S(1)} %fusion.203, ...), kind=kOutput, calls=%fused_computation.300 | convolution fusion | flops 5040242688 | bytes 39335936 | tf_op jit(solution)/shard_map/dot_general | solution.py:284
  695.5 15.9 add_convert_fusion
  711.4 10.7 fusion.235
  742.9 1613.7 %while.140 = (s32[]{:T(128)}, f32[1280,768]{1,0:T(8,128)}, f32[1280,768]{1,0:T(8,128)}, f32[256,768]{1,0:T(8,128)}, f32[256,768]{1,0:T(8,128)}, /*index=5*/f32[1...) while((s32[]{:T(128)}, f32[1280,768]{1,0:T(8,128)}, ...), condition=%wide.region_45.47_spmd.clone.clone, body=%wide.region_21.0_spmd.clone.sunk.clone | while | flops 356598848 | bytes 204220624 | solution.py:449
  802.6 719.2 %while.139 = (s32[]{:T(128)}, bf16[12,512,64]{1,2,0:T(8,128)(2,1)}, f32[12,768,64]{1,2,0:T(8,128)}, f32[12,768,64]{1,2,0:T(8,128)}, f32[12,128,64]{1,2,0:T(8,128...) while((s32[]{:T(128)}, bf16[12,512,64]{1,2,0:T(8,128)(2,1)}, ...), condition=%wide.region_42.43_spmd.clone, body=%wide.region_26.42_spmd.clone.sunk | while | flops 350194688 | bytes 67362744 | solution.py:416
  1609.2 719.2 %while.139 = (s32[]{:T(128)}, bf16[12,512,64]{1,2,0:T(8,128)(2,1)}, f32[12,768,64]{1,2,0:T(8,128)}, f32[12,768,64]{1,2,0:T(8,128)}, f32[12,128,64]{1,2,0:T(8,128...) while((s32[]{:T(128)}, bf16[12,512,64]{1,2,0:T(8,128)(2,1)}, ...), condition=%wide.region_42.43_spmd.clone, body=%wide.region_26.42_spmd.clone.sunk | while | flops 350194688 | bytes 67362744 | solution.py:416
  2409.1 10.1 convolution_convert_fusion.2
  2421.0 10.0 fusion.183
  2433.8 38.9 %all-reduce.21 = (f32[4,12]{1,0:T(4,128)}, f32[2,12]{1,0:T(2,128)}) all-reduce(f32[4,12]{1,0:T(4,128)S(1)} %bitcast.740, f32[2,12]{1,0:T(2,128)S(1)} %bitcast.741), channel_id=1, replica_groups=mesh['stream'=4,'seq'=8] {'stream','seq'}, use_global_device_ids=true, to_apply=%region_77.79 | all-reduce | flops 72 | bytes 576 | tf_op jit(solution)/shard_map/psum | solution.py:541
  2491.2 43.5 %reduce-scatter.14.cloned.1.call-done = bf16[96,2304]{1,0:T(8,128)(2,1)} async-done(((bf16[768,2304]{1,0:T(8,128)(2,1)}), bf16[96,2304]{1,0:T(8,128)(2,1)}) %reduce-scatter.14.cloned.1.call-update) | async-done | bytes 442384 | tf_op jit(solution)/shard_map/reduce_scatter | solution.py:508
  2534.6 55.7 %reduce-scatter.20.cloned.1.call-done = bf16[384,768]{1,0:T(8,128)(2,1)} async-done(((bf16[3072,768]{1,0:T(8,128)(2,1)}), bf16[384,768]{1,0:T(8,128)(2,1)}) %reduce-scatter.20.cloned.1.call-update) | async-done | bytes 589840 | tf_op jit(solution)/shard_map/reduce_scatter | solution.py:499
  2590.3 55.7 %reduce-scatter.18.cloned.1.call-done = bf16[96,3072]{1,0:T(8,128)(2,1)} async-done(((bf16[768,3072]{1,0:T(8,128)(2,1)}), bf16[96,3072]{1,0:T(8,128)(2,1)}) %reduce-scatter.18.cloned.1.call-update) | async-done | bytes 589840 | tf_op jit(solution)/shard_map/reduce_scatter | solution.py:496
  2657.2 13.9 all-reduce.22
  2671.5 10.0 all-reduce.23
  2685.6 27.1 all-reduce.27.cloned.1.call-done
  (2065 shorter events, 1977.8 us)
Async XLA Ops:
  7.2 648.4 %copy-start = (bf16[768,768]{1,0:T(8,128)(2,1)S(1)}, bf16[768,768]{1,0:T(8,128)(2,1)}, u32[]{:S(2)}) copy-start(bf16[768,768]{1,0:T(8,128)(2,1)} %param.37) | copy-start | bytes 3538948
  7.2 2386.7 %reduce-scatter.12.cloned.1.call-start = ((), (), s32[]{:S(2)}) async-start(), calls=%async_computation.7 | async-start | bytes 884736 | tf_op jit(solution)/shard_map/reduce_scatter | solution.py:473
  21.1 39.5 %collective-permute-start = (bf16[2,128,768]{2,1,0:T(8,128)(2,1)}, bf16[2,128,768]{2,1,0:T(8,128)(2,1)}, u32[]{:S(2)}, u32[]{:S(2)}) collective-permute-start(bf16[2,128,768]{2,1,0:T(8,128)(2,1)} %get-tuple-element.2414), channel_id=1, source_target_pairs={{0,1},{1,2},{2,3},{3,4},{4,5},{5,6},{6,7},{8,9},{9,10},{10,11},{11... | collective-permute-start | bytes 1179656 | tf_op jit(solution)/shard_map/ppermute | solution.py:26
  24.3 36.4 %collective-permute-start.1 = (bf16[2,128,768]{2,1,0:T(8,128)(2,1)}, bf16[2,128,768]{2,1,0:T(8,128)(2,1)}, u32[]{:S(2)}, u32[]{:S(2)}) collective-permute-start(bf16[2,128,768]{2,1,0:T(8,128)(2,1)} %get-tuple-element.2415), channel_id=1, source_target_pairs={{1,0},{2,1},{3,2},{4,3},{5,4},{6,5},{7,6},{9,8},{10,9},{11,10},{12... | collective-permute-start | bytes 1179656 | tf_op jit(solution)/shard_map/ppermute | solution.py:27
  28.7 20.8 copy-start.33
  659.2 36.4 %copy-start.16 = (f32[1024,768]{0,1:T(8,128)}, f32[1024,768]{0,1:T(8,128)S(1)}, u32[]{:S(2)}) copy-start(f32[1024,768]{0,1:T(8,128)S(1)} %get-tuple-element.2419) | copy-start | bytes 9437188
  659.2 71.0 %copy-start.68 = (f32[1024]{0:T(1024)}, f32[1024]{0:T(1024)S(1)}, u32[]{:S(2)}) copy-start(f32[1024]{0:T(1024)S(1)} %broadcast_multiply_fusion) | copy-start | bytes 12292
  660.0 70.3 %copy-start.81 = (f32[1024]{0:T(1024)}, f32[1024]{0:T(1024)S(1)}, u32[]{:S(2)}) copy-start(f32[1024]{0:T(1024)S(1)} %fusion.203) | copy-start | bytes 12292
  660.0 35.6 %copy-start.34 = (bf16[1,1024,768]{2,1,0:T(8,128)(2,1)S(1)}, bf16[1,1024,768]{2,1,0:T(8,128)(2,1)}, u32[]{:S(2)}) copy-start(bf16[1,1024,768]{2,1,0:T(8,128)(2,1)} %param.35) | copy-start | bytes 4718596
  743.1 23.0 copy-start.28
  743.1 23.0 copy-start.60
  743.1 23.0 copy-start.71
  743.1 23.0 copy-start.73
  1222.0 17.1 copy-start.2
  1401.8 17.1 copy-start.2
  1549.7 23.0 copy-start.28
  1549.7 23.0 copy-start.60
  1549.7 23.0 copy-start.71
  1549.7 23.0 copy-start.73
  2028.6 17.1 copy-start.2
  2208.4 17.1 copy-start.2
  2360.0 112.7 %reduce-scatter.24.cloned.1.call-start = ((), (), s32[]{:S(2)}) async-start(), calls=%async_computation.13 | async-start | bytes 221184
  2361.0 112.5 %reduce-scatter.22.cloned.1.call-start = ((), (), s32[]{:S(2)}) async-start(), calls=%async_computation.12 | async-start | bytes 221184
  2366.0 11.0 collective-permute-start.2
  2368.3 8.8 collective-permute-start.3
  2369.6 121.5 %reduce-scatter.16.cloned.1.call-start = ((), (), s32[]{:S(2)}) async-start(), calls=%async_computation.9 | async-start | bytes 1327104 | tf_op jit(solution)/shard_map/reduce_scatter | solution.py:511
  2373.6 161.1 %reduce-scatter.14.cloned.1.call-start = ((), (), s32[]{:S(2)}) async-start(), calls=%async_computation.8 | async-start | bytes 3981312 | tf_op jit(solution)/shard_map/reduce_scatter | solution.py:508
  2399.2 191.2 %reduce-scatter.20.cloned.1.call-start = ((), (), s32[]{:S(2)}) async-start(), calls=%async_computation.11 | async-start | bytes 5308416 | tf_op jit(solution)/shard_map/reduce_scatter | solution.py:499
  2408.4 237.6 %reduce-scatter.18.cloned.1.call-start = ((), (), s32[]{:S(2)}) async-start(), calls=%async_computation.10 | async-start | bytes 5308416 | tf_op jit(solution)/shard_map/reduce_scatter | solution.py:496
  2419.1 293.5 %all-reduce.27.cloned.1.call-start = ((), (), s32[]{:S(2)}) async-start(), calls=%async_computation.14 | async-start | bytes 3538944 | tf_op jit(solution)/shard_map/psum | solution.py:532
  2489.8 156.2 %copy-start.80 = (f32[1024]{0:T(1024)S(1)}, f32[1024]{0:T(1024)}, u32[]{:S(2)}) copy-start(f32[1024]{0:T(1024)} %copy-done.79) | copy-start | bytes 12292
  2651.9 32.7 %copy-start.97 = (f32[32]{0:T(128)S(1)}, f32[32]{0:T(128)}, u32[]{:S(2)}) copy-start(f32[32]{0:T(128)} %copy-done.96) | copy-start | bytes 388
  (214 other events, 1483.2 us)
Sparse Core Ops, SparseCore 0:
  2360.1 33.6 reduce-scatter.11
  2396.8 28.4 reduce-scatter.23
  2428.1 28.4 reduce-scatter.21
  2459.4 31.0 reduce-scatter.15
  2492.7 41.8 reduce-scatter.13
  2536.8 53.4 reduce-scatter.19
  2592.6 53.3 reduce-scatter.17
  2649.4 63.2 all-reduce.26
where the time goes:
time: 2770 us; the launch traced here: 2730 us
  matrix products  1100 us (40%)
  other arithmetic  565 us (20%)
  local copies, waits for them, and re-layouts  499 us (18%)
  loops' own time  268 us (10%)
  waiting for transfers between devices  186 us (7%)
  blocking collectives  81.2 us (3%)
    dot_general x48, matrix products, head_scores(): jnp.einsum('qe,ke->qk', query_head, key_head, preferred_element_type=jnp....  424 us
    reduce_sum x48, other arithmetic, summed(): query_rich[column][:, None] + key_rich[column][None, :] + rich_shift[column]  189 us
    another operation x2, loops' own time, backward_block(): results = lax.map(backward_one_head, head_items + extra_items)  186 us
    reduce_sum x24, other arithmetic, rich_terms(): 0.5 * rich_width[1] * rich_width[1] * gap_y * gap_y  179 us
    another operation x2, loops' own time, forward_block(): contexts, log_totals = lax.map(forward_one_head, head_items)  63.1 us
    dynamic_update_slice x48, local copies, waits for them, and re-layouts, backward_block(): results = lax.map(backward_one_head, head_items + extra_items)  61.4 us
    reduce_scatter x1, waiting for transfers between devices, body(): lax.psum_scatter(grad_w_down.astype(jnp.bfloat16), 'seq', scatter_dimensi...  55.7 us
    reduce_scatter x1, waiting for transfers between devices, body(): lax.psum_scatter(grad_w_up.astype(jnp.bfloat16), 'seq', scatter_dimension...  55.7 us
  transfers between devices with their start and end apart: 12, of which 5 were waited for; matrix products, arithmetic and copies ran while one was open for 4% of the time, Pallas kernels for 0%

commit v1 on v0

v1 whole, which is shorter than its diff:
```python
from functools import partial
import math

import jax
import jax.numpy as jnp
from jax import lax
from jax.experimental import pallas as pl
from jax.experimental.pallas import tpu as pltpu
from jax.sharding import PartitionSpec as P

RADIUS = 128
GLOB_FORM = 64
QBLOCK = 512
TOK_DEV = 1024


EPSILON = 1e-06
HIGHEST = lax.Precision.HIGHEST


def padded(shard, sides, width):
    for axis, dim in sides:
        peers, length = (lax.axis_size(axis), shard.shape[dim])
        up = [(i, (i + 1) % peers) for i in range(peers - 1)]
        down = [(j, i) for i, j in up]
        last = lax.slice_in_dim(shard, length - width, length, axis=dim)
        first = lax.slice_in_dim(shard, 0, width, axis=dim)
        before = lax.ppermute(last, axis, up)
        after = lax.ppermute(first, axis, down)
        shard = jnp.concatenate([before, shard, after], axis=dim)
    return shard


def layer_norm(values, norm_gain, norm_shift):
    centre = jnp.mean(values, axis=-1, keepdims=True)
    centred = values - centre
    spread = jnp.mean(centred * centred, axis=-1, keepdims=True)
    return centred * lax.rsqrt(spread + EPSILON) * norm_gain + norm_shift


def gelu_exact(values):
    return jax.nn.gelu(values, approximate=False)


def bucket_starts(unit_counts):
    position = jnp.arange(unit_counts.shape[0], dtype=jnp.int32)
    before = jnp.cumsum(unit_counts) - unit_counts
    return jnp.where(position == 0, 0, TOK_DEV // 2 + TOK_DEV * before)


def locate(position, starts, lengths, stream_len):
    form_count = starts.shape[0]
    form_index = jnp.sum((position[:, None] >= starts[None, 1:]).astype(jnp.int32), axis=1)
    chosen = form_index[:, None] == jnp.arange(form_count, dtype=jnp.int32)[None, :]
    first_row = jnp.sum(jnp.where(chosen, starts[None, :], 0), axis=1)
    live_rows = jnp.sum(jnp.where(chosen, lengths[None, :], 0), axis=1)
    is_live = (position >= 0) & (position < stream_len) & (position - first_row < live_rows)
    return (form_index, is_live)


TILE = 128
SPAN = 384
LOG2E = math.log2(math.e)
FAR_AWAY = 1e15
CH = 16
F32 = jnp.float32
BF16 = jnp.bfloat16

def mm(a, b):
    return lax.dot_general(a, b, (((1,), (0,)), ((), ())), preferred_element_type=F32)

def mm_nt(a, b):
    return lax.dot_general(a, b, (((1,), (1,)), ((), ())), preferred_element_type=F32)

def split3(values):
    hi = lax.reduce_precision(values, 8, 7)
    rest = values - hi
    mid = lax.reduce_precision(rest, 8, 7)
    low = rest - mid
    return hi.astype(BF16), mid.astype(BF16), low.astype(BF16)

def half_masks(dtype):
    lane = lax.broadcasted_iota(jnp.int32, (1, 128), 1)
    low = (lane < 64).astype(F32)
    return low.astype(dtype), (1.0 - low).astype(dtype)

def geometry_into(cq_ref, ck_ref, t, refs, masked):
    ox_ref, oy_ref, dx_ref, dy_ref = refs
    for r in range(0, TILE, 32):
        xq = cq_ref[r : r + 32, 0:1]
        yq = cq_ref[r : r + 32, 1:2]
        fq = cq_ref[r : r + 32, 2:3]
        for lt in range(3):
            cols = pl.ds(pl.multiple_of(t * TILE + lt * 128, 128), 128)
            xk = ck_ref[0:1, cols]
            yk = ck_ref[1:2, cols]
            out = (slice(r, r + 32), slice(lt * 128, lt * 128 + 128))
            dx = jnp.log(1.0 + jnp.abs(xq - xk))
            dy = jnp.log(1.0 + jnp.abs(yq - yk))
            if masked:
                fk = ck_ref[2:3, cols]
                row = lax.broadcasted_iota(jnp.int32, (32, 128), 0) + r
                col = lax.broadcasted_iota(jnp.int32, (32, 128), 1) + lt * 128
                ok = (fq == fk) & (col >= row) & (col - row <= 2 * RADIUS)
                dx = jnp.where(ok, dx, FAR_AWAY)
                ox_ref[out] = jnp.where(xk > xq, 1.0, -1.0)
                oy_ref[out] = jnp.where(yk > yq, 1.0, -1.0)
            dx_ref[out] = dx
            dy_ref[out] = dy

def fwd_kernel(w_ref, q_ref, k_ref, v_ref, kg_ref, vg_ref, cq_ref, ck_ref, rq_ref, rk_ref, rb_ref,
               ctx_ref, pn_ref, pf_ref, g0_ref, g1_ref,
               ox_ref, oy_ref, dx_ref, dy_ref, s_ref, sf_ref, a_ref, b_ref, *, pairs):
    t = pl.program_id(0)
    geometry_into(cq_ref, ck_ref, t, (ox_ref, oy_ref, dx_ref, dy_ref), True)
    lo16, hi16 = half_masks(BF16)
    lane = lax.broadcasted_iota(jnp.int32, (CH, 128), 1)
    low = lane < 64
    rows = pl.ds(pl.multiple_of(t * TILE, TILE), SPAN)

    def one_pair(p, carry):
        cols = pl.ds(pl.multiple_of(p * 128, 128), 128)
        qp = q_ref[:, cols]
        kp = k_ref[rows, cols]
        vp = v_ref[rows, cols]
        kgp = kg_ref[0, :, cols]
        vgp = vg_ref[0, :, cols]
        s_ref[...] = mm_nt(jnp.concatenate([qp * lo16, qp * hi16], axis=0), kp)
        sf_ref[...] = mm_nt(qp, jnp.concatenate([kgp * lo16, kgp * hi16], axis=0))
        a_ref[...] = mm_nt(jnp.concatenate([qp, qp, qp], axis=1), rq_ref[p]) + rb_ref[p]
        b24 = mm_nt(rk_ref[p], kp)
        b_ref[...] = b24[0:8] + b24[8:16] + b24[16:24]
        for r in range(0, TILE, CH):
            far = sf_ref[r : r + CH, :] * (0.125 * LOG2E)
            tops = []
            held = []
            for e in range(2):
                u0 = (a_ref[r : r + CH, e : e + 1] + b_ref[e : e + 1, :]) * ox_ref[r : r + CH, :]
                u1 = (a_ref[r : r + CH, 2 + e : 3 + e] + b_ref[2 + e : 3 + e, :]) * oy_ref[r : r + CH, :]
                e0 = jnp.exp2(jnp.minimum(u0, -u0))
                e1 = jnp.exp2(jnp.minimum(u1, -u1))
                f0 = 1.0 + e0
                f1 = 1.0 + e1
                rr = 1.0 / (f0 * f1)
                gx = (w_ref[2 * p + e, 0] * dx_ref[r : r + CH, :] - a_ref[r : r + CH, 4 + e : 5 + e]) - b_ref[4 + e : 5 + e, :]
                gy = (w_ref[2 * p + e, 1] * dy_ref[r : r + CH, :] - a_ref[r : r + CH, 6 + e : 7 + e]) - b_ref[6 + e : 7 + e, :]
                s = s_ref[e * TILE + r : e * TILE + r + CH, :] * (0.125 * LOG2E)
                s = s + jnp.minimum(u0, 0.0) + jnp.minimum(u1, 0.0) - gx * gx - gy * gy
                top = jnp.maximum(jnp.maximum(s[:, 0:128], s[:, 128:256]), s[:, 256:384])
                here = low if e == 0 else ~low
                top = jnp.maximum(top, jnp.where(here, far, -3e38))
                tops.append(jnp.max(top, axis=1, keepdims=True))
                g0 = jnp.where(u0 >= 0.0, e0, 1.0) * ox_ref[r : r + CH, :] * (f1 * rr)
                g1 = jnp.where(u1 >= 0.0, e1, 1.0) * oy_ref[r : r + CH, :] * (f0 * rr)
                g0_ref[0, 2 * p + e, r : r + CH, :] = g0.astype(BF16)
                g1_ref[0, 2 * p + e, r : r + CH, :] = g1.astype(BF16)
                held.append((s, rr))
            pfar = jnp.exp2(far - jnp.where(low, tops[0], tops[1]))
            invs = []
            for e in range(2):
                s, rr = held[e]
                pe = jnp.exp2(s - tops[e]) * rr
                here = low if e == 0 else ~low
                tot = pe[:, 0:128] + pe[:, 128:256] + pe[:, 256:384] + jnp.where(here, pfar, 0.0)
                inv = 1.0 / jnp.sum(tot, axis=1, keepdims=True)
                invs.append(inv)
                pn_ref[0, 2 * p + e, r : r + CH, :] = (pe * inv).astype(BF16)
            pf_ref[0, p, r : r + CH, :] = (pfar * jnp.where(low, invs[0], invs[1])).astype(BF16)
        ctx = mm(pn_ref[0, 2 * p], vp * lo16) + mm(pn_ref[0, 2 * p + 1], vp * hi16)
        ctx = ctx + mm(pf_ref[0, p], jnp.concatenate([vgp * lo16, vgp * hi16], axis=0))
        ctx_ref[:, cols] = ctx.astype(BF16)
        return carry

    lax.fori_loop(0, pairs, one_pair, 0)

def bwd_kernel(q_ref, dc_ref, ctx_ref, k_ref, v_ref, kg_ref, vg_ref, cq_ref, ck_ref, rq_ref, rk_ref, rb_ref, rv_ref,
               pn_ref, pf_ref, g0_ref, g1_ref,
               dq_ref, dk_ref, dv_ref, dkg_ref, dvg_ref, db_ref, rqg_ref, th_ref,
               dx_ref, dy_ref, dp_ref, dpf_ref, ds_ref, dsf_ref, a_ref, b_ref, dqr_ref, D_ref, *, pairs, per_block):
    t = pl.program_id(0)

    @pl.when(t == 0)
    def _():
        dk_ref[...] = jnp.zeros_like(dk_ref)
        dv_ref[...] = jnp.zeros_like(dv_ref)
        db_ref[...] = jnp.zeros_like(db_ref)
        rqg_ref[...] = jnp.zeros_like(rqg_ref)
        th_ref[...] = jnp.zeros_like(th_ref)

    @pl.when(t % per_block == 0)
    def _():
        dkg_ref[...] = jnp.zeros_like(dkg_ref)
        dvg_ref[...] = jnp.zeros_like(dvg_ref)

    geometry_into(cq_ref, ck_ref, t, (None, None, dx_ref, dy_ref), False)
    lo16, hi16 = half_masks(BF16)
    lane = lax.broadcasted_iota(jnp.int32, (CH, 128), 1)
    low = lane < 64
    sub = lax.broadcasted_iota(jnp.int32, (128, 1), 0)
    lo16c = (sub < 64).astype(F32).astype(BF16)
    hi16c = (sub >= 64).astype(F32).astype(BF16)
    rows = pl.ds(pl.multiple_of(t * TILE, TILE), SPAN)

    def one_pair(p, carry):
        cols = pl.ds(pl.multiple_of(p * 128, 128), 128)
        qp = q_ref[:, cols]
        dcp = dc_ref[:, cols]
        kp = k_ref[rows, cols]
        vp = v_ref[rows, cols]
        kgp = kg_ref[0, :, cols]
        vgp = vg_ref[0, :, cols]
        kg2 = jnp.concatenate([kgp * lo16, kgp * hi16], axis=0)
        vg2 = jnp.concatenate([vgp * lo16, vgp * hi16], axis=0)
        dp_ref[...] = mm_nt(jnp.concatenate([dcp * lo16, dcp * hi16], axis=0), vp)
        dpf_ref[...] = mm_nt(dcp, vg2)
        a_ref[...] = mm_nt(jnp.concatenate([qp, qp, qp], axis=1), rq_ref[p]) + rb_ref[p]
        b24 = mm_nt(rk_ref[p], kp)
        b_ref[...] = b24[0:8] + b24[8:16] + b24[16:24]
        col_sums = [[jnp.zeros((8, SPAN), F32) for _ in range(4)] for _ in range(2)]
        thetas = [[jnp.zeros((8, 128), F32) for _ in range(2)] for _ in range(2)]
        query_sums = [jnp.zeros((8, 128), F32) for _ in range(4)]
        for r in range(0, TILE, CH):
            prod = dc_ref[r : r + CH, cols].astype(F32) * ctx_ref[r : r + CH, cols].astype(F32)
            row_sums = []
            dots = []
            for e in range(2):
                here = low if e == 0 else ~low
                dot = jnp.sum(jnp.where(here, prod, 0.0), axis=1, keepdims=True)
                dots.append(dot)
                rs = slice(r, r + CH)
                es = slice(e * TILE + r, e * TILE + r + CH)
                ds = pn_ref[0, 2 * p + e, rs, :].astype(F32) * (dp_ref[es, :] - dot)
                ds_ref[es, :] = ds.astype(BF16)
                t0 = ds * g0_ref[0, 2 * p + e, rs, :].astype(F32)
                t1 = ds * g1_ref[0, 2 * p + e, rs, :].astype(F32)
                gx = (dx_ref[rs, :] - a_ref[rs, 4 + e : 5 + e]) - b_ref[4 + e : 5 + e, :]
                gy = (dy_ref[rs, :] - a_ref[rs, 6 + e : 7 + e]) - b_ref[6 + e : 7 + e, :]
                tx = ds * gx
                ty = ds * gy
                xx = tx * gx
                yy = ty * gy
                for i, full in enumerate((xx, yy)):
                    part = full[:, 0:128] + full[:, 128:256] + full[:, 256:384]
                    thetas[e][i] = thetas[e][i] + (part[0:8] + part[8:16])
                sums = []
                for c, full in enumerate((t0, t1, tx, ty)):
                    col_sums[e][c] = col_sums[e][c] + (full[0:8] + full[8:16])
                    sums.append(jnp.sum(full[:, 0:128] + full[:, 128:256] + full[:, 256:384], axis=1, keepdims=True))
                row_sums.append(sums)
            dsf = pf_ref[0, p, r : r + CH, :].astype(F32) * (dpf_ref[r : r + CH, :] - jnp.where(low, dots[0], dots[1]))
            dsf_ref[r : r + CH, :] = dsf.astype(BF16)
            qf = q_ref[r : r + CH, cols].astype(F32)
            dqr = jnp.zeros((CH, 128), F32)
            for c in range(4):
                da = jnp.where(low, row_sums[0][c], row_sums[1][c])
                dqr = dqr + da * rv_ref[p, c : c + 1, :]
                part = da * qf
                query_sums[c] = query_sums[c] + (part[0:8] + part[8:16])
            dqr_ref[r : r + CH, :] = dqr
        for c in range(4):
            rqg_ref[p, c] += query_sums[c]
        for e in range(2):
            for i in range(2):
                th_ref[p, 2 * e + i] += thetas[e][i]
        packed = jnp.concatenate([jnp.sum(col_sums[e][c], axis=0, keepdims=True) for c in range(4) for e in range(2)], axis=0)
        db_ref[p, :, rows] += packed
        dq = mm(ds_ref[0:TILE, :], kp * lo16) + mm(ds_ref[TILE : 2 * TILE, :], kp * hi16) + mm(dsf_ref[...], kg2)
        dq_ref[:, cols] = (dq * 0.125 + dqr_ref[...]).astype(BF16)
        qT = jnp.transpose(qp)
        dcT = jnp.transpose(dcp)
        dk_ref[cols, rows] += mm(jnp.concatenate([qT * lo16c, qT * hi16c], axis=1), ds_ref[...])
        dv_ref[cols, rows] += mm(dcT * lo16c, pn_ref[0, 2 * p]) + mm(dcT * hi16c, pn_ref[0, 2 * p + 1])
        dkg_ref[0, cols, :] += mm(qT, dsf_ref[...])
        dvg_ref[0, cols, :] += mm(dcT, pf_ref[0, p])
        return carry

    lax.fori_loop(0, pairs, one_pair, 0)

def rich_rows(vectors, scale):
    heads = scale.shape[1]
    v = vectors.reshape(4, heads, 64) * scale[:, :, None]
    v = v.reshape(4, heads // 2, 2, 64)
    eye = jnp.eye(2, dtype=F32)
    full = v[:, :, :, None, :] * eye[None, None, :, :, None]
    return full.transpose(1, 0, 2, 3, 4).reshape(heads // 2, 8, 128)

def rich_operands(rich_query, rich_key, rich_bias, scale):
    heads = scale.shape[1]
    rq = jnp.concatenate(split3(rich_rows(rich_query, scale)), axis=2)
    rk = jnp.concatenate(split3(rich_rows(rich_key, scale)), axis=1)
    rb = (rich_bias * scale).reshape(4, heads // 2, 2).transpose(1, 0, 2).reshape(heads // 2, 1, 8)
    return rq, rk, rb

VMEM_LIMIT = 58 * 1024 * 1024

def attn_forward(q, k_pad, v_pad, kg, vg, cq, ck, rich_query, rich_key, rich_bias, rich_theta):
    rows, width = q.shape
    heads = rich_bias.shape[1]
    pairs = heads // 2
    tiles = rows // TILE
    blocks = kg.shape[0]
    per_block = tiles // blocks
    w = rich_theta * math.sqrt(0.5 * LOG2E)
    scale = jnp.concatenate([jnp.full((2, heads), LOG2E, F32), w], axis=0)
    rq, rk, rb = rich_operands(rich_query, rich_key, rich_bias, scale)
    whole = lambda a: pl.BlockSpec(a.shape, lambda t: (0,) * a.ndim)
    return pl.pallas_call(
        partial(fwd_kernel, pairs=pairs),
        grid=(tiles,),
        in_specs=[
            pl.BlockSpec(memory_space=pltpu.SMEM),
            pl.BlockSpec((TILE, width), lambda t: (t, 0)),
            whole(k_pad), whole(v_pad),
            pl.BlockSpec((1,) + kg.shape[1:], lambda t: (t // per_block, 0, 0)),
            pl.BlockSpec((1,) + vg.shape[1:], lambda t: (t // per_block, 0, 0)),
            pl.BlockSpec((TILE, cq.shape[1]), lambda t: (t, 0)),
            whole(ck), whole(rq), whole(rk), whole(rb),
        ],
        out_specs=[
            pl.BlockSpec((TILE, width), lambda t: (t, 0)),
            pl.BlockSpec((1, heads, TILE, SPAN), lambda t: (t, 0, 0, 0)),
            pl.BlockSpec((1, pairs, TILE, 128), lambda t: (t, 0, 0, 0)),
            pl.BlockSpec((1, heads, TILE, SPAN), lambda t: (t, 0, 0, 0)),
            pl.BlockSpec((1, heads, TILE, SPAN), lambda t: (t, 0, 0, 0)),
        ],
        out_shape=[
            jax.ShapeDtypeStruct((rows, width), BF16),
            jax.ShapeDtypeStruct((tiles, heads, TILE, SPAN), BF16),
            jax.ShapeDtypeStruct((tiles, pairs, TILE, 128), BF16),
            jax.ShapeDtypeStruct((tiles, heads, TILE, SPAN), BF16),
            jax.ShapeDtypeStruct((tiles, heads, TILE, SPAN), BF16),
        ],
        scratch_shapes=[
            pltpu.VMEM((TILE, SPAN), F32), pltpu.VMEM((TILE, SPAN), F32),
            pltpu.VMEM((TILE, SPAN), F32), pltpu.VMEM((TILE, SPAN), F32),
            pltpu.VMEM((2 * TILE, SPAN), F32), pltpu.VMEM((TILE, 128), F32),
            pltpu.VMEM((TILE, 8), F32), pltpu.VMEM((8, SPAN), F32),
        ],
        compiler_params=pltpu.CompilerParams(vmem_limit_bytes=VMEM_LIMIT),
        name="attn_forward",
    )(w.T, q, k_pad, v_pad, kg, vg, cq, ck, rq, rk, rb)

def attn_backward(q, dctx, ctx, k_pad, v_pad, kg, vg, cq, ck, rich_query, rich_key, rich_bias, rich_theta, pn, pf, g0, g1):
    rows, width = q.shape
    heads = rich_bias.shape[1]
    pairs = heads // 2
    tiles = rows // TILE
    blocks = kg.shape[0]
    per_block = tiles // blocks
    rq, rk, rb = rich_operands(rich_query, rich_key, rich_bias, jnp.ones((4, heads), F32))
    factor = jnp.concatenate([jnp.ones((2, heads), F32), rich_theta * rich_theta], axis=0)
    rv = (rich_query.reshape(4, heads, 64) * factor[:, :, None]).reshape(4, pairs, 128).transpose(1, 0, 2)
    whole = lambda a: pl.BlockSpec(a.shape, lambda t: (0,) * a.ndim)
    tile_rows = pl.BlockSpec((TILE, width), lambda t: (t, 0))
    padded = k_pad.shape[0]
    outs = pl.pallas_call(
        partial(bwd_kernel, pairs=pairs, per_block=per_block),
        grid=(tiles,),
        in_specs=[
            tile_rows, tile_rows, tile_rows,
            whole(k_pad), whole(v_pad),
            pl.BlockSpec((1,) + kg.shape[1:], lambda t: (t // per_block, 0, 0)),
            pl.BlockSpec((1,) + vg.shape[1:], lambda t: (t // per_block, 0, 0)),
            pl.BlockSpec((TILE, cq.shape[1]), lambda t: (t, 0)),
            whole(ck), whole(rq), whole(rk), whole(rb), whole(rv),
            pl.BlockSpec((1, heads, TILE, SPAN), lambda t: (t, 0, 0, 0)),
            pl.BlockSpec((1, pairs, TILE, 128), lambda t: (t, 0, 0, 0)),
            pl.BlockSpec((1, heads, TILE, SPAN), lambda t: (t, 0, 0, 0)),
            pl.BlockSpec((1, heads, TILE, SPAN), lambda t: (t, 0, 0, 0)),
        ],
        out_specs=[
            tile_rows,
            pl.BlockSpec((width, padded), lambda t: (0, 0)),
            pl.BlockSpec((width, padded), lambda t: (0, 0)),
            pl.BlockSpec((1, width, 128), lambda t: (t // per_block, 0, 0)),
            pl.BlockSpec((1, width, 128), lambda t: (t // per_block, 0, 0)),
            pl.BlockSpec((pairs, 8, padded), lambda t: (0, 0, 0)),
            pl.BlockSpec((pairs, 4, 8, 128), lambda t: (0, 0, 0, 0)),
            pl.BlockSpec((pairs, 4, 8, 128), lambda t: (0, 0, 0, 0)),
        ],
        out_shape=[
            jax.ShapeDtypeStruct((rows, width), BF16),
            jax.ShapeDtypeStruct((width, padded), F32),
            jax.ShapeDtypeStruct((width, padded), F32),
            jax.ShapeDtypeStruct((blocks, width, 128), F32),
            jax.ShapeDtypeStruct((blocks, width, 128), F32),
            jax.ShapeDtypeStruct((pairs, 8, padded), F32),
            jax.ShapeDtypeStruct((pairs, 4, 8, 128), F32),
            jax.ShapeDtypeStruct((pairs, 4, 8, 128), F32),
        ],
        scratch_shapes=[
            pltpu.VMEM((TILE, SPAN), F32), pltpu.VMEM((TILE, SPAN), F32),
            pltpu.VMEM((2 * TILE, SPAN), F32), pltpu.VMEM((TILE, 128), F32),
            pltpu.VMEM((2 * TILE, SPAN), BF16), pltpu.VMEM((TILE, 128), BF16),
            pltpu.VMEM((TILE, 8), F32), pltpu.VMEM((8, SPAN), F32),
            pltpu.VMEM((TILE, 128), F32), pltpu.VMEM((TILE, 128), F32),
        ],
        compiler_params=pltpu.CompilerParams(vmem_limit_bytes=VMEM_LIMIT),
        name="attn_backward",
    )(q, dctx, ctx, k_pad, v_pad, kg, vg, cq, ck, rq, rk, rb, rv, pn, pf, g0, g1)
    dq, dkT, dvT, dkgT, dvgT, db, rqg, th = outs
    dbh = db.reshape(pairs, 4, 2, padded).transpose(1, 0, 2, 3).reshape(4, heads, padded) * factor[:, :, None]
    bias_grad = jnp.sum(dbh, axis=2)
    theta_grad = -rich_theta * jnp.sum(th, axis=(2, 3)).reshape(pairs, 2, 2).transpose(2, 0, 1).reshape(2, heads)
    rich_query_grad = (jnp.sum(rqg, axis=2).transpose(1, 0, 2).reshape(4, heads, 64) * factor[:, :, None]).reshape(4, width)
    kvec = rich_key.reshape(4, heads, 64)
    dk_rich = jnp.einsum("chs,che->hes", dbh, kvec, precision=HIGHEST).reshape(width, padded)
    rich_key_grad = jnp.einsum("chs,she->che", dbh, k_pad.astype(F32).reshape(padded, heads, 64), precision=HIGHEST).reshape(4, width)
    dkT = dkT * 0.125 + dk_rich

    def pick(full, factor):
        f = full.reshape(blocks, pairs, 2, 64, 2, 64)
        own = jnp.stack([f[:, :, 0, :, 0, :], f[:, :, 1, :, 1, :]], axis=2)
        return own.transpose(0, 4, 1, 2, 3).reshape(blocks, 64, width) * factor

    return dq, dkT, dvT, pick(dkgT, 0.125), pick(dvgT, 1.0), rich_query_grad, rich_key_grad, bias_grad, theta_grad


def body(
    tokens,
    global_states,
    cotangent,
    w_qkv,
    w_out,
    w_up,
    w_down,
    first_gain,
    first_shift,
    second_gain,
    second_shift,
    rich_query,
    rich_key,
    rich_bias,
    rich_theta,
    bucket_units,
    form_lengths,
    coords,
    glob_owner,
):
    row_count = tokens.shape[1]
    model_width = tokens.shape[2]
    stream_len = row_count * lax.axis_size("seq")
    offset = lax.axis_index("seq") * row_count
    block_count = row_count // QBLOCK
    starts = bucket_starts(bucket_units[0])
    lengths = form_lengths[0]
    coord_pad = jnp.pad(coords[0], ((0, 0), (RADIUS, RADIUS)))

    block_row = offset + QBLOCK * jnp.arange(block_count, dtype=jnp.int32)
    block_form = locate(block_row, starts, lengths, stream_len)[0]
    matches = (glob_owner[0][None, :] == block_form[:, None]).astype(jnp.int32)
    ranks = jnp.cumsum(matches, axis=1) - 1
    slots = jnp.arange(GLOB_FORM, dtype=jnp.int32)
    picked = (matches[:, None, :] == 1) & (ranks[:, None, :] == slots[None, :, None])
    picked = picked.reshape(block_count * GLOB_FORM, glob_owner.shape[1])

    pos_key = offset - RADIUS + jnp.arange(row_count + 2 * RADIUS, dtype=jnp.int32)
    form_key, live_key = locate(pos_key, starts, lengths, stream_len)
    coord_key = lax.dynamic_slice_in_dim(coord_pad, offset, row_count + 2 * RADIUS, 1)
    key_info = jnp.concatenate(
        [
            coord_key.astype(jnp.float32),
            jnp.where(live_key, form_key, -1).astype(jnp.float32)[None],
            jnp.zeros((5, row_count + 2 * RADIUS), jnp.float32),
        ],
        axis=0,
    )
    form_query = jnp.repeat(block_form, QBLOCK).astype(jnp.float32)
    query_info = jnp.stack(
        [
            coord_key[0, RADIUS : RADIUS + row_count].astype(jnp.float32),
            coord_key[1, RADIUS : RADIUS + row_count].astype(jnp.float32),
            form_query,
            jnp.zeros_like(form_query),
        ],
        axis=1,
    )

    every_glob = lax.all_gather(global_states[0], "seq", axis=0, tiled=True)
    inputs = tokens[0].astype(jnp.float32)
    norm_first, pull_first = jax.vjp(layer_norm, inputs, first_gain, first_shift)
    hidden_one = norm_first.astype(jnp.bfloat16)
    projected = jnp.dot(hidden_one, w_qkv, preferred_element_type=jnp.float32).astype(jnp.bfloat16)
    queries = projected[:, :model_width]
    stacked_pairs = jnp.stack(
        [projected[:, model_width : 2 * model_width], projected[:, 2 * model_width :]]
    )
    padded_pairs = padded(stacked_pairs, (("seq", 1),), RADIUS)
    key_pad = padded_pairs[0]
    value_pad = padded_pairs[1]
    pick_low = picked.astype(jnp.bfloat16)
    glob_in = jnp.dot(pick_low, every_glob, preferred_element_type=jnp.float32)
    glob_hidden = layer_norm(glob_in, first_gain, first_shift).astype(jnp.bfloat16)
    w_pair = w_qkv[:, model_width:]
    glob_pairs = jnp.dot(glob_hidden, w_pair, preferred_element_type=jnp.float32)
    glob_pairs = glob_pairs.astype(jnp.bfloat16).reshape(block_count, GLOB_FORM, 2 * model_width)
    glob_keys = glob_pairs[:, :, :model_width]
    glob_values = glob_pairs[:, :, model_width:]
    pull_glob = jax.vjp(
        layer_norm, global_states[0].astype(jnp.float32), first_gain, first_shift
    )[1]
    rich = (rich_query, rich_key, rich_bias, rich_theta)
    context_low, *kept = attn_forward(
        queries, key_pad, value_pad, glob_keys, glob_values, query_info, key_info, *rich
    )
    middle = inputs + jnp.dot(context_low, w_out, preferred_element_type=jnp.float32)
    norm_second, pull_second = jax.vjp(layer_norm, middle, second_gain, second_shift)
    hidden_two = norm_second.astype(jnp.bfloat16)
    pre_act = jnp.dot(hidden_two, w_up, preferred_element_type=jnp.float32)
    activated, pull_gelu = jax.vjp(gelu_exact, pre_act)
    act_low = activated.astype(jnp.bfloat16)
    layer_out = (middle + jnp.dot(act_low, w_down, preferred_element_type=jnp.float32)).astype(
        jnp.bfloat16
    )
    grad_branch = cotangent[0]
    grad_w_down = jnp.einsum("nf,nd->fd", act_low, grad_branch, preferred_element_type=jnp.float32)
    grad_act = jnp.einsum("nd,fd->nf", grad_branch, w_down, preferred_element_type=jnp.float32)
    grad_pre = pull_gelu(grad_act)[0].astype(jnp.bfloat16)
    grad_w_up = jnp.einsum("nd,nf->df", hidden_two, grad_pre, preferred_element_type=jnp.float32)
    grad_hidden_two = jnp.einsum("nf,df->nd", grad_pre, w_up, preferred_element_type=jnp.float32)
    grad_middle_norm, grad_second_gain, grad_second_shift = pull_second(grad_hidden_two)
    grad_middle = grad_branch.astype(jnp.float32) + grad_middle_norm
    grad_attn = grad_middle.astype(jnp.bfloat16)
    grad_w_out = jnp.einsum("nd,ne->de", context_low, grad_attn, preferred_element_type=jnp.float32)
    grad_context = jnp.einsum(
        "ne,de->nd", grad_attn, w_out, preferred_element_type=jnp.float32
    ).astype(jnp.bfloat16)

    (
        query_grads,
        grad_key_pad,
        grad_value_pad,
        grad_glob_key,
        grad_glob_value,
        rich_query_grad,
        rich_key_grad,
        grad_shift,
        grad_width,
    ) = attn_backward(
        queries, grad_context, context_low, key_pad, value_pad, glob_keys, glob_values,
        query_info, key_info, *rich, *kept
    )
    grad_pads = jnp.stack([grad_key_pad.T, grad_value_pad.T])
    rim_send = jnp.concatenate([grad_pads[:, :RADIUS], grad_pads[:, row_count + RADIUS :]], axis=1)
    rim_back = padded(rim_send.astype(jnp.bfloat16), (("seq", 1),), RADIUS).astype(rim_send.dtype)
    own_pairs = grad_pads[:, RADIUS : RADIUS + row_count]
    own_pairs = own_pairs.at[:, :RADIUS].add(rim_back[:, :RADIUS])
    own_pairs = own_pairs.at[:, row_count - RADIUS :].add(rim_back[:, 3 * RADIUS :])
    grad_projected = jnp.concatenate(
        [query_grads, own_pairs[0].astype(jnp.bfloat16), own_pairs[1].astype(jnp.bfloat16)], axis=1
    )
    glob_grad_own = jnp.concatenate([grad_glob_key, grad_glob_value], axis=2).reshape(
        block_count * GLOB_FORM, 2 * model_width
    )
    grad_w_pair = jnp.dot(glob_hidden.astype(jnp.float32).T, glob_grad_own, precision=HIGHEST)
    grad_glob_part = jnp.dot(glob_grad_own, w_pair.astype(jnp.float32).T, precision=HIGHEST)
    grad_glob_part = jnp.dot(picked.astype(jnp.float32).T, grad_glob_part, precision=HIGHEST)
    grad_glob_hidden = lax.psum_scatter(
        grad_glob_part.astype(jnp.bfloat16), "seq", scatter_dimension=0, tiled=True
    ).astype(jnp.float32)
    grad_w_qkv = jnp.einsum(
        "nd,ne->de", hidden_one, grad_projected, preferred_element_type=jnp.float32
    )
    grad_w_qkv = jnp.concatenate(
        [grad_w_qkv[:, :model_width], grad_w_qkv[:, model_width:] + grad_w_pair], axis=1
    )
    grad_hidden_one = jnp.einsum(
        "ne,de->nd", grad_projected, w_qkv, preferred_element_type=jnp.float32
    )
    grad_inputs_norm, grad_gain_tokens, grad_shift_tokens = pull_first(grad_hidden_one)
    grad_glob_in, grad_gain_globals, grad_shift_globals = pull_glob(grad_glob_hidden)
    tokens_grad = (grad_middle + grad_inputs_norm).astype(jnp.bfloat16)
    glob_grad = grad_glob_in.astype(jnp.bfloat16)
    grad_first_gain = grad_gain_tokens + grad_gain_globals
    grad_first_shift = grad_shift_tokens + grad_shift_globals
    every_share = (
        lax.psum_scatter(
            grad_w_up.astype(jnp.bfloat16), "seq", scatter_dimension=0, tiled=True
        ).astype(jnp.float32),
        lax.psum_scatter(
            grad_w_down.astype(jnp.bfloat16), "seq", scatter_dimension=0, tiled=True
        ).astype(jnp.float32),
        lax.psum_scatter(
            grad_second_gain.astype(jnp.bfloat16), "seq", scatter_dimension=0, tiled=True
        ).astype(jnp.float32),
        lax.psum_scatter(
            grad_second_shift.astype(jnp.bfloat16), "seq", scatter_dimension=0, tiled=True
        ).astype(jnp.float32),
        lax.psum_scatter(
            grad_w_qkv.astype(jnp.bfloat16), "seq", scatter_dimension=0, tiled=True
        ).astype(jnp.float32),
        lax.psum_scatter(
            grad_w_out.astype(jnp.bfloat16), "seq", scatter_dimension=0, tiled=True
        ).astype(jnp.float32),
        lax.psum_scatter(
            grad_first_gain.astype(jnp.bfloat16), "seq", scatter_dimension=0, tiled=True
        ).astype(jnp.float32),
        lax.psum_scatter(
            grad_first_shift.astype(jnp.bfloat16), "seq", scatter_dimension=0, tiled=True
        ).astype(jnp.float32),
        lax.psum_scatter(
            rich_query_grad.astype(jnp.bfloat16), "seq", scatter_dimension=1, tiled=True
        ).astype(jnp.float32),
        lax.psum_scatter(
            rich_key_grad.astype(jnp.bfloat16), "seq", scatter_dimension=1, tiled=True
        ).astype(jnp.float32),
    )
    every_share = (
        lax.psum(every_share[0].astype(jnp.bfloat16), "stream").astype(jnp.float32),
        lax.psum(every_share[1].astype(jnp.bfloat16), "stream").astype(jnp.float32),
        lax.psum(every_share[2].astype(jnp.bfloat16), "stream").astype(jnp.float32),
        lax.psum(every_share[3].astype(jnp.bfloat16), "stream").astype(jnp.float32),
        lax.psum(every_share[4].astype(jnp.bfloat16), "stream").astype(jnp.float32),
        lax.psum(every_share[5].astype(jnp.bfloat16), "stream").astype(jnp.float32),
        lax.psum(every_share[6].astype(jnp.bfloat16), "stream").astype(jnp.float32),
        lax.psum(every_share[7].astype(jnp.bfloat16), "stream").astype(jnp.float32),
        lax.psum(every_share[8].astype(jnp.bfloat16), "stream").astype(jnp.float32),
        lax.psum(every_share[9].astype(jnp.bfloat16), "stream").astype(jnp.float32),
    )
    ffn_shares = every_share[:4]
    attn_shares = every_share[4:]
    small_sums = lax.psum((grad_shift, grad_width), ("stream", "seq"))
    return (
        layer_out[None],
        tokens_grad[None],
        glob_grad[None],
        attn_shares[0],
        attn_shares[1],
        ffn_shares[0],
        ffn_shares[1],
        attn_shares[2],
        attn_shares[3],
        ffn_shares[2],
        ffn_shares[3],
        attn_shares[4],
        attn_shares[5],
        small_sums[0],
        small_sums[1],
    )


def solution(mesh):
    return jax.shard_map(
        body,
        mesh=mesh,
        in_specs=(
            P("stream", "seq", None),
            P("stream", "seq", None),
            P("stream", "seq", None),
            P(),
            P(),
            P(),
            P(),
            P(),
            P(),
            P(),
            P(),
            P(),
            P(),
            P(),
            P(),
            P("stream", None),
            P("stream", None),
            P("stream", None, None),
            P("stream", None),
        ),
        out_specs=(
            P("stream", "seq", None),
            P("stream", "seq", None),
            P("stream", "seq", None),
            P("seq", None),
            P("seq", None),
            P("seq", None),
            P("seq", None),
            P("seq"),
            P("seq"),
            P("seq"),
            P("seq"),
            P(None, "seq"),
            P(None, "seq"),
            P(),
            P(),
        ),
        check_vma=False,
    )
```

time: 2770 us -> 679 us (0.25); the launches traced: 2730 us -> 670 us
  matrix products: 1100 us -> 135 us
  other arithmetic: 565 us -> 48.5 us
  local copies, waits for them, and re-layouts: 499 us -> 63 us
  loops' own time: 268 us -> 0 us
  Pallas kernels: 0 us -> 135 us
    dot_general x435 -> x5, matrix products: 977 us -> 12.2 us  [the longest x1 4.08 us: body(): jnp.dot(glob_grad_own, w_pair.astype(jnp.float32).T, precision=HIGHEST)]
    reduce_sum x120 -> x3, other arithmetic: 393 us -> 0.36 us  [the longest x1 0.21 us: attn_backward(): bias_grad = jnp.sum(dbh, axis=2)]
    another operation x6 -> x0, loops' own time: 268 us -> none  [the longest x2 186 us: backward_block(): results = lax.map(backward_one_head, head_items + extra_items)]
    slice x197 -> x3, local copies, waits for them, and re-layouts: 144 us -> 3.97 us  [the longest x2 3.2 us: pick(): own = jnp.stack([f[:, :, 0, :, 0, :], f[:, :, 1, :, 1, :]], axis=2)]
    dynamic_slice x166 -> x0, local copies, waits for them, and re-layouts: 136 us -> none  [the longest x96 39.6 us: forward_block(): contexts, log_totals = lax.map(forward_one_head, head_items)]
    pallas_call x0 -> x2, Pallas kernels: none -> 135 us  [the longest x1 69.5 us: attn_forward(): pl.pallas_call(partial(fwd_kernel, pairs=pairs), grid=(tiles,), in_specs=...]
    dynamic_update_slice x88 -> x0, local copies, waits for them, and re-layouts: 126 us -> none  [the longest x48 61.4 us: backward_block(): results = lax.map(backward_one_head, head_items + extra_items)]
    reduce_scatter x1, waiting for transfers between devices: 43.5 us -> 8.55 us  [body(): lax.psum_scatter(grad_w_qkv.astype(jnp.bfloat16), 'seq', scatter_dimensio...]
  transfers between devices with their start and end apart: 12 -> 12, of which waited for: 5 -> 5; matrix products, arithmetic and copies ran while one was open for 4% -> 17% of each run, Pallas kernels for 0% -> 0%
where the time goes in v1:
time: 679 us; the launch traced here: 670 us
  waiting for transfers between devices  179 us (26%)
  matrix products  135 us (20%)
  Pallas kernels  135 us (20%)
  blocking collectives  84.7 us (12%)
  local copies, waits for them, and re-layouts  63 us (9%)
  other arithmetic  48.5 us (7%)
  between operations  16.4 us (2%)
  starting transfers between devices  8.19 us (1%)
    pallas_call x1, Pallas kernels, attn_forward(): pl.pallas_call(partial(fwd_kernel, pairs=pairs), grid=(tiles,), in_specs=...  69.5 us
    pallas_call x1, Pallas kernels, attn_backward(): pl.pallas_call(partial(bwd_kernel, pairs=pairs, per_block=per_block), gri...  65.2 us
    reduce_scatter x1, waiting for transfers between devices, body(): lax.psum_scatter(grad_w_up.astype(jnp.bfloat16), 'seq', scatter_dimension...  55.8 us
    reduce_scatter x1, waiting for transfers between devices, body(): lax.psum_scatter(grad_w_down.astype(jnp.bfloat16), 'seq', scatter_dimensi...  55.6 us
    psum x1, blocking collectives, body(): small_sums = lax.psum((grad_shift, grad_width), ('stream', 'seq'))  42.5 us
    dot_general x1, matrix products, body(): pre_act = jnp.dot(hidden_two, w_up, preferred_element_type=jnp.float32)  35.6 us
    psum x1, waiting for transfers between devices, body(): lax.psum(every_share[4].astype(jnp.bfloat16), 'stream').astype(jnp.float32)  35.4 us
    unnamed x170, local copies, waits for them, and re-layouts  28.4 us
  transfers between devices with their start and end apart: 12, of which 5 were waited for; matrix products, arithmetic and copies ran while one was open for 17% of the time, Pallas kernels for 0%

profile of v1, /device:TPU:0, one launch (start us, length us, event | category | flops | bytes accessed | tf_op | source)
XLA Modules:
  0.0 669.5 jit_solution(10162013582464278271)
XLA Ops:
  9.9 6.4 convolution_convert_fusion
  29.6 18.1 %all-gather = bf16[1,256,768]{2,1,0:T(8,128)(2,1)S(1)} all-gather(bf16[1,32,768]{2,1,0:T(8,128)(2,1)S(1)} %copy-done.29), channel_id=2, replica_groups=mesh['stream'=4,'seq'=8] {'seq'}, dimensions={1}, use_global_device_ids=true | all-gather | bytes 442368 | tf_op jit(solution)/shard_map/all_gather | solution.py:479
  62.7 2.7 fusion.82
  65.4 69.5 %attn_forward.1 = (bf16[1024,768]{1,0:T(8,128)(2,1)}, bf16[8,12,128,384]{3,2,1,0:T(8,128)(2,1)}, bf16[8,6,128,128]{3,2,1,0:T(8,128)(2,1)}, bf16[8,12,128,384]{3,2,1,0:T(8,128)(2,1)}, bf16[8,12,128,384]{3,2,1,0:T(8,128)(2,1)}) custom-call(f32[12,2]{1,0:T(8,128)} %get-tuple-element.223.w_ref, bf16[1024,768]{1,0:T(8,128)(2,1)} %get-tuple-element.188.q_ref, ...), custom_call_target="tpu_custom_call" | custom-call | tf_op jit(solution)/shard_map/attn_forward/pallas_call | solution.py:307
  135.0 3.1 fusion.88
  138.9 35.6 %multiply_convert_fusion = (bf16[1024,3072]{1,0:T(8,128)(2,1)}, f32[1024,3072]{1,0:T(8,128)}, f32[1024,3072]{1,0:T(8,128)}) fusion(bf16[768,3072]{1,0:T(8,128)(2,1)S(1)} %bitcast.278, f32[1024,768]{0,1:T(8,128)S(1)} %get-tuple-element.238, f32[768]{0:T(1024)S(1)} %copy-done.69, f32[768]{0:T(1024)S(1)} %copy-done.56, f32[1024]{0:T(1024)S(1)} %fusion.65, ...), kind=kOutput, calls=%fused_computation.3 | convolution fusion | flops 5040242688 | bytes 39335936 | tf_op jit(solution)/shard_map/dot_general | solution.py:509
  174.5 15.8 %add_convert_fusion = bf16[1024,3072]{1,0:T(8,128)(2,1)} fusion(f32[1024,3072]{1,0:T(8,128)} %get-tuple-element.185, f32[1024,3072]{1,0:T(8,128)} %get-tuple-element.239, bf16[3072,768]{1,0:T(8,128)(2,1)} %param.29, bf16[1,1024,768]{2,1,0:T(8,128)(2,1)S(1)} %copy-done.23), kind=kOutput, calls=%fused_computation.2 | convolution fusion | flops 4875878400 | bytes 37748736 | tf_op jit(solution)/shard_map/nd,fd->nf/dot_general | solution.py:517
  190.3 10.5 %fusion.90 = (bf16[768]{0:T(1024)(128)(2,1)}, f32[1024,768]{1,0:T(8,128)}) fusion(bf16[1024,3072]{1,0:T(8,128)(2,1)} %add_convert_fusion, bf16[768,3072]{1,0:T(8,128)(2,1)} %param.28), kind=kOutput, calls=%fused_computation.225 | convolution fusion | flops 4832623616 | bytes 14157312 | tf_op jit(solution)/shard_map/nf,df->nd/dot_general | solution.py:520
  200.8 3.5 copy.240
  204.3 4.5 multiply_reduce_fusion
  216.6 65.2 %attn_backward.1 = (bf16[1024,768]{1,0:T(8,128)(2,1)}, f32[768,1280]{1,0:T(8,128)}, f32[768,1280]{1,0:T(8,128)}, f32[2,768,128]{2,1,0:T(8,128)}, f32[2,768,128]{...) custom-call(bf16[1024,768]{1,0:T(8,128)(2,1)} %get-tuple-element.188.q_ref, ...), custom_call_target="tpu_custom_call" | custom-call | tf_op jit(solution)/shard_map/attn_backward/pallas_call | solution.py:356
  283.0 2.7 reshape.492
  290.0 3.3 fusion.58
  293.8 3.0 copy-done.7
  300.7 3.2 fusion.32
  317.3 3.6 fusion.7
  326.4 4.1 fusion.26
  335.7 9.8 %convolution_convert_fusion.2 = bf16[768,3072]{1,0:T(8,128)(2,1)} fusion(bf16[1024,3072]{1,0:T(8,128)(2,1)} %add_convert_fusion, f32[1024,768]{0,1:T(8,128)} %copy-done.9, f32[768]{0:T(1024)S(1)} %copy-done.70, f32[768]{0:T(1024)S(1)} %copy-done.57, f32[1024]{0:T(1024)S(1)} %copy-done.53, f32[1024]{0:T(1024)S(1)} %broadcast_multiply_fusion.1), kind=kOutput, calls=%fused_computation.26 | convolution fusion | flops 4838129664 | bytes 14170112 | tf_op jit(solution)/shard_map/nd,nf->df/dot_general | solution.py:519
  345.8 9.2 %convolution_convert_fusion.1 = bf16[3072,768]{1,0:T(8,128)(2,1)} fusion(bf16[1024,3072]{1,0:T(8,128)(2,1)} %get-tuple-element.184, bf16[1,1024,768]{2,1,0:T(8,128)(2,1)} %param.25), kind=kOutput, calls=%fused_computation.25 | convolution fusion | flops 4834197504 | bytes 12582912 | tf_op jit(solution)/shard_map/nf,nd->fd/dot_general | solution.py:516
  357.7 42.5 %all-reduce.7 = (f32[4,12]{0,1:T(8,128)S(1)}, f32[2,12]{1,0:T(2,128)}) all-reduce(f32[4,12]{0,1:T(8,128)S(1)} %reduce_sum.328, f32[2,12]{1,0:T(2,128)S(1)} %negate_multiply_fusion.3), channel_id=1, replica_groups=mesh['stream'=4,'seq'=8] {'stream','seq'}, use_global_device_ids=true, to_apply=%region_50.51 | all-reduce | flops 72 | bytes 576 | tf_op jit(solution)/shard_map/psum | solution.py:622
  400.8 10.0 %fusion.31 = bf16[1,1024,768]{1,2,0:T(8,128)(2,1)} fusion(f32[1024,768]{0,1:T(8,128)} %copy-done.9, bf16[1024,3072]{1,0:T(8,128)(2,1)} %get-tuple-element.184, bf16[3072,768]{1,0:T(8,128)(2,1)} %param.29), kind=kOutput, calls=%fused_computation.75 | convolution fusion | flops 4833411072 | bytes 15728640 | tf_op jit(solution)/shard_map/dot_general | solution.py:512
  413.4 4.1 fusion.22
  420.8 9.1 %fusion.89 = (f32[768]{0:T(1024)S(1)}, f32[1024,768]{1,0:T(8,128)}) fusion(bf16[768,2304]{1,0:T(8,128)(2,1)} %param.26, bf16[1024,768]{0,1:T(8,128)(2,1)} %copy-done.26, bf16[1024,768]{0,1:T(8,128)(2,1)} %copy-done.25, bf16[1024,768]{0,1:T(8,128)(2,1)} %copy.251), kind=kOutput, calls=%fused_computation.224 | convolution fusion | flops 3638820096 | bytes 11406336 | tf_op jit(solution)/shard_map/ne,de->nd/dot_general | solution.py:567
  429.9 3.6 copy.252
  437.7 8.6 %reduce-scatter.14.cloned.1.call-done = bf16[96,2304]{1,0:T(8,128)(2,1)} async-done(((bf16[768,2304]{1,0:T(8,128)(2,1)}), bf16[96,2304]{1,0:T(8,128)(2,1)}) %reduce-scatter.14.cloned.1.call-update) | async-done | bytes 442384 | tf_op jit(solution)/shard_map/reduce_scatter | solution.py:589
  446.3 55.8 %reduce-scatter.18.cloned.1.call-done = bf16[96,3072]{1,0:T(8,128)(2,1)} async-done(((bf16[768,3072]{1,0:T(8,128)(2,1)}), bf16[96,3072]{1,0:T(8,128)(2,1)}) %reduce-scatter.18.cloned.1.call-update) | async-done | bytes 589840 | tf_op jit(solution)/shard_map/reduce_scatter | solution.py:577
  502.1 55.6 %reduce-scatter.20.cloned.1.call-done = bf16[384,768]{1,0:T(8,128)(2,1)} async-done(((bf16[3072,768]{1,0:T(8,128)(2,1)}), bf16[384,768]{1,0:T(8,128)(2,1)}) %reduce-scatter.20.cloned.1.call-update) | async-done | bytes 589840 | tf_op jit(solution)/shard_map/reduce_scatter | solution.py:580
  557.7 6.0 fusion.28
  566.4 23.2 %reduce-scatter.12.cloned.1.call-done = bf16[32,768]{1,0:T(8,128)(2,1)} async-done(((bf16[256,768]{1,0:T(8,128)(2,1)}), bf16[32,768]{1,0:T(8,128)(2,1)}) %reduce-scatter.12.cloned.1.call-update) | async-done | bytes 49168 | tf_op jit(solution)/shard_map/reduce_scatter | solution.py:558
  591.7 14.0 %all-reduce.8 = (bf16[768]{0:T(1024)(128)(2,1)S(1)}, bf16[768]{0:T(1024)(128)(2,1)S(1)}, bf16[768]{0:T(1024)(128)(2,1)S(1)}, bf16[768]{0:T(1024)(128)(2,1)S(1)}) all-reduce(bf16[768]{0:T(1024)(128)(2,1)S(1)} %add_convert_fusion.7, bf16[768]{0:T(1024)(128)(2,1)S(1)} %add_convert_fusion.6, ...), channel_id=8, replica_groups=mesh['stream'=4,'seq'=8] {'seq'}, use_global_device_ids=true, to_apply=%region_32.33.clone | all-reduce | flops 3072 | bytes 12288
  606.0 10.1 %all-reduce.9 = (bf16[96]{0:T(256)(128)(2,1)S(1)}, bf16[96]{0:T(256)(128)(2,1)S(1)}, bf16[96]{0:T(256)(128)(2,1)S(1)}, bf16[96]{0:T(256)(128)(2,1)S(1)}, bf16[4,...) all-reduce(bf16[96]{0:T(256)(128)(2,1)S(1)} %dynamic-slice.17, ...), channel_id=1, replica_groups=mesh['stream'=4,'seq'=8] {'stream'}, use_global_device_ids=true, to_apply=%region_33.34 | all-reduce | flops 1152 | bytes 4608 | tf_op jit(solution)/shard_map/psum | solution.py:615
  620.7 35.4 %all-reduce.13.cloned.1.call-done = (bf16[96,2304]{1,0:T(8,128)(2,1)}, bf16[96,768]{1,0:T(8,128)(2,1)}, bf16[96,3072]{1,0:T(8,128)(2,1)}, bf16[384,768]{1,0:T(8,128)(2,1)}) async-done(((bf16[96,2304]{1,0:T(8,128)(2,1)}, bf16[96,768]{1,0:T(8,128)(2,1)}, bf16[96,3072]{1,0:T(8,128)(2,1)}, bf16[384,768]{1,0:T(8,128)(2,1)}), (bf16[96,2304]{1,0:T(8,128)(2,1)}, bf16[96,768]{1,0:T(8,128)(2,1)}, ...) | async-done | bytes 1769488 | tf_op jit(solution)/shard_map/psum | solution.py:613
  (345 shorter events, 101.2 us)
Async XLA Ops:
  7.2 127.8 %copy-start = (bf16[768,768]{1,0:T(8,128)(2,1)S(1)}, bf16[768,768]{1,0:T(8,128)(2,1)}, u32[]{:S(2)}) copy-start(bf16[768,768]{1,0:T(8,128)(2,1)} %param.27) | copy-start | bytes 3538948
  7.2 411.9 %reduce-scatter.24.cloned.1.call-start = ((), (), s32[]{:S(2)}) async-start(), calls=%async_computation.13 | async-start | bytes 221184
  9.1 125.9 %copy-start.4 = (bf16[1,1024,768]{1,2,0:T(8,128)(2,1)}, bf16[1,1024,768]{1,2,0:T(8,128)(2,1)S(1)}, u32[]{:S(2)}) copy-start(bf16[1,1024,768]{1,2,0:T(8,128)(2,1)S(1)} %copy.229) | copy-start | bytes 4718596
  9.4 6.9 %copy-start.39 = (f32[1024]{0:T(1024)}, f32[1024]{0:T(1024)S(1)}, u32[]{:S(2)}) copy-start(f32[1024]{0:T(1024)S(1)} %broadcast_multiply_fusion.2) | copy-start | bytes 12292
  17.8 9.0 %copy-start.64 = (f32[4,12]{1,0:T(4,128)S(1)}, f32[4,12]{1,0:T(4,128)}, u32[]{:S(2)}) copy-start(f32[4,12]{1,0:T(4,128)} %param.36) | copy-start | bytes 580
  17.8 9.3 %copy-start.46 = (f32[4,768]{1,0:T(4,128)S(1)}, f32[4,768]{1,0:T(4,128)}, u32[]{:S(2)}) copy-start(f32[4,768]{1,0:T(4,128)} %param.34) | copy-start | bytes 36868
  17.8 10.5 %copy-start.61 = (s32[1,256]{1,0:T(1,128)S(1)}, s32[1,256]{1,0:T(1,128)}, u32[]{:S(2)}) copy-start(s32[1,256]{1,0:T(1,128)} %param.41) | copy-start | bytes 3076
  17.8 11.8 %copy-start.29 = (bf16[1,32,768]{2,1,0:T(8,128)(2,1)S(1)}, bf16[1,32,768]{2,1,0:T(8,128)(2,1)}, u32[]{:S(2)}) copy-start(bf16[1,32,768]{2,1,0:T(8,128)(2,1)} %param.24) | copy-start | bytes 147460
  19.8 40.6 %collective-permute-start = (bf16[2,128,768]{2,1,0:T(8,128)(2,1)}, bf16[2,128,768]{2,1,0:T(8,128)(2,1)S(1)}, u32[]{:S(2)}, u32[]{:S(2)}) collective-permute-start(bf16[2,128,768]{2,1,0:T(8,128)(2,1)} %get-tuple-element.196), channel_id=1, source_target_pairs={{0,1},{1,2},{2,3},{3,4},{4,5},{5,6},{6,7},{8,9},{9,10},{10,11},{11... | collective-permute-start | bytes 1179656 | tf_op jit(solution)/shard_map/ppermute | solution.py:28
  22.2 38.3 %collective-permute-start.1 = (bf16[2,128,768]{2,1,0:T(8,128)(2,1)}, bf16[2,128,768]{2,1,0:T(8,128)(2,1)}, u32[]{:S(2)}, u32[]{:S(2)}) collective-permute-start(bf16[2,128,768]{2,1,0:T(8,128)(2,1)} %get-tuple-element.197), channel_id=1, source_target_pairs={{1,0},{2,1},{3,2},{4,3},{5,4},{6,5},{7,6},{9,8},{10,9},{11,10},{12... | collective-permute-start | bytes 1179656 | tf_op jit(solution)/shard_map/ppermute | solution.py:29
  27.9 24.1 %copy-start.35 = (s32[1,2,8192]{2,1,0:T(2,128)S(1)}, s32[1,2,8192]{2,1,0:T(2,128)}, u32[]{:S(2)}) copy-start(s32[1,2,8192]{2,1,0:T(2,128)} %param.40) | copy-start | bytes 196612
  51.2 7.2 %copy-start.68 = (s32[1,4]{1,0:T(1,128)S(1)}, s32[1,4]{1,0:T(1,128)}, u32[]{:S(2)}) copy-start(s32[1,4]{1,0:T(1,128)} %param.39) | copy-start | bytes 52
  138.1 36.4 %copy-start.9 = (f32[1024,768]{0,1:T(8,128)}, f32[1024,768]{0,1:T(8,128)S(1)}, u32[]{:S(2)}) copy-start(f32[1024,768]{0,1:T(8,128)S(1)} %get-tuple-element.238) | copy-start | bytes 9437188
  138.9 70.0 %copy-start.52 = (f32[1024]{0:T(1024)}, f32[1024]{0:T(1024)S(1)}, u32[]{:S(2)}) copy-start(f32[1024]{0:T(1024)S(1)} %fusion.65) | copy-start | bytes 12292
  138.9 35.6 %copy-start.23 = (bf16[1,1024,768]{2,1,0:T(8,128)(2,1)S(1)}, bf16[1,1024,768]{2,1,0:T(8,128)(2,1)}, u32[]{:S(2)}) copy-start(bf16[1,1024,768]{2,1,0:T(8,128)(2,1)} %param.25) | copy-start | bytes 4718596
  283.0 6.9 %copy-start.20 = (f32[6,4,2,1280]{3,2,1,0:T(2,128)}, f32[6,4,2,1280]{3,2,1,0:T(2,128)S(1)}, u32[]{:S(2)}) copy-start(f32[6,4,2,1280]{3,2,1,0:T(2,128)S(1)} %reshape.487) | copy-start | bytes 737284
  298.4 6.5 copy-start.43
  304.9 115.1 %reduce-scatter.22.cloned.1.call-start = ((), (), s32[]{:S(2)}) async-start(), calls=%async_computation.12 | async-start | bytes 221184
  309.5 128.2 %reduce-scatter.16.cloned.1.call-start = ((), (), s32[]{:S(2)}) async-start(), calls=%async_computation.9 | async-start | bytes 1327104 | tf_op jit(solution)/shard_map/reduce_scatter | solution.py:592
  310.8 10.1 %collective-permute-start.2 = (bf16[2,128,768]{1,2,0:T(8,128)(2,1)S(1)}, bf16[2,128,768]{1,2,0:T(8,128)(2,1)S(1)}, u32[]{:S(2)}, u32[]{:S(2)}) collective-permute-start(bf16[2,128,768]{1,2,0:T(8,128)(2,1)S(1)} %get-tuple-element.192), channel_id=1, source_target_pairs={{0,1},{1,2},{2,3},{3,4},{4,5},{5,6},{6,7},{8,9},{9,10},{10,11},{11... | collective-permute-start | bytes 1179656 | tf_op jit(solution)/shard_map/ppermute | solution.py:28
  313.1 7.8 %collective-permute-start.3 = (bf16[2,128,768]{1,2,0:T(8,128)(2,1)S(1)}, bf16[2,128,768]{1,2,0:T(8,128)(2,1)S(1)}, u32[]{:S(2)}, u32[]{:S(2)}) collective-permute-start(bf16[2,128,768]{1,2,0:T(8,128)(2,1)S(1)} %get-tuple-element.193), channel_id=1, source_target_pairs={{1,0},{2,1},{3,2},{4,3},{5,4},{6,5},{7,6},{9,8},{10,9},{11,10},{12... | collective-permute-start | bytes 1179656 | tf_op jit(solution)/shard_map/ppermute | solution.py:29
  317.0 129.3 %reduce-scatter.14.cloned.1.call-start = ((), (), s32[]{:S(2)}) async-start(), calls=%async_computation.8 | async-start | bytes 3981312 | tf_op jit(solution)/shard_map/reduce_scatter | solution.py:589
  323.7 6.8 %copy-start.25 = (bf16[1024,768]{0,1:T(8,128)(2,1)}, bf16[1024,768]{0,1:T(8,128)(2,1)S(1)}, u32[]{:S(2)}) copy-start(bf16[1024,768]{0,1:T(8,128)(2,1)S(1)} %get-tuple-element.194) | copy-start | bytes 4718596
  323.7 6.8 %copy-start.26 = (bf16[1024,768]{0,1:T(8,128)(2,1)}, bf16[1024,768]{0,1:T(8,128)(2,1)S(1)}, u32[]{:S(2)}) copy-start(bf16[1024,768]{0,1:T(8,128)(2,1)S(1)} %get-tuple-element.195) | copy-start | bytes 4718596
  335.0 167.1 %reduce-scatter.18.cloned.1.call-start = ((), (), s32[]{:S(2)}) async-start(), calls=%async_computation.10 | async-start | bytes 5308416 | tf_op jit(solution)/shard_map/reduce_scatter | solution.py:577
  345.5 212.1 %reduce-scatter.20.cloned.1.call-start = ((), (), s32[]{:S(2)}) async-start(), calls=%async_computation.11 | async-start | bytes 5308416 | tf_op jit(solution)/shard_map/reduce_scatter | solution.py:580
  355.0 234.5 %reduce-scatter.12.cloned.1.call-start = ((), (), s32[]{:S(2)}) async-start(), calls=%async_computation.7 | async-start | bytes 442368 | tf_op jit(solution)/shard_map/reduce_scatter | solution.py:558
  410.8 6.7 copy-start.34
  418.8 237.3 %all-reduce.13.cloned.1.call-start = ((), (), s32[]{:S(2)}) async-start(), calls=%async_computation.14 | async-start | bytes 3538944 | tf_op jit(solution)/shard_map/psum | solution.py:613
  563.7 27.9 %copy-start.58 = (bf16[768]{0:T(1024)(128)(2,1)S(1)}, bf16[768]{0:T(1024)(128)(2,1)}, u32[]{:S(2)}) copy-start(bf16[768]{0:T(1024)(128)(2,1)} %get-tuple-element.155) | copy-start | bytes 4612
  563.7 28.0 %copy-start.65 = (bf16[768]{0:T(1024)(128)(2,1)S(1)}, bf16[768]{0:T(1024)(128)(2,1)}, u32[]{:S(2)}) copy-start(bf16[768]{0:T(1024)(128)(2,1)} %get-tuple-element.242) | copy-start | bytes 4612
  563.7 98.5 %copy-start.1 = (bf16[768,768]{1,0:T(8,128)(2,1)S(1)}, bf16[768,768]{1,0:T(8,128)(2,1)}, u32[]{:S(2)}) copy-start(bf16[768,768]{1,0:T(8,128)(2,1)} %param.27) | copy-start | bytes 3538948
  (55 other events, 187.0 us)
Sparse Core Ops, SparseCore 0:
  305.0 31.5 reduce-scatter.23
  339.5 28.4 reduce-scatter.21
  370.8 30.9 reduce-scatter.15
  404.0 42.2 reduce-scatter.13
  448.5 53.4 reduce-scatter.17
  504.3 53.2 reduce-scatter.19
  560.6 28.9 reduce-scatter.11
  593.0 63.0 all-reduce.12

commit v2 on v1

v2 whole, which is shorter than its diff:
```python
from functools import partial
import math

import jax
import jax.numpy as jnp
from jax import lax
from jax.experimental import pallas as pl
from jax.experimental.pallas import tpu as pltpu
from jax.sharding import PartitionSpec as P

RADIUS = 128
GLOB_FORM = 64
QBLOCK = 512
TOK_DEV = 1024


EPSILON = 1e-06


TILE = 128
SPAN = 384
LOG2E = math.log2(math.e)
FAR_AWAY = 1e15
CH = 16
F32 = jnp.float32
BF16 = jnp.bfloat16
VMEM_LIMIT = 58 * 1024 * 1024


def mm(a, b):
    return lax.dot_general(a, b, (((1,), (0,)), ((), ())), preferred_element_type=F32)


def mm_nt(a, b):
    return lax.dot_general(a, b, (((1,), (1,)), ((), ())), preferred_element_type=F32)


def mm_tn(a, b):
    return lax.dot_general(a, b, (((0,), (0,)), ((), ())), preferred_element_type=F32)


def norm_parts(values):
    centre = jnp.mean(values, axis=-1, keepdims=True)
    centred = values - centre
    spread = jnp.mean(centred * centred, axis=-1, keepdims=True)
    scale = lax.rsqrt(spread + EPSILON)
    return centred * scale, scale


def norm_pull(grad, normed, scale, gain):
    e = grad * gain
    mean_e = jnp.mean(e, axis=-1, keepdims=True)
    mean_en = jnp.mean(e * normed, axis=-1, keepdims=True)
    return scale * (e - mean_e - normed * mean_en)


def split3(values):
    hi = values.astype(BF16).astype(F32)
    rest = values - hi
    mid = rest.astype(BF16).astype(F32)
    return hi, mid, rest - mid


def half_masks(dtype):
    lane = lax.broadcasted_iota(jnp.int32, (1, 128), 1)
    low = (lane < 64).astype(F32)
    return low.astype(dtype), (1.0 - low).astype(dtype)


def by_row(values):
    row = lax.broadcasted_iota(jnp.int32, (8, 128), 0)
    out = jnp.full((8, 128), values[7], F32)
    for index in range(7):
        out = jnp.where(row == index, values[index], out)
    return out


def rich_rows(vectors, scales):
    row = lax.broadcasted_iota(jnp.int32, (8, 128), 0)
    lane = lax.broadcasted_iota(jnp.int32, (8, 128), 1)
    both = jnp.concatenate([vectors, vectors], axis=0)
    both = both if scales is None else both * scales
    return jnp.where((row < 4) == (lane < 64), both, 0.0)


def rich_sums(qp, kp, query_vec, key_vec, scales, bias8):
    rq = jnp.concatenate(split3(rich_rows(query_vec, scales)), axis=1).astype(BF16)
    rk = jnp.concatenate(split3(rich_rows(key_vec, scales)), axis=0).astype(BF16)
    a = mm_nt(jnp.concatenate([qp, qp, qp], axis=1), rq)
    b24 = mm_nt(rk, kp)
    return a, b24[0:8] + b24[8:16] + b24[16:24] + bias8[:, 0:1]


def form_of(units_ref, lengths_ref, row):
    form, low, high, before = 0, 0, lengths_ref[0, 0], 0
    for index in range(1, units_ref.shape[1]):
        before = before + units_ref[0, index - 1]
        start = TOK_DEV // 2 + TOK_DEV * before
        taken = row >= start
        form = jnp.where(taken, index, form)
        low = jnp.where(taken, start, low)
        high = jnp.where(taken, start + lengths_ref[0, index], high)
    return form, low, high


def coord_row(coords_ref, axis, tile_index):
    tile_index = jnp.clip(tile_index, 0, coords_ref.shape[1] // 128 - 1)
    return coords_ref[axis : axis + 1, pl.ds(pl.multiple_of(tile_index * 128, 128), 128)].astype(F32)


def query_columns(coords_ref, axis, tile_index):
    return jnp.transpose(jnp.broadcast_to(coord_row(coords_ref, axis, tile_index), (128, 128)))


def geometry_into(coords_ref, first_tile, span, refs):
    ox_ref, oy_ref, dx_ref, dy_ref = refs
    xq = query_columns(coords_ref, 0, first_tile + 1)
    yq = query_columns(coords_ref, 1, first_tile + 1)
    for lt in range(3):
        xk = coord_row(coords_ref, 0, first_tile + lt)
        yk = coord_row(coords_ref, 1, first_tile + lt)
        out = (slice(None), slice(lt * 128, lt * 128 + 128))
        dx = jnp.log(1.0 + jnp.abs(xq - xk))
        dy = jnp.log(1.0 + jnp.abs(yq - yk))
        if span is not None:
            row = lax.broadcasted_iota(jnp.int32, (128, 128), 0)
            col = lax.broadcasted_iota(jnp.int32, (128, 128), 1) + lt * 128
            near = (col >= row) & (col - row <= 2 * RADIUS)
            dx = jnp.where(near & (col >= span[0]) & (col < span[1]), dx, FAR_AWAY)
            ox_ref[out] = jnp.where(xk > xq, 1.0, -1.0)
            oy_ref[out] = jnp.where(yk > yq, 1.0, -1.0)
        dx_ref[out] = dx
        dy_ref[out] = dy


def qkv_kernel(tok_ref, w_ref, norms_ref, q_ref, k_ref, v_ref, ht_ref):
    width = tok_ref.shape[1]
    normed, _ = norm_parts(tok_ref[...].astype(F32))
    hidden = (normed * norms_ref[0:1, :] + norms_ref[1:2, :]).astype(BF16)
    for index, out in enumerate((q_ref, k_ref, v_ref)):
        out[...] = mm(hidden, w_ref[:, index * width : (index + 1) * width]).astype(BF16)
    ht_ref[...] = jnp.transpose(hidden)


def project_tokens(tokens, w_qkv, norms):
    rows, width = tokens.shape
    step = 256
    block = pl.BlockSpec((step, width), lambda i: (i, 0))
    return pl.pallas_call(
        qkv_kernel,
        grid=(rows // step,),
        in_specs=[block, pl.BlockSpec(w_qkv.shape, lambda i: (0, 0)), pl.BlockSpec(norms.shape, lambda i: (0, 0))],
        out_specs=[block, block, block, pl.BlockSpec((width, step), lambda i: (0, i))],
        out_shape=[jax.ShapeDtypeStruct((rows, width), BF16)] * 3 + [jax.ShapeDtypeStruct((width, rows), BF16)],
        compiler_params=pltpu.CompilerParams(vmem_limit_bytes=VMEM_LIMIT),
        cost_estimate=cost(8.0),
        name="project_tokens",
    )(tokens, w_qkv, norms)


def cost(micros):
    return pl.CostEstimate(flops=int(micros * 1e9), bytes_accessed=0, transcendentals=0)


def global_pairs(form, owner_ref, glob_ref, norms_ref, kw_ref, vw_ref, kg_ref, vg_ref, hg_ref, ng_ref, oh_ref):
    count = glob_ref.shape[0]
    match = (owner_ref[...] == form).astype(F32)
    row = lax.broadcasted_iota(jnp.int32, (count, count), 0)
    col = lax.broadcasted_iota(jnp.int32, (count, count), 1)
    upto = (row <= col).astype(F32).astype(BF16)
    rank = mm(jnp.broadcast_to(match, (16, count)).astype(BF16), upto)[0:1]
    slot = lax.broadcasted_iota(jnp.int32, (GLOB_FORM, count), 0).astype(F32) + 1.0
    picked = jnp.where(rank == slot, match, 0.0).astype(BF16)
    oh_ref[0] = picked
    normed, _ = norm_parts(mm(picked, glob_ref[...]))
    ng_ref[0] = normed
    hidden = (normed * norms_ref[0:1, :] + norms_ref[1:2, :]).astype(BF16)
    hg_ref[0] = hidden
    kg_ref[0] = mm(hidden, kw_ref[...]).astype(BF16)
    vg_ref[0] = mm(hidden, vw_ref[...]).astype(BF16)


def fwd_kernel(units_ref, lengths_ref, offset_ref, bias_ref, theta_ref,
               q_ref, k_ref, v_ref, before_ref, after_ref, glob_ref, owner_ref, kw_ref, vw_ref, norms_ref,
               coords_ref, rq_ref, rk_ref,
               ctx_ref, pn_ref, pf_ref, g0_ref, g1_ref, kp_ref, vp_ref, kg_ref, vg_ref, hg_ref, ng_ref, oh_ref,
               ox_ref, oy_ref, dx_ref, dy_ref, s_ref, sf_ref, a_ref, b_ref, *, pairs, per_block):
    t = pl.program_id(0)
    rows_all = k_ref.shape[0]
    offset = offset_ref[0, 0]
    first = offset + t * TILE
    form, low_end, high_end = form_of(units_ref, lengths_ref, first)

    @pl.when(t == 0)
    def _():
        for refs in ((k_ref, kp_ref, kw_ref), (v_ref, vp_ref, vw_ref)):
            own, padded_ref, weight = refs
            padded_ref[RADIUS : RADIUS + rows_all, :] = own[...]
        for halo, start in ((before_ref, 0), (after_ref, RADIUS + rows_all)):
            normed, _ = norm_parts(halo[...].astype(F32))
            hidden = (normed * norms_ref[0:1, :] + norms_ref[1:2, :]).astype(BF16)
            kp_ref[start : start + RADIUS, :] = mm(hidden, kw_ref[...]).astype(BF16)
            vp_ref[start : start + RADIUS, :] = mm(hidden, vw_ref[...]).astype(BF16)

    @pl.when(t % per_block == 0)
    def _():
        global_pairs(form, owner_ref, glob_ref, norms_ref, kw_ref, vw_ref, kg_ref, vg_ref, hg_ref, ng_ref, oh_ref)

    shifted = first - RADIUS
    geometry_into(coords_ref, offset // 128 + t - 1, (low_end - shifted, high_end - shifted), (ox_ref, oy_ref, dx_ref, dy_ref))
    lo16, hi16 = half_masks(BF16)
    lane = lax.broadcasted_iota(jnp.int32, (CH, 128), 1)
    low = lane < 64
    rows = pl.ds(pl.multiple_of(t * TILE, TILE), SPAN)
    root = math.sqrt(0.5 * LOG2E)

    def one_pair(p, carry):
        cols = pl.ds(pl.multiple_of(p * 128, 128), 128)
        qp = q_ref[:, cols]
        kp = kp_ref[rows, cols]
        vp = vp_ref[rows, cols]
        kgp = kg_ref[0, :, cols]
        vgp = vg_ref[0, :, cols]
        widths = [[theta_ref[i, 2 * p + e] * root for i in range(2)] for e in range(2)]
        scales = by_row([LOG2E, LOG2E] + widths[0] + [LOG2E, LOG2E] + widths[1])
        biases = by_row([bias_ref[c, 2 * p + e] for e in range(2) for c in range(4)]) * scales
        s_ref[...] = mm_nt(jnp.concatenate([qp * lo16, qp * hi16], axis=0), kp)
        sf_ref[...] = mm_nt(qp, jnp.concatenate([kgp * lo16, kgp * hi16], axis=0))
        a, b = rich_sums(qp, kp, rq_ref[:, cols], rk_ref[:, cols], scales, biases)
        a_ref[...] = a
        b_ref[...] = b
        for r in range(0, TILE, CH):
            rs = slice(r, r + CH)
            far = sf_ref[rs, :] * (0.125 * LOG2E)
            tops = []
            held = []
            for e in range(2):
                base = 4 * e
                part = [a_ref[rs, base + c : base + c + 1] for c in range(4)]
                line = [b_ref[base + c : base + c + 1, :] for c in range(4)]
                u0 = (part[0] + line[0]) * ox_ref[rs, :]
                u1 = (part[1] + line[1]) * oy_ref[rs, :]
                e0 = jnp.exp2(jnp.minimum(u0, -u0))
                e1 = jnp.exp2(jnp.minimum(u1, -u1))
                f0 = 1.0 + e0
                f1 = 1.0 + e1
                rr = 1.0 / (f0 * f1)
                gx = (widths[e][0] * dx_ref[rs, :] - part[2]) - line[2]
                gy = (widths[e][1] * dy_ref[rs, :] - part[3]) - line[3]
                s = s_ref[e * TILE + r : e * TILE + r + CH, :] * (0.125 * LOG2E)
                s = s + jnp.minimum(u0, 0.0) + jnp.minimum(u1, 0.0) - gx * gx - gy * gy
                top = jnp.maximum(jnp.maximum(s[:, 0:128], s[:, 128:256]), s[:, 256:384])
                here = low if e == 0 else ~low
                top = jnp.maximum(top, jnp.where(here, far, -3e38))
                tops.append(jnp.max(top, axis=1, keepdims=True))
                g0 = jnp.where(u0 >= 0.0, e0, 1.0) * ox_ref[rs, :] * (f1 * rr)
                g1 = jnp.where(u1 >= 0.0, e1, 1.0) * oy_ref[rs, :] * (f0 * rr)
                g0_ref[0, 2 * p + e, rs, :] = g0.astype(BF16)
                g1_ref[0, 2 * p + e, rs, :] = g1.astype(BF16)
                held.append((s, rr))
            pfar = jnp.exp2(far - jnp.where(low, tops[0], tops[1]))
            invs = []
            for e in range(2):
                s, rr = held[e]
                pe = jnp.exp2(s - tops[e]) * rr
                here = low if e == 0 else ~low
                tot = pe[:, 0:128] + pe[:, 128:256] + pe[:, 256:384] + jnp.where(here, pfar, 0.0)
                inv = 1.0 / jnp.sum(tot, axis=1, keepdims=True)
                invs.append(inv)
                pn_ref[0, 2 * p + e, rs, :] = (pe * inv).astype(BF16)
            pf_ref[0, p, rs, :] = (pfar * jnp.where(low, invs[0], invs[1])).astype(BF16)
        ctx = mm(pn_ref[0, 2 * p], vp * lo16) + mm(pn_ref[0, 2 * p + 1], vp * hi16)
        ctx = ctx + mm(pf_ref[0, p], jnp.concatenate([vgp * lo16, vgp * hi16], axis=0))
        ctx_ref[:, cols] = ctx.astype(BF16)
        return carry

    lax.fori_loop(0, pairs, one_pair, 0)


def attn_forward(q, k, v, before, after, every_glob, owner, w_qkv, norms, coords, units, lengths, offset, rich):
    rich_query, rich_key, rich_bias, rich_theta = rich
    rows, width = q.shape
    heads = rich_bias.shape[1]
    pairs = heads // 2
    tiles = rows // TILE
    blocks = rows // QBLOCK
    per_block = tiles // blocks
    padded_rows = rows + 2 * RADIUS
    globs = every_glob.shape[0]
    scalars = pl.BlockSpec(memory_space=pltpu.SMEM)

    def whole(*shape):
        return pl.BlockSpec(shape, lambda t: (0,) * len(shape))

    def block3(*shape):
        return pl.BlockSpec((1,) + shape, lambda t: (t // per_block, 0, 0))

    near = pl.BlockSpec((1, heads, TILE, SPAN), lambda t: (t, 0, 0, 0))
    near_shape = jax.ShapeDtypeStruct((tiles, heads, TILE, SPAN), BF16)
    tile_rows = pl.BlockSpec((TILE, width), lambda t: (t, 0))
    return pl.pallas_call(
        partial(fwd_kernel, pairs=pairs, per_block=per_block),
        grid=(tiles,),
        in_specs=[
            scalars, scalars, scalars, scalars, scalars,
            tile_rows, whole(rows, width), whole(rows, width),
            whole(RADIUS, width), whole(RADIUS, width),
            whole(globs, width), whole(1, globs),
            pl.BlockSpec((width, width), lambda t: (0, 1)),
            pl.BlockSpec((width, width), lambda t: (0, 2)),
            whole(*norms.shape),
            whole(*coords.shape), whole(4, width), whole(4, width),
        ],
        out_specs=[
            tile_rows, near,
            pl.BlockSpec((1, pairs, TILE, 128), lambda t: (t, 0, 0, 0)),
            near, near,
            whole(padded_rows, width), whole(padded_rows, width),
            block3(GLOB_FORM, width), block3(GLOB_FORM, width), block3(GLOB_FORM, width),
            block3(GLOB_FORM, width), block3(GLOB_FORM, globs),
        ],
        out_shape=[
            jax.ShapeDtypeStruct((rows, width), BF16),
            near_shape,
            jax.ShapeDtypeStruct((tiles, pairs, TILE, 128), BF16),
            near_shape, near_shape,
            jax.ShapeDtypeStruct((padded_rows, width), BF16),
            jax.ShapeDtypeStruct((padded_rows, width), BF16),
            jax.ShapeDtypeStruct((blocks, GLOB_FORM, width), BF16),
            jax.ShapeDtypeStruct((blocks, GLOB_FORM, width), BF16),
            jax.ShapeDtypeStruct((blocks, GLOB_FORM, width), BF16),
            jax.ShapeDtypeStruct((blocks, GLOB_FORM, width), F32),
            jax.ShapeDtypeStruct((blocks, GLOB_FORM, globs), BF16),
        ],
        scratch_shapes=[
            pltpu.VMEM((TILE, SPAN), F32), pltpu.VMEM((TILE, SPAN), F32),
            pltpu.VMEM((TILE, SPAN), F32), pltpu.VMEM((TILE, SPAN), F32),
            pltpu.VMEM((2 * TILE, SPAN), F32), pltpu.VMEM((TILE, 128), F32),
            pltpu.VMEM((TILE, 8), F32), pltpu.VMEM((8, SPAN), F32),
        ],
        compiler_params=pltpu.CompilerParams(vmem_limit_bytes=VMEM_LIMIT),
        cost_estimate=cost(65.0),
        name="attn_forward",
    )(units, lengths, offset, rich_bias, rich_theta, q, k, v, before, after, every_glob, owner,
      w_qkv, w_qkv, norms, coords, rich_query, rich_key)


def bwd_kernel(offset_ref, bias_ref, theta_ref,
               q_ref, dc_ref, ctx_ref, k_ref, v_ref, kg_ref, vg_ref, coords_ref, rq_ref, rk_ref,
               pn_ref, pf_ref, g0_ref, g1_ref,
               dq_ref, dk_ref, dv_ref, dkg_ref, dvg_ref, vec_ref,
               dx_ref, dy_ref, dp_ref, dpf_ref, ds_ref, dsf_ref, a_ref, b_ref, dqr_ref, db_ref,
               *, pairs, first_pair, tiles, per_block, edge):
    step = pl.program_id(0)
    t = step * (tiles - 1) if edge else step + 1

    @pl.when(step == 0)
    def _():
        vec_ref[...] = jnp.zeros_like(vec_ref)
        if not edge:
            dk_ref[...] = jnp.zeros_like(dk_ref)
            dv_ref[...] = jnp.zeros_like(dv_ref)
            db_ref[...] = jnp.zeros_like(db_ref)

    if edge:
        fresh = step >= 0
    else:
        fresh = (step == 0) | (t % per_block == 0)

    @pl.when(fresh)
    def _():
        dkg_ref[...] = jnp.zeros_like(dkg_ref)
        dvg_ref[...] = jnp.zeros_like(dvg_ref)

    geometry_into(coords_ref, offset_ref[0, 0] // 128 + t - 1, None, (None, None, dx_ref, dy_ref))
    lo16, hi16 = half_masks(BF16)
    lane = lax.broadcasted_iota(jnp.int32, (CH, 128), 1)
    low = lane < 64
    low64 = lax.broadcasted_iota(jnp.int32, (64, 128), 1) < 64
    lane8 = lax.broadcasted_iota(jnp.int32, (4, 128), 1)
    lane1 = lax.broadcasted_iota(jnp.int32, (1, 128), 1)
    sub = lax.broadcasted_iota(jnp.int32, (128, 1), 0)
    lo16c = (sub < 64).astype(F32).astype(BF16)
    hi16c = (sub >= 64).astype(F32).astype(BF16)
    rows = pl.ds(pl.multiple_of(t * TILE, TILE), SPAN)
    out_rows = pl.ds(pl.multiple_of((t - 1) * TILE, TILE), SPAN)

    def rich_key_parts(p, cols, sums, keys, columns):
        head = 2 * (p + first_pair)
        squares = [theta_ref[i, head + e] * theta_ref[i, head + e] for e in range(2) for i in range(2)]
        scales = by_row([1.0, 1.0, squares[0], squares[1], 1.0, 1.0, squares[2], squares[3]])
        scaled = sums * scales[:, 0:1]
        vectors = jnp.concatenate(split3(rich_rows(rk_ref[:, cols], None)), axis=0)
        parts = split3(scaled)
        left = jnp.concatenate([vectors[0:8]] * 3 + [vectors[8:16]] * 2 + [vectors[16:24]], axis=0)
        left = jnp.transpose(left).astype(BF16)
        right = jnp.concatenate([parts[0], parts[1], parts[2], parts[0], parts[1], parts[0]], axis=0).astype(BF16)
        extra = mm(left, right)
        stacked = jnp.concatenate(parts, axis=0).astype(BF16)
        key24 = mm(stacked, keys)
        key8 = key24[0:8] + key24[8:16] + key24[16:24]
        vec_ref[p, 4:8, :] += jnp.where(lane8 < 64, key8[0:4], key8[4:8])
        totals = jnp.sum(scaled, axis=1, keepdims=True)
        line = jnp.zeros((1, 128), F32)
        for index in range(8):
            line = jnp.where(lane1 == index, totals[index : index + 1, :], line)
        vec_ref[p, 8:9, :] += line
        return extra

    def one_pair(p, carry):
        cols = pl.ds(pl.multiple_of(p * 128, 128), 128)
        head = 2 * (p + first_pair)
        qp = q_ref[:, cols]
        dcp = dc_ref[:, cols]
        kp = k_ref[rows, cols]
        vp = v_ref[rows, cols]
        kgp = kg_ref[0, :, cols]
        vgp = vg_ref[0, :, cols]
        kg2 = jnp.concatenate([kgp * lo16, kgp * hi16], axis=0)
        vg2 = jnp.concatenate([vgp * lo16, vgp * hi16], axis=0)
        dp_ref[...] = mm_nt(jnp.concatenate([dcp * lo16, dcp * hi16], axis=0), vp)
        dpf_ref[...] = mm_nt(dcp, vg2)
        biases = by_row([bias_ref[c, head + e] for e in range(2) for c in range(4)])
        a, b = rich_sums(qp, kp, rq_ref[:, cols], rk_ref[:, cols], None, biases)
        a_ref[...] = a
        b_ref[...] = b
        squares = [[theta_ref[i, head + e] * theta_ref[i, head + e] for i in range(2)] for e in range(2)]
        halves = [jnp.where(lane1 < 64, squares[0][i], squares[1][i]) for i in range(2)]
        lines = [rq_ref[0:1, cols], rq_ref[1:2, cols], rq_ref[2:3, cols] * halves[0], rq_ref[3:4, cols] * halves[1]]
        col_sums = [[jnp.zeros((8, SPAN), F32) for _ in range(4)] for _ in range(2)]
        thetas = [[jnp.zeros((8, 128), F32) for _ in range(2)] for _ in range(2)]
        query_sums = [jnp.zeros((8, 128), F32) for _ in range(4)]
        for r in range(0, TILE, CH):
            rs = slice(r, r + CH)
            prod = dc_ref[rs, cols].astype(F32) * ctx_ref[rs, cols].astype(F32)
            row_sums = []
            dots = []
            for e in range(2):
                here = low if e == 0 else ~low
                base = 4 * e
                dot = jnp.sum(jnp.where(here, prod, 0.0), axis=1, keepdims=True)
                dots.append(dot)
                es = slice(e * TILE + r, e * TILE + r + CH)
                ds = pn_ref[0, 2 * p + e, rs, :].astype(F32) * (dp_ref[es, :] - dot)
                ds_ref[es, :] = ds.astype(BF16)
                t0 = ds * g0_ref[0, 2 * p + e, rs, :].astype(F32)
                t1 = ds * g1_ref[0, 2 * p + e, rs, :].astype(F32)
                gx = (dx_ref[rs, :] - a_ref[rs, base + 2 : base + 3]) - b_ref[base + 2 : base + 3, :]
                gy = (dy_ref[rs, :] - a_ref[rs, base + 3 : base + 4]) - b_ref[base + 3 : base + 4, :]
                tx = ds * gx
                ty = ds * gy
                for i, full in enumerate((tx * gx, ty * gy)):
                    part = full[:, 0:128] + full[:, 128:256] + full[:, 256:384]
                    thetas[e][i] = thetas[e][i] + (part[0:8] + part[8:16])
                sums = []
                for c, full in enumerate((t0, t1, tx, ty)):
                    col_sums[e][c] = col_sums[e][c] + (full[0:8] + full[8:16])
                    sums.append(jnp.sum(full[:, 0:128] + full[:, 128:256] + full[:, 256:384], axis=1, keepdims=True))
                row_sums.append(sums)
            dsf = pf_ref[0, p, rs, :].astype(F32) * (dpf_ref[rs, :] - jnp.where(low, dots[0], dots[1]))
            dsf_ref[rs, :] = dsf.astype(BF16)
            qf = q_ref[rs, cols].astype(F32)
            dqr = jnp.zeros((CH, 128), F32)
            for c in range(4):
                da = jnp.where(low, row_sums[0][c], row_sums[1][c])
                dqr = dqr + da * lines[c]
                part = da * qf
                query_sums[c] = query_sums[c] + (part[0:8] + part[8:16])
            dqr_ref[rs, :] = dqr
        folded = jnp.concatenate([jnp.sum(query_sums[c], axis=0, keepdims=True) for c in range(4)], axis=0)
        scale4 = jnp.concatenate([jnp.ones((2, 128), F32), halves[0], halves[1]], axis=0)
        vec_ref[p, 0:4, :] += folded * scale4
        line = jnp.zeros((1, 128), F32)
        for e in range(2):
            for i in range(2):
                total = jnp.sum(jnp.sum(thetas[e][i], axis=0, keepdims=True), axis=1, keepdims=True)
                line = jnp.where(lane1 == 8 + 2 * e + i, total * (-theta_ref[i, head + e]), line)
        vec_ref[p, 8:9, :] += line
        packed = jnp.concatenate([jnp.sum(col_sums[e][c], axis=0, keepdims=True) for e in range(2) for c in range(4)], axis=0)
        dq = mm(ds_ref[0:TILE, :], kp * lo16) + mm(ds_ref[TILE : 2 * TILE, :], kp * hi16) + mm(dsf_ref[...], kg2)
        dq_ref[:, cols] = (dq * 0.125 + dqr_ref[...]).astype(BF16)
        qT = jnp.transpose(qp)
        dcT = jnp.transpose(dcp)
        dk = mm(jnp.concatenate([qT * lo16c, qT * hi16c], axis=1), ds_ref[...]) * 0.125
        dv = mm(dcT * lo16c, pn_ref[0, 2 * p]) + mm(dcT * hi16c, pn_ref[0, 2 * p + 1])
        if edge:
            dk_ref[0, cols, :] = dk + rich_key_parts(p, cols, packed, kp, rows)
            dv_ref[0, cols, :] = dv
        else:
            dk_ref[cols, out_rows] += dk
            dv_ref[cols, out_rows] += dv
            db_ref[p, :, out_rows] += packed
        dkg2 = mm(jnp.transpose(dsf_ref[...]), qp) * 0.125
        dvg2 = mm(jnp.transpose(pf_ref[0, p]), dcp)
        dkg_ref[0, :, cols] += jnp.where(low64, dkg2[0:64], dkg2[64:128])
        dvg_ref[0, :, cols] += jnp.where(low64, dvg2[0:64], dvg2[64:128])
        return carry

    lax.fori_loop(0, pairs, one_pair, 0)

    if not edge:

        @pl.when(step == pl.num_programs(0) - 1)
        def _():
            own = k_ref.shape[0] - 2 * RADIUS

            def finish(p, carry):
                cols = pl.ds(pl.multiple_of(p * 128, 128), 128)
                keys = k_ref[RADIUS : RADIUS + own, cols]
                dk_ref[cols, :] += rich_key_parts(p, cols, db_ref[p], keys, None)
                return carry

            lax.fori_loop(0, pairs, finish, 0)


def attn_backward(q, dctx, ctx, k_pad, v_pad, kg, vg, coords, offset, rich, kept, first_pair, pairs, edge):
    rich_query, rich_key, rich_bias, rich_theta = rich
    rows, width = q.shape
    tiles = rows // TILE
    blocks = kg.shape[0]
    per_block = tiles // blocks
    part = pairs * 128
    half = first_pair // pairs
    steps = 2 if edge else tiles - 2
    padded_rows = k_pad.shape[0]
    scalars = pl.BlockSpec(memory_space=pltpu.SMEM)

    def tile(i):
        return i * (tiles - 1) if edge else i + 1

    tile_rows = pl.BlockSpec((TILE, part), lambda i: (tile(i), half))
    padded_cols = pl.BlockSpec((padded_rows, part), lambda i: (0, half))
    block3 = pl.BlockSpec((1, GLOB_FORM, part), lambda i: (tile(i) // per_block, 0, half))
    out3 = pl.BlockSpec((1, GLOB_FORM, part), lambda i: (tile(i) // per_block, 0, 0))
    vectors = pl.BlockSpec((4, part), lambda i: (0, half))
    near = pl.BlockSpec((1, 2 * pairs, TILE, SPAN), lambda i: (tile(i), half, 0, 0))
    far = pl.BlockSpec((1, pairs, TILE, 128), lambda i: (tile(i), half, 0, 0))
    if edge:
        key_out = pl.BlockSpec((1, part, SPAN), lambda i: (i, 0, 0))
        key_shape = jax.ShapeDtypeStruct((2, part, SPAN), F32)
    else:
        key_out = pl.BlockSpec((part, rows), lambda i: (0, 0))
        key_shape = jax.ShapeDtypeStruct((part, rows), F32)
    glob_shape = jax.ShapeDtypeStruct((blocks, GLOB_FORM, part), F32)
    return pl.pallas_call(
        partial(bwd_kernel, pairs=pairs, first_pair=first_pair, tiles=tiles, per_block=per_block, edge=edge),
        grid=(steps,),
        in_specs=[
            scalars, scalars, scalars,
            tile_rows, tile_rows, tile_rows, padded_cols, padded_cols, block3, block3,
            pl.BlockSpec(coords.shape, lambda i: (0, 0)), vectors, vectors,
            near, far, near, near,
        ],
        out_specs=[
            pl.BlockSpec((TILE, part), lambda i: (i, 0)),
            key_out, key_out, out3, out3,
            pl.BlockSpec((pairs, 16, 128), lambda i: (0, 0, 0)),
        ],
        out_shape=[
            jax.ShapeDtypeStruct((steps * TILE, part), BF16),
            key_shape, key_shape, glob_shape, glob_shape,
            jax.ShapeDtypeStruct((pairs, 16, 128), F32),
        ],
        scratch_shapes=[
            pltpu.VMEM((TILE, SPAN), F32), pltpu.VMEM((TILE, SPAN), F32),
            pltpu.VMEM((2 * TILE, SPAN), F32), pltpu.VMEM((TILE, 128), F32),
            pltpu.VMEM((2 * TILE, SPAN), BF16), pltpu.VMEM((TILE, 128), BF16),
            pltpu.VMEM((TILE, 8), F32), pltpu.VMEM((8, SPAN), F32),
            pltpu.VMEM((TILE, 128), F32), pltpu.VMEM((pairs, 8, rows), F32),
        ],
        compiler_params=pltpu.CompilerParams(vmem_limit_bytes=VMEM_LIMIT),
        cost_estimate=cost(8.2 * steps * pairs / 6),
        name="attn_backward_edge" if edge else "attn_backward_mid",
    )(offset, rich_bias, rich_theta, q, dctx, ctx, k_pad, v_pad, kg, vg, coords, rich_query, rich_key, *kept)


FF_CHUNK = 384
ROW_CHUNK = 256

def normal_tail(values):
    z = jnp.abs(values) * math.sqrt(0.5)
    t = 1.0 / (1.0 + 0.5 * z)
    poly = jnp.full_like(t, 0.17087277)
    for coef in (-0.82215223, 1.48851587, -1.13520398, 0.27886807, -0.18628806, 0.09678418, 0.37409196, 1.00002368, -1.26551223):
        poly = poly * t + coef
    return 0.5 * t * jnp.exp(poly - z * z)

def gelu_pair(values):
    tail = normal_tail(values)
    phi = jnp.where(values >= 0.0, 1.0 - tail, tail)
    density = jnp.exp(-0.5 * values * values) * (1.0 / math.sqrt(2.0 * math.pi))
    return values * phi, phi + values * density

def ffn_kernel(tok_ref, ctx_ref, ct_ref, wo_ref, wu_ref, wd_ref, norms_ref,
               out_ref, dmid_ref, dctx_ref, wog_ref, wug_ref, wdg_ref, vec_ref,
               mid_ref, h2_ref, h2t_ref, acc_ref, dh_ref, act_ref, dpre_ref, *, rows):
    step = pl.program_id(0)
    last = pl.num_programs(0) - 1

    @pl.when(step == 0)
    def _():
        for r in range(0, rows, ROW_CHUNK):
            rs = slice(r, r + ROW_CHUNK)
            mid = tok_ref[rs, :].astype(F32) + mm(ctx_ref[rs, :], wo_ref[...])
            mid_ref[rs, :] = mid
            normed, _ = norm_parts(mid)
            h2 = (normed * norms_ref[2:3, :] + norms_ref[3:4, :]).astype(BF16)
            h2_ref[rs, :] = h2
            h2t_ref[:, rs] = jnp.transpose(h2)
            acc_ref[rs, :] = jnp.zeros_like(mid)
            dh_ref[rs, :] = jnp.zeros_like(mid)

    for r in range(0, rows, ROW_CHUNK):
        rs = slice(r, r + ROW_CHUNK)
        pre = mm(h2_ref[rs, :], wu_ref[...])
        dact = mm_nt(ct_ref[rs, :], wd_ref[...])
        act, slope = gelu_pair(pre)
        act_ref[rs, :] = act.astype(BF16)
        dpre_ref[rs, :] = (dact * slope).astype(BF16)
        acc_ref[rs, :] += mm(act_ref[rs, :], wd_ref[...])
        dh_ref[rs, :] += mm_nt(dpre_ref[rs, :], wu_ref[...])
    wug_ref[...] = mm(h2t_ref[...], dpre_ref[...]).astype(BF16)
    wdg_ref[...] = mm_tn(act_ref[...], ct_ref[...]).astype(BF16)

    @pl.when(step == last)
    def _():
        gains = jnp.zeros((8, norms_ref.shape[1]), F32)
        shifts = jnp.zeros((8, norms_ref.shape[1]), F32)
        for r in range(0, rows, ROW_CHUNK):
            rs = slice(r, r + ROW_CHUNK)
            mid = mid_ref[rs, :]
            out_ref[rs, :] = (mid + acc_ref[rs, :]).astype(BF16)
            normed, scale = norm_parts(mid)
            dh = dh_ref[rs, :]
            gains = gains + jnp.sum((dh * normed).reshape(ROW_CHUNK // 8, 8, -1), axis=0)
            shifts = shifts + jnp.sum(dh.reshape(ROW_CHUNK // 8, 8, -1), axis=0)
            dmid = ct_ref[rs, :].astype(F32) + norm_pull(dh, normed, scale, norms_ref[2:3, :])
            dmid_ref[rs, :] = dmid
            dattn = dmid.astype(BF16)
            h2_ref[rs, :] = dattn
            dctx_ref[rs, :] = mm_nt(dattn, wo_ref[...]).astype(BF16)
        wog_ref[...] = mm_tn(ctx_ref[...], h2_ref[...]).astype(BF16)
        vec_ref[0:1, :] = jnp.sum(gains, axis=0, keepdims=True)
        vec_ref[1:2, :] = jnp.sum(shifts, axis=0, keepdims=True)

def feed_forward(tokens, context, cotangent, w_out, w_up, w_down, norms):
    rows, width = tokens.shape
    hidden = w_up.shape[1]
    steps = hidden // FF_CHUNK
    whole = lambda *shape: pl.BlockSpec(shape, lambda s: (0,) * len(shape))
    return pl.pallas_call(
        partial(ffn_kernel, rows=rows),
        grid=(steps,),
        in_specs=[
            whole(rows, width), whole(rows, width), whole(rows, width), whole(width, width),
            pl.BlockSpec((width, FF_CHUNK), lambda s: (0, s)),
            pl.BlockSpec((FF_CHUNK, width), lambda s: (s, 0)),
            whole(*norms.shape),
        ],
        out_specs=[
            whole(rows, width), whole(rows, width), whole(rows, width), whole(width, width),
            pl.BlockSpec((width, FF_CHUNK), lambda s: (0, s)),
            pl.BlockSpec((FF_CHUNK, width), lambda s: (s, 0)),
            whole(8, width),
        ],
        out_shape=[
            jax.ShapeDtypeStruct((rows, width), BF16),
            jax.ShapeDtypeStruct((rows, width), F32),
            jax.ShapeDtypeStruct((rows, width), BF16),
            jax.ShapeDtypeStruct((width, width), BF16),
            jax.ShapeDtypeStruct((width, hidden), BF16),
            jax.ShapeDtypeStruct((hidden, width), BF16),
            jax.ShapeDtypeStruct((8, width), F32),
        ],
        scratch_shapes=[
            pltpu.VMEM((rows, width), F32), pltpu.VMEM((rows, width), BF16), pltpu.VMEM((width, rows), BF16),
            pltpu.VMEM((rows, width), F32), pltpu.VMEM((rows, width), F32),
            pltpu.VMEM((rows, FF_CHUNK), BF16), pltpu.VMEM((rows, FF_CHUNK), BF16),
        ],
        compiler_params=pltpu.CompilerParams(vmem_limit_bytes=VMEM_LIMIT),
        cost_estimate=cost(60.0),
        name="feed_forward",
    )(tokens, context, cotangent, w_out, w_up, w_down, norms)


def qkv_back_kernel(*refs, half, final, pairs, kept):
    (ht_ref, hg_ref, w_ref, dqe_ref, dqm_ref, dke_ref, dve_ref, dkm_ref, dvm_ref, before_ref, after_ref,
     dkge_ref, dvge_ref, dkgm_ref, dvgm_ref) = refs[:15]
    refs = refs[15:]
    if final:
        (dh0_ref, dhg0_ref, tok_ref, dmid_ref, norms_ref, oh_ref, ng_ref, second_ref, ve_ref, va_ref, vb_ref) = refs[:11]
        refs = refs[11:]
        grad_ref, vec_ref, tg_ref, gp_ref, dh_ref, dhg_ref, part_ref, dkt_ref, rows_ref = refs
    else:
        grad_ref, dh_ref, dhg_ref, part_ref, dkt_ref = refs
    step = pl.program_id(0)
    rows, part = part_ref.shape
    width = ht_ref.shape[0]
    edge = 128

    @pl.when(step == 0)
    def _():
        part_ref[0:edge, :] = dqe_ref[0:edge, :]
        part_ref[edge : rows - edge, :] = dqm_ref[...]
        part_ref[rows - edge : rows, :] = dqe_ref[edge : 2 * edge, :]

    for index, edge_ref, mid_ref in ((1, dke_ref, dkm_ref), (2, dve_ref, dvm_ref)):

        @pl.when(step == index)
        def _():
            dkt_ref[...] = mid_ref[...].astype(BF16)
            dkt_ref[:, 0:128] = (mid_ref[:, 0:128] + edge_ref[0, :, 128:256] + before_ref[index - 1].astype(F32)).astype(BF16)
            dkt_ref[:, 128:256] = (mid_ref[:, 128:256] + edge_ref[0, :, 256:384]).astype(BF16)
            dkt_ref[:, rows - 256 : rows - 128] = (mid_ref[:, rows - 256 : rows - 128] + edge_ref[1, :, 0:128]).astype(BF16)
            dkt_ref[:, rows - 128 : rows] = (
                mid_ref[:, rows - 128 : rows] + edge_ref[1, :, 128:256] + after_ref[index - 1].astype(F32)
            ).astype(BF16)
            part_ref[...] = jnp.transpose(dkt_ref[...])

    grad = mm(ht_ref[...], part_ref[...])
    moved = mm_nt(part_ref[...], w_ref[...])

    @pl.when(step == 0)
    def _():
        grad_ref[...] = grad.astype(BF16)
        if final:
            dh_ref[...] = dh0_ref[...] + moved
            dhg_ref[...] = dhg0_ref[...]
        else:
            dh_ref[...] = moved
            dhg_ref[...] = jnp.zeros_like(dhg_ref)

    for index, edge_ref, mid_ref in ((1, dkge_ref, dkgm_ref), (2, dvge_ref, dvgm_ref)):

        @pl.when(step == index)
        def _():
            glob = (edge_ref[...] + mid_ref[...]).reshape(-1, part).astype(BF16)
            hg = hg_ref[...].reshape(-1, width)
            grad_ref[...] = (grad + mm_tn(hg, glob)).astype(BF16)
            dh_ref[...] += moved
            dhg_ref[...] += mm_nt(glob, w_ref[...])

    if final:

        @pl.when(step == 2)
        def _():
            gains = jnp.zeros((8, width), F32)
            shifts = jnp.zeros((8, width), F32)
            for r in range(0, rows, 128):
                rs = slice(r, r + 128)
                normed, scale = norm_parts(tok_ref[rs, :].astype(F32))
                dh = dh_ref[rs, :]
                gains = gains + jnp.sum((dh * normed).reshape(16, 8, width), axis=0)
                shifts = shifts + jnp.sum(dh.reshape(16, 8, width), axis=0)
                tg_ref[rs, :] = (dmid_ref[rs, :] + norm_pull(dh, normed, scale, norms_ref[0:1, :])).astype(BF16)
            dhg = dhg_ref[...]
            normed = ng_ref[...].reshape(-1, width)
            rows_ref[...] = jnp.zeros_like(rows_ref)
            rows_ref[0:1, :] = jnp.sum(gains, axis=0, keepdims=True) + jnp.sum(dhg * normed, axis=0, keepdims=True)
            rows_ref[1:2, :] = jnp.sum(shifts, axis=0, keepdims=True) + jnp.sum(dhg, axis=0, keepdims=True)
            rows_ref[2:4, :] = second_ref[0:2, :]
            gp_ref[...] = mm_tn(oh_ref[...].reshape(-1, oh_ref.shape[2]), dhg.astype(BF16)).astype(BF16)
            lines = []
            for p in range(2 * pairs):
                mid = va_ref[p] if p < pairs else vb_ref[p - pairs]
                both = ve_ref[p] + mid
                rows_ref[4:12, p * 128 : p * 128 + 128] = both[0:8]
                lines.append(both[8:9])
            lines.append(jnp.zeros((8 - len(lines), 128), F32))
            lines = jnp.concatenate(split3(jnp.concatenate(lines, axis=0)), axis=0).astype(BF16)
            spot = lax.broadcasted_iota(jnp.int32, (128, width), 0)
            lane = lax.broadcasted_iota(jnp.int32, (128, width), 1)
            spread = mm(lines, (lax.rem(lane, kept) == spot).astype(F32).astype(BF16))
            rows_ref[12:20, :] = spread[0:8] + spread[8:16] + spread[16:24]
            vec_ref[...] = jnp.transpose(rows_ref[...]).astype(BF16)


def qkv_backward(hidden_t, hg, w_qkv, dq, dk, dv, rims, dkg, dvg, half, pairs, kept, last=None):
    width, rows = hidden_t.shape
    part = pairs * 128
    halves = width // part
    final = last is not None

    def whole(*shape):
        return pl.BlockSpec(shape, lambda i: (0,) * len(shape))

    blocks = hg.shape[0]
    edge_keys = pl.BlockSpec((2, part, SPAN), lambda i: (0, half, 0))
    edge_glob = pl.BlockSpec((blocks, GLOB_FORM, part), lambda i: (0, 0, half))
    rim = pl.BlockSpec((2, part, RADIUS), lambda i: (0, half, 0))
    operands = [hidden_t, hg, w_qkv, dq[0], dq[1], dk[0], dv[0], dk[1], dv[1], rims[0], rims[1],
                dkg[0], dvg[0], dkg[1], dvg[1]]
    in_specs = [
        whole(width, rows), whole(blocks, GLOB_FORM, width),
        pl.BlockSpec((width, part), lambda i: (0, halves * i + half)),
        pl.BlockSpec((2 * TILE, part), lambda i: (0, half)), whole(rows - 2 * TILE, part),
        edge_keys, edge_keys, whole(part, rows), whole(part, rows), rim, rim,
        edge_glob, edge_glob, whole(blocks, GLOB_FORM, part), whole(blocks, GLOB_FORM, part),
    ]
    out_specs = [pl.BlockSpec((width, part), lambda i: (0, i))]
    out_shape = [jax.ShapeDtypeStruct((width, 3 * part), BF16)]
    scratch = [pltpu.VMEM((rows, part), BF16), pltpu.VMEM((part, rows), BF16)]
    sums_shape = [(rows, width), (blocks * GLOB_FORM, width)]
    if final:
        operands += list(last)
        in_specs += [whole(*a.shape) for a in last]
        globs = last[5].shape[2]
        out_specs += [whole(width, 128), whole(rows, width), whole(globs, width)]
        out_shape += [
            jax.ShapeDtypeStruct((width, 128), BF16),
            jax.ShapeDtypeStruct((rows, width), BF16),
            jax.ShapeDtypeStruct((globs, width), BF16),
        ]
        scratch = [pltpu.VMEM(s, F32) for s in sums_shape] + scratch + [pltpu.VMEM((128, width), F32)]
    else:
        out_specs += [whole(*s) for s in sums_shape]
        out_shape += [jax.ShapeDtypeStruct(s, F32) for s in sums_shape]
    return pl.pallas_call(
        partial(qkv_back_kernel, half=half, final=final, pairs=pairs, kept=kept),
        grid=(3,),
        in_specs=in_specs,
        out_specs=out_specs,
        out_shape=out_shape,
        scratch_shapes=scratch,
        compiler_params=pltpu.CompilerParams(vmem_limit_bytes=VMEM_LIMIT),
        cost_estimate=cost(15.0 if final else 8.0),
        name="qkv_backward",
    )(*operands)


def swap_on(axis, mask):
    return [(i, i ^ mask) for i in range(lax.axis_size(axis))]


def add_low(kept, received):
    return (kept.astype(F32) + received.astype(F32)).astype(BF16)


def core_halves(grads, place):
    count = lax.axis_size("seq")
    view = grads.reshape(count // 2, 2, grads.shape[0] // count, grads.shape[1])
    send = lax.dynamic_index_in_dim(view, 1 - place % 2, 1, keepdims=False)
    kept = lax.dynamic_index_in_dim(view, place % 2, 1, keepdims=False)
    return kept, send


def core_swap(send):
    return lax.ppermute(send, "seq", swap_on("seq", 1))


def stream_blocks(summed, group_count):
    outer, rows, columns = summed.shape
    return jnp.moveaxis(summed.reshape(outer, group_count, rows // group_count, columns), 1, 0)


def halve_step(blocks, axis, place, bit, width):
    mine = (place >> bit) & 1
    send = lax.dynamic_index_in_dim(blocks, 1 - mine, width, keepdims=False)
    kept = lax.dynamic_index_in_dim(blocks, mine, width, keepdims=False)
    return add_low(kept, lax.ppermute(send, axis, swap_on(axis, 1 << bit)))


def exchange_sum(blocks, axis, place, stride):
    count = blocks.shape[0]
    total = lax.dynamic_index_in_dim(blocks, place, 0, keepdims=False).astype(F32)
    for step in range(1, count):
        send = lax.dynamic_index_in_dim(blocks, place ^ step, 0, keepdims=False)
        total = total + lax.ppermute(send, axis, swap_on(axis, step * stride)).astype(F32)
    return total.astype(BF16)


def exchange_all(piece, axis, place):
    count = lax.axis_size(axis)
    every = [piece] + [lax.ppermute(piece, axis, swap_on(axis, step)) for step in range(1, count)]
    return ordered(jnp.stack(every), place)


def gather_rows(rows, axis, place, bit):
    other = lax.ppermute(rows, axis, swap_on(axis, bit))
    upper = (place & bit) > 0
    return jnp.concatenate([jnp.where(upper, other, rows), jnp.where(upper, rows, other)], axis=0)


def gather_blocks(rows, axis, place, stride):
    count = lax.axis_size(axis) // stride
    every = [rows] + [lax.ppermute(rows, axis, swap_on(axis, step * stride)) for step in range(1, count)]
    return ordered(jnp.stack(every), place).reshape(count * rows.shape[0], rows.shape[1])


def ordered(stacked, place):
    count = stacked.shape[0]
    rest = stacked.shape[1:]
    bit = 1
    while bit < count:
        view = stacked.reshape((count // (2 * bit), 2, bit) + rest)
        stacked = jnp.where((place & bit) > 0, view[:, ::-1], view).reshape((count,) + rest)
        bit *= 2
    return stacked


def tied(*values):
    return lax.optimization_barrier(values)


def body(
    tokens,
    global_states,
    cotangent,
    w_qkv,
    w_out,
    w_up,
    w_down,
    first_gain,
    first_shift,
    second_gain,
    second_shift,
    rich_query,
    rich_key,
    rich_bias,
    rich_theta,
    bucket_units,
    form_lengths,
    coords,
    glob_owner,
):
    row_count = tokens.shape[1]
    model_width = tokens.shape[2]
    place = lax.axis_index("seq")
    group = lax.axis_index("stream")
    seq_count = lax.axis_size("seq")
    group_count = lax.axis_size("stream")
    rich = (rich_query, rich_key, rich_bias, rich_theta)
    offset = (place * row_count).astype(jnp.int32).reshape(1, 1)
    norms = jnp.stack([first_gain, first_shift, second_gain, second_shift])
    up = [(i, i + 1) for i in range(seq_count - 1)]
    down = [(i + 1, i) for i in range(seq_count - 1)]
    pairs = rich_bias.shape[1] // 2
    half_pairs = pairs // 2
    kept_rows = model_width // seq_count

    before = lax.ppermute(tokens[0, row_count - RADIUS :], "seq", up)
    after = lax.ppermute(tokens[0, :RADIUS], "seq", down)
    pair_glob = gather_rows(global_states[0], "seq", place, 1)
    pair_glob, norms, before, after = tied(pair_glob, norms, before, after)
    every_glob = gather_blocks(pair_glob, "seq", place // 2, 2)
    queries, keys, values, hidden_t = project_tokens(tokens[0], w_qkv, norms)
    (context, pn, pf, g0, g1, key_pad, value_pad, glob_keys, glob_values, glob_hidden, glob_normed, picked) = attn_forward(
        queries, keys, values, before, after, every_glob, glob_owner, w_qkv, norms,
        coords[0], bucket_units, form_lengths, offset, rich,
    )
    layer_out, grad_middle, grad_context, grad_w_out, grad_w_up, grad_w_down, second_sums = feed_forward(
        tokens[0], context, cotangent[0], w_out, w_up, w_down, norms
    )

    def attention_back(first_pair, count, edge, grad_context):
        return attn_backward(
            queries, grad_context, context, key_pad, value_pad, glob_keys, glob_values, coords[0], offset, rich,
            (pn, pf, g0, g1), first_pair, count, edge,
        )

    halves = [core_halves(grad, place) for grad in (grad_w_up, grad_w_down, grad_w_out)]
    sends = [half[1] for half in halves]
    grad_context, *sends = tied(grad_context, *sends)
    halves = [(half[0], core_swap(send)) for half, send in zip(halves, sends)]
    dq_e, dk_e, dv_e, dkg_e, dvg_e, vec_e = attention_back(0, pairs, True, grad_context)
    to_before = jnp.stack([dk_e[0, :, :RADIUS], dv_e[0, :, :RADIUS]]).astype(BF16)
    to_after = jnp.stack([dk_e[1, :, 2 * RADIUS :], dv_e[1, :, 2 * RADIUS :]]).astype(BF16)
    rims = (lax.ppermute(to_after, "seq", up), lax.ppermute(to_before, "seq", down))

    (dq_e, *swapped) = tied(dq_e, *[half[1] for half in halves])
    halves = [(half[0], received) for half, received in zip(halves, swapped)]

    sums = [add_low(*half) for half in halves]
    outer = seq_count // 2
    bits = group_count.bit_length() - 1
    pieces = [
        jnp.moveaxis(sums[0].reshape(outer, kept_rows, group_count, -1), 2, 0).reshape(group_count, outer, -1, model_width),
        jnp.moveaxis(sums[1].reshape(outer, group_count, -1, model_width), 1, 0),
        jnp.moveaxis(sums[2].reshape(outer, group_count, -1, model_width), 1, 0),
    ]
    piece_rows = [piece.shape[2] for piece in pieces]
    early = jnp.concatenate(pieces, axis=2).reshape((2,) * bits + (outer, sum(piece_rows), model_width))
    columns = model_width // 2
    early_x, early_y = early[..., :columns], early[..., columns:]
    order_x = list(range(bits))
    order_y = order_x[1:] + order_x[:1]

    def halved(blocks, order, done):
        bit = order[done]
        rest = sorted(order[done:], reverse=True)
        return halve_step(blocks, "stream", group, bit, rest.index(bit))

    early_x, early_y, grad_context, *rims = tied(early_x, early_y, grad_context, *rims)
    early_x = halved(early_x, order_x, 0)
    early_y = halved(early_y, order_y, 0)
    dq_a, dk_a, dv_a, dkg_a, dvg_a, vec_a = attention_back(0, half_pairs, False, grad_context)
    early_x, early_y, dq_a = tied(early_x, early_y, dq_a)
    for done in range(1, bits):
        early_x = halved(early_x, order_x, done)
        early_y = halved(early_y, order_y, done)
    grads_a, grad_hidden, grad_glob_hidden = qkv_backward(
        hidden_t, glob_hidden, w_qkv, (dq_e, dq_a), (dk_e, dk_a), (dv_e, dv_a), rims,
        (dkg_e, dkg_a), (dvg_e, dvg_a), 0, half_pairs, kept_rows,
    )
    kept_a, send_a = core_halves(grads_a, place)
    early = jnp.concatenate([early_x, early_y], axis=-1)
    late_a = stream_blocks(add_low(kept_a, core_swap(send_a)), group_count)
    early, late_a, grad_context = tied(early, late_a, grad_context)
    dq_b, dk_b, dv_b, dkg_b, dvg_b, vec_b = attention_back(half_pairs, half_pairs, False, grad_context)
    early = exchange_sum(early, "seq", place // 2, 2)
    early, dq_b = tied(early, dq_b)
    early = exchange_all(early, "stream", group)
    late_a, dq_b = tied(late_a, dq_b)
    late_a = exchange_sum(late_a, "stream", group, 1)
    late_a = exchange_sum(late_a, "seq", place // 2, 2)
    grads_b, vectors, tokens_grad, glob_part = qkv_backward(
        hidden_t, glob_hidden, w_qkv, (dq_e, dq_b), (dk_e, dk_b), (dv_e, dv_b), rims,
        (dkg_e, dkg_b), (dvg_e, dvg_b), 1, half_pairs, kept_rows,
        (grad_hidden, grad_glob_hidden, tokens[0], grad_middle, norms, picked, glob_normed, second_sums, vec_e, vec_a, vec_b),
    )

    early, late_a, grads_b = tied(early, late_a, grads_b)
    share_a = exchange_all(late_a, "stream", group).reshape(kept_rows, -1).astype(F32)
    kept_b, send_b = core_halves(jnp.concatenate([grads_b, vectors], axis=1), place)
    late_b = stream_blocks(add_low(kept_b, core_swap(send_b)), group_count)
    late_b = exchange_sum(late_b, "stream", group, 1)
    late_b = exchange_sum(late_b, "seq", place // 2, 2)
    share_b = exchange_all(late_b, "stream", group).reshape(kept_rows, -1).astype(F32)
    kept_glob, send_glob = core_halves(glob_part, place)
    glob_blocks = add_low(kept_glob, core_swap(send_glob))
    grad_glob = exchange_sum(glob_blocks, "seq", place // 2, 2).astype(F32)
    own_glob, own_scale = norm_parts(global_states[0].astype(F32))
    glob_grad = norm_pull(grad_glob, own_glob, own_scale, first_gain).astype(BF16)

    part = half_pairs * 128
    share_qkv = jnp.concatenate(
        [share[:, i * part : (i + 1) * part] for i in range(3) for share in (share_a, share_b)], axis=1
    )
    cuts = [0, piece_rows[0], piece_rows[0] + piece_rows[1], sum(piece_rows)]
    early = early.astype(F32)
    share_up = jnp.moveaxis(early[:, : cuts[1]].reshape(group_count, kept_rows, -1), 0, 1).reshape(kept_rows, -1)
    share_down = early[:, cuts[1] : cuts[2]].reshape(-1, model_width)
    share_out = early[:, cuts[2] :].reshape(-1, model_width)
    small = share_b[:, 3 * part :]
    own_vectors = small[:, :12].T
    heads = small[:12, 12 : 12 + pairs].T.reshape(pairs, 12)
    bias_grad = heads[:, :8].reshape(pairs, 2, 4).transpose(2, 0, 1).reshape(rich_bias.shape)
    theta_grad = heads[:, 8:].reshape(pairs, 2, 2).transpose(2, 0, 1).reshape(rich_theta.shape)
    return (
        layer_out[None],
        tokens_grad[None],
        glob_grad[None],
        share_qkv,
        share_out,
        share_up,
        share_down,
        own_vectors[0],
        own_vectors[1],
        own_vectors[2],
        own_vectors[3],
        own_vectors[4:8],
        own_vectors[8:12],
        bias_grad,
        theta_grad,
    )


def solution(mesh):
    return jax.shard_map(
        body,
        mesh=mesh,
        in_specs=(
            P("stream", "seq", None),
            P("stream", "seq", None),
            P("stream", "seq", None),
            P(),
            P(),
            P(),
            P(),
            P(),
            P(),
            P(),
            P(),
            P(),
            P(),
            P(),
            P(),
            P("stream", None),
            P("stream", None),
            P("stream", None, None),
            P("stream", None),
        ),
        out_specs=(
            P("stream", "seq", None),
            P("stream", "seq", None),
            P("stream", "seq", None),
            P("seq", None),
            P("seq", None),
            P("seq", None),
            P("seq", None),
            P("seq"),
            P("seq"),
            P("seq"),
            P("seq"),
            P(None, "seq"),
            P(None, "seq"),
            P(),
            P(),
        ),
        check_vma=False,
    )
```

time: 679 us -> 407 us (0.60)
  waiting for transfers between devices: 179 us -> 38.2 us
  matrix products: 135 us -> 0 us
  Pallas kernels: 135 us -> 261 us
  blocking collectives: 84.7 us -> 0 us
  starting transfers between devices: 8.19 us -> 56.5 us
  local copies, waits for them, and re-layouts: 63 us -> 24.9 us
  other arithmetic: 48.5 us -> 19.7 us
  between operations: 16.4 us -> 1.66 us
    reduce_scatter x5 -> x0, waiting for transfers between devices: 143 us -> none  [the longest x1 55.8 us: body(): lax.psum_scatter(grad_w_up.astype(jnp.bfloat16), 'seq', scatter_dimension...]
    dot_general x19 -> x0, matrix products: 135 us -> none  [the longest x1 35.6 us: body(): pre_act = jnp.dot(hidden_two, w_up, preferred_element_type=jnp.float32)]
    pallas_call x2 -> x8, Pallas kernels: 135 us -> 261 us  [the longest x3 82.6 us: attn_backward(): pl.pallas_call(partial(bwd_kernel, pairs=pairs, first_pair=first_pair, ti...]
    psum x2 -> x0, blocking collectives: 52.6 us -> none  [the longest x1 42.5 us: body(): small_sums = lax.psum((grad_shift, grad_width), ('stream', 'seq'))]
    ppermute x4 -> x45, starting transfers between devices: 7.22 us -> 56.5 us  [the longest x18 25.9 us: exchange_sum(): lax.ppermute(send, axis, swap_on(axis, step * stride)).astype(F32)]
    ppermute x4 -> x45, waiting for transfers between devices: 0.01 us -> 38.2 us  [the longest x18 31.1 us: exchange_sum(): lax.ppermute(send, axis, swap_on(axis, step * stride)).astype(F32)]
    psum x1 -> x0, waiting for transfers between devices: 35.4 us -> none  [body(): lax.psum(every_share[4].astype(jnp.bfloat16), 'stream').astype(jnp.float32)]
    unnamed x170 -> x45, local copies, waits for them, and re-layouts: 28.4 us -> 3.59 us
  transfers between devices with their start and end apart: 12 -> 45, of which waited for: 5 -> 18; matrix products, arithmetic and copies ran while one was open for 17% -> 7% of each run, Pallas kernels for 0% -> 31%
where the time goes in v2:
time: 407 us; the launch traced here: 402 us
  Pallas kernels  261 us (64%)
  starting transfers between devices  56.5 us (14%)
  waiting for transfers between devices  38.2 us (9%)
  local copies, waits for them, and re-layouts  24.9 us (6%)
  other arithmetic  19.7 us (5%)
    pallas_call x3, Pallas kernels, attn_backward(): pl.pallas_call(partial(bwd_kernel, pairs=pairs, first_pair=first_pair, ti...  82.6 us
    pallas_call x1, Pallas kernels, attn_forward(): pl.pallas_call(partial(fwd_kernel, pairs=pairs, per_block=per_block), gri...  75.1 us
    pallas_call x1, Pallas kernels, feed_forward(): pl.pallas_call(partial(ffn_kernel, rows=rows), grid=(steps,), in_specs=[w...  63.1 us
    pallas_call x2, Pallas kernels, qkv_backward(): pl.pallas_call(partial(qkv_back_kernel, half=half, final=final, pairs=pai...  32.5 us
    ppermute x18, waiting for transfers between devices, exchange_sum(): lax.ppermute(send, axis, swap_on(axis, step * stride)).astype(F32)  31.1 us
    ppermute x18, starting transfers between devices, exchange_sum(): lax.ppermute(send, axis, swap_on(axis, step * stride)).astype(F32)  25.9 us
    convert_element_type x10, other arithmetic, add_low(): return (kept.astype(F32) + received.astype(F32)).astype(BF16)  10.8 us
    ppermute x9, starting transfers between devices, exchange_all(): lax.ppermute(piece, axis, swap_on(axis, step))  10.7 us
  transfers between devices with their start and end apart: 45, of which 18 were waited for; matrix products, arithmetic and copies ran while one was open for 7% of the time, Pallas kernels for 31%

profile of v2, /device:TPU:0, one launch (start us, length us, event | category | flops | bytes accessed | tf_op | source)
XLA Modules:
  0.0 402.3 jit_solution(4700017569989727472)
XLA Ops:
  3.5 3.0 collective-permute-start.1
  11.7 4.7 %collective-permute-start.5 = (bf16[64,768]{1,0:T(8,128)(2,1)S(1)}, bf16[64,768]{1,0:T(8,128)(2,1)S(1)}, u32[]{:S(2)}, u32[]{:S(2)}) collective-permute-start(bf16[64,768]{1,0:T(8,128)(2,1)S(1)} %pad_maximum_fusion.9), channel_id=1, source_target_pairs={{0,6},{1,7},{2,4},{3,5},{4,2},{5,3},{6,0},{7,1},{8,14},{9,15},{10,... | collective-permute-start | bytes 294920 | tf_op jit(solution)/shard_map/ppermute | solution.py:886
  17.1 8.2 %project_tokens.1 = (bf16[1024,768]{1,0:T(8,128)(2,1)}, bf16[1024,768]{1,0:T(8,128)(2,1)}, bf16[1024,768]{1,0:T(8,128)(2,1)}, bf16[768,1024]{1,0:T(8,128)(2,1)}) custom-call(bf16[1024,768]{1,0:T(8,128)(2,1)} %bitcast.249, bf16[768,2304]{1,0:T(8,128)(2,1)} %refs_2_.3, f32[4,768]{1,0:T(4,128)} %pad_maximum_fusion.10.norms_ref.refs_19_), custom_call_target="tpu_custom_call" | custom-call | flops 8000000000 | tf_op jit(solution)/shard_map/project_tokens/pallas_call | solution.py:149
  26.3 75.1 %attn_forward.1 = (bf16[1024,768]{1,0:T(8,128)(2,1)}, bf16[8,12,128,384]{3,2,1,0:T(8,128)(2,1)}, bf16[8,6,128,128]{3,2,1,0:T(8,128)(2,1)}, bf16[8,12,128,384]{3,...) custom-call(s32[1,4]{1,0:T(1,128)} %units_ref.1, ...), custom_call_target="tpu_custom_call" | custom-call | flops 65000001536 | tf_op jit(solution)/shard_map/attn_forward/pallas_call | solution.py:301
  101.4 63.1 %feed_forward.1 = (bf16[1024,768]{1,0:T(8,128)(2,1)}, f32[1024,768]{1,0:T(8,128)}, bf16[1024,768]{1,0:T(8,128)(2,1)}, bf16[768,768]{1,0:T(8,128)(2,1)}, bf16[768...) custom-call(bf16[1024,768]{1,0:T(8,128)(2,1)} %bitcast.250, ...), custom_call_target="tpu_custom_call" | custom-call | flops 60000002048 | tf_op jit(solution)/shard_map/feed_forward/pallas_call | solution.py:651
  165.6 3.4 dynamic-slice_bitcast_fusion.1
  171.8 21.2 %attn_backward_edge.1 = (bf16[256,768]{1,0:T(8,128)(2,1)}, f32[2,768,384]{2,1,0:T(8,128)}, f32[2,768,384]{2,1,0:T(8,128)}, f32[2,64,768]{2,1,0:T(8,128)}, f32[2,64,768]{2,1,0:T(8,128)}, /*index=5*/f32[6,16,128]{2,1,0:T(8,128)}) custom-call(s32[1,1]{1,0:T(1,128)} %bitcast.1.offset_ref, f32[4,12]{1,0:T(4,128)} %bias_ref.7, f32[2,12]{1,0:T(2,128)} %theta_ref.7, ...), custom_call_target="tpu_custom_call" | custom-call | flops 16400000000 | tf_op jit(solution)/shard_map/attn_backward_edge/pallas_call | solution.py:545
  193.0 1.9 convert.30
  195.7 2.2 collective-permute-start.9
  200.6 2.2 fusion
  202.9 2.6 fusion.1
  208.3 2.0 collective-permute-start.12
  213.1 30.7 %attn_backward_mid.2 = (bf16[768,384]{1,0:T(8,128)(2,1)}, f32[384,1024]{1,0:T(8,128)}, f32[384,1024]{1,0:T(8,128)}, f32[2,64,384]{2,1,0:T(8,128)}, f32[2,64,384]{2,1,0:T(8,128)}, /*index=5*/f32[3,16,128]{2,1,0:T(8,128)}) custom-call(s32[1,1]{1,0:T(1,128)} %bitcast.1.offset_ref, f32[4,12]{1,0:T(4,128)} %bias_ref.7, f32[2,12]{1,0:T(2,128)} %theta_ref.7, ...), custom_call_target="tpu_custom_call" | custom-call | flops 24600000512 | tf_op jit(solution)/shard_map/attn_backward_mid/pallas_call | solution.py:545
  245.5 2.1 fusion.3
  248.5 13.9 %qkv_backward.2 = (bf16[768,1152]{1,0:T(8,128)(2,1)}, f32[1024,768]{1,0:T(8,128)}, f32[128,768]{1,0:T(8,128)}) custom-call(bf16[768,1024]{1,0:T(8,128)(2,1)} %get-tuple-element.102.refs_0_, bf16[2,64,768]{2,1,0:T(8,128)(2,1)} %get-tuple-element.103.refs_1_, bf16[768,2304]{1,0:T(8,128)(2,1)} %refs_2_.3, bf16[256,768]{1,0:T(8,128)(2,1)} %get-tuple-element.121.refs_3_, ...), custom_call_target="tpu_custom_call" | custom-call | flops 8000000000 | tf_op jit(solution)/shard_map/qkv_backward/pallas_call | solution.py:818
  267.8 2.3 collective-permute-start.16
  270.1 2.5 collective-permute-start.18
  272.8 30.7 %attn_backward_mid.3 = (bf16[768,384]{1,0:T(8,128)(2,1)}, f32[384,1024]{1,0:T(8,128)}, f32[384,1024]{1,0:T(8,128)}, f32[2,64,384]{2,1,0:T(8,128)}, f32[2,64,384]{2,1,0:T(8,128)}, /*index=5*/f32[3,16,128]{2,1,0:T(8,128)}) custom-call(s32[1,1]{1,0:T(1,128)} %bitcast.1.offset_ref, f32[4,12]{1,0:T(4,128)} %bias_ref.7, f32[2,12]{1,0:T(2,128)} %theta_ref.7, ...), custom_call_target="tpu_custom_call" | custom-call | flops 24600000512 | tf_op jit(solution)/shard_map/attn_backward_mid/pallas_call | solution.py:545
  303.7 2.5 collective-permute-start.25
  306.7 18.6 %qkv_backward.3 = (bf16[768,1152]{1,0:T(8,128)(2,1)}, bf16[768,128]{1,0:T(8,128)(2,1)}, bf16[1024,768]{1,0:T(8,128)(2,1)}, bf16[256,768]{1,0:T(8,128)(2,1)}) custom-call(bf16[768,1024]{1,0:T(8,128)(2,1)} %get-tuple-element.102.refs_0_, bf16[2,64,768]{2,1,0:T(8,128)(2,1)} %get-tuple-element.103.refs_1_, bf16[768,2304]{1,0:T(8,128)(2,1)} %refs_2_.3, ...), custom_call_target="tpu_custom_call" | custom-call | flops 15000000512 | tf_op jit(solution)/shard_map/qkv_backward/pallas_call | solution.py:818
  327.1 2.4 collective-permute-start.28
  330.2 4.6 %collective-permute-done.26 = bf16[4,24,1152]{2,1,0:T(8,128)(2,1)S(1)} collective-permute-done((bf16[4,24,1152]{2,1,0:T(8,128)(2,1)S(1)}, bf16[4,24,1152]{2,1,0:T(8,128)(2,1)S(1)}, u32[]{:S(2)}, u32[]{:S(2)}) %collective-permute-start.26) | collective-permute-done | bytes 221216 | tf_op jit(solution)/shard_map/ppermute | solution.py:868
  336.5 3.7 collective-permute-done.28
  340.2 2.9 collective-permute-start.22
  346.4 3.1 collective-permute-start.31
  352.5 2.7 collective-permute-done.30
  355.2 2.8 collective-permute-done.23
  369.8 5.2 %collective-permute-done.36 = bf16[4,24,1280]{2,1,0:T(8,128)(2,1)S(1)} collective-permute-done((bf16[4,24,1280]{2,1,0:T(8,128)(2,1)S(1)}, bf16[4,24,1280]{2,1,0:T(8,128)(2,1)S(1)}, u32[]{:S(2)}, u32[]{:S(2)}) %collective-permute-start.36) | collective-permute-done | bytes 245792 | tf_op jit(solution)/shard_map/ppermute | solution.py:868
  375.0 5.0 %collective-permute-done.38 = bf16[4,24,1280]{2,1,0:T(8,128)(2,1)S(1)} collective-permute-done((bf16[4,24,1280]{2,1,0:T(8,128)(2,1)S(1)}, bf16[4,24,1280]{2,1,0:T(8,128)(2,1)S(1)}, u32[]{:S(2)}, u32[]{:S(2)}) %collective-permute-start.38) | collective-permute-done | bytes 245792 | tf_op jit(solution)/shard_map/ppermute | solution.py:868
  381.5 2.5 collective-permute-start.39
  386.3 3.7 collective-permute-done.41
  395.3 2.0 collective-permute-done.44
  (199 shorter events, 67.2 us)
Async XLA Ops:
  0.6 10.2 %collective-permute-start = (bf16[32,768]{1,0:T(8,128)(2,1)}, bf16[32,768]{1,0:T(8,128)(2,1)S(1)}, u32[]{:S(2)}, u32[]{:S(2)}) collective-permute-start(bf16[32,768]{1,0:T(8,128)(2,1)} %bitcast.229), channel_id=1, source_target_pairs={{0,1},{1,0},{2,3},{3,2},{4,5},{5,4},{6,7},{7,6},{8,9},{9,8},{10,11... | collective-permute-start | bytes 147464 | tf_op jit(solution)/shard_map/ppermute | solution.py:879
  2.2 9.5 %collective-permute-start.2 = (bf16[128,768]{1,0:T(8,128)(2,1)S(1)}, bf16[128,768]{1,0:T(8,128)(2,1)S(1)}, u32[]{:S(2)}, u32[]{:S(2)}) collective-permute-start(bf16[128,768]{1,0:T(8,128)(2,1)S(1)} %get-tuple-element.210), channel_id=1, source_target_pairs={{1,0},{2,1},{3,2},{4,3},{5,4},{6,5},{7,6},{9,8},{10,9},{11,10},{12... | collective-permute-start | bytes 589832 | tf_op jit(solution)/shard_map/ppermute | solution.py:942
  3.5 8.2 %collective-permute-start.1 = (bf16[128,768]{1,0:T(8,128)(2,1)S(1)}, bf16[128,768]{1,0:T(8,128)(2,1)S(1)}, u32[]{:S(2)}, u32[]{:S(2)}) collective-permute-start(bf16[128,768]{1,0:T(8,128)(2,1)S(1)} %get-tuple-element.211), channel_id=1, source_target_pairs={{0,1},{1,2},{2,3},{3,4},{4,5},{5,6},{6,7},{8,9},{9,10},{10,11},{11... | collective-permute-start | bytes 589832 | tf_op jit(solution)/shard_map/ppermute | solution.py:941
  11.7 13.5 %collective-permute-start.5 = (bf16[64,768]{1,0:T(8,128)(2,1)S(1)}, bf16[64,768]{1,0:T(8,128)(2,1)S(1)}, u32[]{:S(2)}, u32[]{:S(2)}) collective-permute-start(bf16[64,768]{1,0:T(8,128)(2,1)S(1)} %pad_maximum_fusion.9), channel_id=1, source_target_pairs={{0,6},{1,7},{2,4},{3,5},{4,2},{5,3},{6,0},{7,1},{8,14},{9,15},{10,... | collective-permute-start | bytes 294920 | tf_op jit(solution)/shard_map/ppermute | solution.py:886
  16.5 8.8 %collective-permute-start.4 = (bf16[64,768]{1,0:T(8,128)(2,1)S(1)}, bf16[64,768]{1,0:T(8,128)(2,1)S(1)}, u32[]{:S(2)}, u32[]{:S(2)}) collective-permute-start(bf16[64,768]{1,0:T(8,128)(2,1)S(1)} %pad_maximum_fusion.9), channel_id=1, source_target_pairs={{0,4},{1,5},{2,6},{3,7},{4,0},{5,1},{6,2},{7,3},{8,12},{9,13},{10,... | collective-permute-start | bytes 294920 | tf_op jit(solution)/shard_map/ppermute | solution.py:886
  16.5 8.8 %collective-permute-start.3 = (bf16[64,768]{1,0:T(8,128)(2,1)S(1)}, bf16[64,768]{1,0:T(8,128)(2,1)S(1)}, u32[]{:S(2)}, u32[]{:S(2)}) collective-permute-start(bf16[64,768]{1,0:T(8,128)(2,1)S(1)} %pad_maximum_fusion.9), channel_id=1, source_target_pairs={{0,2},{1,3},{2,0},{3,1},{4,6},{5,7},{6,4},{7,5},{8,10},{9,11},{10,... | collective-permute-start | bytes 294920 | tf_op jit(solution)/shard_map/ppermute | solution.py:886
  170.6 28.7 %collective-permute-start.6 = (bf16[4,96,3072]{2,1,0:T(8,128)(2,1)}, bf16[4,96,3072]{2,1,0:T(8,128)(2,1)}, u32[]{:S(2)}, u32[]{:S(2)}) collective-permute-start(bf16[4,96,3072]{2,1,0:T(8,128)(2,1)} %dynamic-slice_bitcast_fusion.1), channel_id=1, source_target_pairs={{0,1},{1,0},{2,3},{3,2},{4,5},{5,4},{6,7},{7,6},{8,9},{9,8},{10,11... | collective-permute-start | bytes 7077896 | tf_op jit(solution)/shard_map/ppermute | solution.py:848
  171.0 28.3 %collective-permute-start.7 = (bf16[4,384,768]{2,1,0:T(8,128)(2,1)}, bf16[4,384,768]{2,1,0:T(8,128)(2,1)}, u32[]{:S(2)}, u32[]{:S(2)}) collective-permute-start(bf16[4,384,768]{2,1,0:T(8,128)(2,1)} %dynamic-slice_bitcast_fusion), channel_id=1, source_target_pairs={{0,1},{1,0},{2,3},{3,2},{4,5},{5,4},{6,7},{7,6},{8,9},{9,8},{10,11... | collective-permute-start | bytes 7077896 | tf_op jit(solution)/shard_map/ppermute | solution.py:848
  171.3 28.0 %collective-permute-start.8 = (bf16[4,96,768]{2,1,0:T(8,128)(2,1)S(1)}, bf16[4,96,768]{2,1,0:T(8,128)(2,1)}, u32[]{:S(2)}, u32[]{:S(2)}) collective-permute-start(bf16[4,96,768]{2,1,0:T(8,128)(2,1)S(1)} %dynamic-slice_bitcast_fusion.8), channel_id=1, source_target_pairs={{0,1},{1,0},{2,3},{3,2},{4,5},{5,4},{6,7},{7,6},{8,9},{9,8},{10,11... | collective-permute-start | bytes 1769480 | tf_op jit(solution)/shard_map/ppermute | solution.py:848
  195.7 11.3 %collective-permute-start.9 = (bf16[2,768,128]{2,1,0:T(8,128)(2,1)S(1)}, bf16[2,768,128]{2,1,0:T(8,128)(2,1)S(1)}, u32[]{:S(2)}, u32[]{:S(2)}) collective-permute-start(bf16[2,768,128]{2,1,0:T(8,128)(2,1)S(1)} %pad_maximum_fusion.5), channel_id=1, source_target_pairs={{0,1},{1,2},{2,3},{3,4},{4,5},{5,6},{6,7},{8,9},{9,10},{10,11},{11... | collective-permute-start | bytes 1179656 | tf_op jit(solution)/shard_map/ppermute | solution.py:968
  198.0 9.0 %collective-permute-start.10 = (bf16[2,768,128]{2,1,0:T(8,128)(2,1)S(1)}, bf16[2,768,128]{2,1,0:T(8,128)(2,1)S(1)}, u32[]{:S(2)}, u32[]{:S(2)}) collective-permute-start(bf16[2,768,128]{2,1,0:T(8,128)(2,1)S(1)} %pad_maximum_fusion.6), channel_id=1, source_target_pairs={{1,0},{2,1},{3,2},{4,3},{5,4},{6,5},{7,6},{9,8},{10,9},{11,10},{12... | collective-permute-start | bytes 1179656 | tf_op jit(solution)/shard_map/ppermute | solution.py:968
  208.3 35.5 %collective-permute-start.12 = (bf16[2,4,216,384]{3,2,0,1:T(8,128)(2,1)}, bf16[2,4,216,384]{3,2,0,1:T(8,128)(2,1)}, u32[]{:S(2)}, u32[]{:S(2)}) collective-permute-start(bf16[2,4,216,384]{3,2,0,1:T(8,128)(2,1)} %dynamic-slice_bitcast_fusion.2), channel_id=1, source_target_pairs={{0,16},{8,24},{16,0},{24,8},{1,17},{9,25},{17,1},{25,9},{2,18},{10... | collective-permute-start | bytes 3981320 | tf_op jit(solution)/shard_map/ppermute | solution.py:860
  211.6 33.9 %collective-permute-start.11 = (bf16[2,4,216,384]{3,2,1,0:T(8,128)(2,1)}, bf16[2,4,216,384]{3,2,1,0:T(8,128)(2,1)}, u32[]{:S(2)}, u32[]{:S(2)}) collective-permute-start(bf16[2,4,216,384]{3,2,1,0:T(8,128)(2,1)} %dynamic-slice_bitcast_fusion.3), channel_id=1, source_target_pairs={{0,8},{8,0},{16,24},{24,16},{1,9},{9,1},{17,25},{25,17},{2,10},{10... | collective-permute-start | bytes 3981320 | tf_op jit(solution)/shard_map/ppermute | solution.py:860
  247.8 17.7 %collective-permute-start.14 = (bf16[4,216,384]{2,1,0:T(8,128)(2,1)S(1)}, bf16[4,216,384]{2,1,0:T(8,128)(2,1)S(1)}, u32[]{:S(2)}, u32[]{:S(2)}) collective-permute-start(bf16[4,216,384]{2,1,0:T(8,128)(2,1)S(1)} %dynamic-slice_bitcast_fusion.6), channel_id=1, source_target_pairs={{0,8},{8,0},{16,24},{24,16},{1,9},{9,1},{17,25},{25,17},{2,10},{10... | collective-permute-start | bytes 1990664 | tf_op jit(solution)/shard_map/ppermute | solution.py:860
  248.4 17.4 %collective-permute-start.13 = (bf16[4,216,384]{2,1,0:T(8,128)(2,1)S(1)}, bf16[4,216,384]{2,1,0:T(8,128)(2,1)S(1)}, u32[]{:S(2)}, u32[]{:S(2)}) collective-permute-start(bf16[4,216,384]{2,1,0:T(8,128)(2,1)S(1)} %dynamic-slice_bitcast_fusion.7), channel_id=1, source_target_pairs={{0,16},{8,24},{16,0},{24,8},{1,17},{9,25},{17,1},{25,9},{2,18},{10... | collective-permute-start | bytes 1990664 | tf_op jit(solution)/shard_map/ppermute | solution.py:860
  267.8 35.7 %collective-permute-start.16 = (bf16[216,768]{1,0:T(8,128)(2,1)S(1)}, bf16[216,768]{1,0:T(8,128)(2,1)S(1)}, u32[]{:S(2)}, u32[]{:S(2)}) collective-permute-start(bf16[216,768]{1,0:T(8,128)(2,1)S(1)} %get-tuple-element.212), channel_id=1, source_target_pairs={{0,2},{1,3},{2,0},{3,1},{4,6},{5,7},{6,4},{7,5},{8,10},{9,11},{10,... | collective-permute-start | bytes 995336 | tf_op jit(solution)/shard_map/ppermute | solution.py:868
  270.1 33.4 %collective-permute-start.18 = (bf16[216,768]{1,0:T(8,128)(2,1)S(1)}, bf16[216,768]{1,0:T(8,128)(2,1)S(1)}, u32[]{:S(2)}, u32[]{:S(2)}) collective-permute-start(bf16[216,768]{1,0:T(8,128)(2,1)S(1)} %get-tuple-element.213), channel_id=1, source_target_pairs={{0,6},{1,7},{2,4},{3,5},{4,2},{5,3},{6,0},{7,1},{8,14},{9,15},{10,... | collective-permute-start | bytes 995336 | tf_op jit(solution)/shard_map/ppermute | solution.py:868
  272.6 30.9 %collective-permute-start.17 = (bf16[216,768]{1,0:T(8,128)(2,1)S(1)}, bf16[216,768]{1,0:T(8,128)(2,1)S(1)}, u32[]{:S(2)}, u32[]{:S(2)}) collective-permute-start(bf16[216,768]{1,0:T(8,128)(2,1)S(1)} %get-tuple-element.214), channel_id=1, source_target_pairs={{0,4},{1,5},{2,6},{3,7},{4,0},{5,1},{6,2},{7,3},{8,12},{9,13},{10,... | collective-permute-start | bytes 995336 | tf_op jit(solution)/shard_map/ppermute | solution.py:868
  303.7 51.5 %collective-permute-start.25 = (bf16[216,768]{1,0:T(8,128)(2,1)S(1)}, bf16[216,768]{1,0:T(8,128)(2,1)S(1)}, u32[]{:S(2)}, u32[]{:S(2)}) collective-permute-start(bf16[216,768]{1,0:T(8,128)(2,1)S(1)} %fusion.12), channel_id=1, source_target_pairs={{0,24},{8,16},{16,8},{24,0},{1,25},{9,17},{17,9},{25,1},{2,26},{10... | collective-permute-start | bytes 995336 | tf_op jit(solution)/shard_map/ppermute | solution.py:874
  306.2 49.0 %collective-permute-start.24 = (bf16[216,768]{1,0:T(8,128)(2,1)S(1)}, bf16[216,768]{1,0:T(8,128)(2,1)S(1)}, u32[]{:S(2)}, u32[]{:S(2)}) collective-permute-start(bf16[216,768]{1,0:T(8,128)(2,1)S(1)} %fusion.12), channel_id=1, source_target_pairs={{0,16},{8,24},{16,0},{24,8},{1,17},{9,25},{17,1},{25,9},{2,18},{10... | collective-permute-start | bytes 995336 | tf_op jit(solution)/shard_map/ppermute | solution.py:874
  326.5 8.3 %collective-permute-start.26 = (bf16[4,24,1152]{2,1,0:T(8,128)(2,1)S(1)}, bf16[4,24,1152]{2,1,0:T(8,128)(2,1)S(1)}, u32[]{:S(2)}, u32[]{:S(2)}) collective-permute-start(bf16[4,24,1152]{2,1,0:T(8,128)(2,1)S(1)} %get-tuple-element.222), channel_id=1, source_target_pairs={{0,8},{8,0},{16,24},{24,16},{1,9},{9,1},{17,25},{25,17},{2,10},{10... | collective-permute-start | bytes 663560 | tf_op jit(solution)/shard_map/ppermute | solution.py:868
  327.1 13.1 %collective-permute-start.28 = (bf16[4,24,1152]{2,1,0:T(8,128)(2,1)S(1)}, bf16[4,24,1152]{2,1,0:T(8,128)(2,1)S(1)}, u32[]{:S(2)}, u32[]{:S(2)}) collective-permute-start(bf16[4,24,1152]{2,1,0:T(8,128)(2,1)S(1)} %get-tuple-element.223), channel_id=1, source_target_pairs={{0,24},{8,16},{16,8},{24,0},{1,25},{9,17},{17,9},{25,1},{2,26},{10... | collective-permute-start | bytes 663560 | tf_op jit(solution)/shard_map/ppermute | solution.py:868
  329.5 13.5 %collective-permute-start.27 = (bf16[4,24,1152]{2,1,0:T(8,128)(2,1)S(1)}, bf16[4,24,1152]{2,1,0:T(8,128)(2,1)S(1)}, u32[]{:S(2)}, u32[]{:S(2)}) collective-permute-start(bf16[4,24,1152]{2,1,0:T(8,128)(2,1)S(1)} %get-tuple-element.224), channel_id=1, source_target_pairs={{0,16},{8,24},{16,0},{24,8},{1,17},{9,25},{17,1},{25,9},{2,18},{10... | collective-permute-start | bytes 663560 | tf_op jit(solution)/shard_map/ppermute | solution.py:868
  334.8 9.6 %collective-permute-start.20 = (bf16[32,768]{1,0:T(8,128)(2,1)S(1)}, bf16[32,768]{1,0:T(8,128)(2,1)S(1)}, u32[]{:S(2)}, u32[]{:S(2)}) collective-permute-start(bf16[32,768]{1,0:T(8,128)(2,1)S(1)} %get-tuple-element.231), channel_id=1, source_target_pairs={{0,2},{1,3},{2,0},{3,1},{4,6},{5,7},{6,4},{7,5},{8,10},{9,11},{10,... | collective-permute-start | bytes 147464 | tf_op jit(solution)/shard_map/ppermute | solution.py:868
  340.2 6.2 %collective-permute-start.22 = (bf16[32,768]{1,0:T(8,128)(2,1)S(1)}, bf16[32,768]{1,0:T(8,128)(2,1)S(1)}, u32[]{:S(2)}, u32[]{:S(2)}) collective-permute-start(bf16[32,768]{1,0:T(8,128)(2,1)S(1)} %get-tuple-element.232), channel_id=1, source_target_pairs={{0,6},{1,7},{2,4},{3,5},{4,2},{5,3},{6,0},{7,1},{8,14},{9,15},{10,... | collective-permute-start | bytes 147464 | tf_op jit(solution)/shard_map/ppermute | solution.py:868
  343.1 6.4 %collective-permute-start.21 = (bf16[32,768]{1,0:T(8,128)(2,1)S(1)}, bf16[32,768]{1,0:T(8,128)(2,1)S(1)}, u32[]{:S(2)}, u32[]{:S(2)}) collective-permute-start(bf16[32,768]{1,0:T(8,128)(2,1)S(1)} %get-tuple-element.233), channel_id=1, source_target_pairs={{0,4},{1,5},{2,6},{3,7},{4,0},{5,1},{6,2},{7,3},{8,12},{9,13},{10,... | collective-permute-start | bytes 147464 | tf_op jit(solution)/shard_map/ppermute | solution.py:868
  350.4 7.5 %collective-permute-start.23 = (bf16[216,768]{1,0:T(8,128)(2,1)S(1)}, bf16[216,768]{1,0:T(8,128)(2,1)S(1)}, u32[]{:S(2)}, u32[]{:S(2)}) collective-permute-start(bf16[216,768]{1,0:T(8,128)(2,1)S(1)} %fusion.12), channel_id=1, source_target_pairs={{0,8},{8,0},{16,24},{24,16},{1,9},{9,1},{17,25},{25,17},{2,10},{10... | collective-permute-start | bytes 995336 | tf_op jit(solution)/shard_map/ppermute | solution.py:874
  358.6 7.1 %collective-permute-start.34 = (bf16[24,1152]{1,0:T(8,128)(2,1)S(1)}, bf16[24,1152]{1,0:T(8,128)(2,1)S(1)}, u32[]{:S(2)}, u32[]{:S(2)}) collective-permute-start(bf16[24,1152]{1,0:T(8,128)(2,1)S(1)} %fusion.32), channel_id=1, source_target_pairs={{0,24},{8,16},{16,8},{24,0},{1,25},{9,17},{17,9},{25,1},{2,26},{10... | collective-permute-start | bytes 165896 | tf_op jit(solution)/shard_map/ppermute | solution.py:874
  359.2 6.6 %collective-permute-start.33 = (bf16[24,1152]{1,0:T(8,128)(2,1)S(1)}, bf16[24,1152]{1,0:T(8,128)(2,1)S(1)}, u32[]{:S(2)}, u32[]{:S(2)}) collective-permute-start(bf16[24,1152]{1,0:T(8,128)(2,1)S(1)} %fusion.32), channel_id=1, source_target_pairs={{0,16},{8,24},{16,0},{24,8},{1,17},{9,25},{17,1},{25,9},{2,18},{10... | collective-permute-start | bytes 165896 | tf_op jit(solution)/shard_map/ppermute | solution.py:874
  366.2 8.8 %collective-permute-start.36 = (bf16[4,24,1280]{2,1,0:T(8,128)(2,1)S(1)}, bf16[4,24,1280]{2,1,0:T(8,128)(2,1)S(1)}, u32[]{:S(2)}, u32[]{:S(2)}) collective-permute-start(bf16[4,24,1280]{2,1,0:T(8,128)(2,1)S(1)} %get-tuple-element.219), channel_id=1, source_target_pairs={{0,8},{8,0},{16,24},{24,16},{1,9},{9,1},{17,25},{25,17},{2,10},{10... | collective-permute-start | bytes 737288 | tf_op jit(solution)/shard_map/ppermute | solution.py:868
  366.8 13.1 %collective-permute-start.38 = (bf16[4,24,1280]{2,1,0:T(8,128)(2,1)S(1)}, bf16[4,24,1280]{2,1,0:T(8,128)(2,1)S(1)}, u32[]{:S(2)}, u32[]{:S(2)}) collective-permute-start(bf16[4,24,1280]{2,1,0:T(8,128)(2,1)S(1)} %get-tuple-element.220), channel_id=1, source_target_pairs={{0,24},{8,16},{16,8},{24,0},{1,25},{9,17},{17,9},{25,1},{2,26},{10... | collective-permute-start | bytes 737288 | tf_op jit(solution)/shard_map/ppermute | solution.py:868
  368.3 13.1 %collective-permute-start.37 = (bf16[4,24,1280]{2,1,0:T(8,128)(2,1)S(1)}, bf16[4,24,1280]{2,1,0:T(8,128)(2,1)S(1)}, u32[]{:S(2)}, u32[]{:S(2)}) collective-permute-start(bf16[4,24,1280]{2,1,0:T(8,128)(2,1)S(1)} %get-tuple-element.221), channel_id=1, source_target_pairs={{0,16},{8,24},{16,0},{24,8},{1,17},{9,25},{17,1},{25,9},{2,18},{10... | collective-permute-start | bytes 737288 | tf_op jit(solution)/shard_map/ppermute | solution.py:868
  (31 other events, 167.7 us)

commit v3 on v2

--- a/solution.py
+++ b/solution.py
@@ -21,7 +21,10 @@
 SPAN = 384
 LOG2E = math.log2(math.e)
 FAR_AWAY = 1e15
-CH = 16
+CH = 128
+UNROLL = 6
+BACK_CH = 128
+BACK_UNROLL = 3
 F32 = jnp.float32
 BF16 = jnp.bfloat16
 VMEM_LIMIT = 58 * 1024 * 1024
@@ -214,50 +217,53 @@
     rows = pl.ds(pl.multiple_of(t * TILE, TILE), SPAN)
     root = math.sqrt(0.5 * LOG2E)
 
-    def one_pair(p, carry):
+    def widths_of(p):
+        return [[theta_ref[i, 2 * p + e] * root for i in range(2)] for e in range(2)]
+
+    def scores(p, slot):
         cols = pl.ds(pl.multiple_of(p * 128, 128), 128)
         qp = q_ref[:, cols]
         kp = kp_ref[rows, cols]
-        vp = vp_ref[rows, cols]
         kgp = kg_ref[0, :, cols]
-        vgp = vg_ref[0, :, cols]
-        widths = [[theta_ref[i, 2 * p + e] * root for i in range(2)] for e in range(2)]
+        widths = widths_of(p)
         scales = by_row([LOG2E, LOG2E] + widths[0] + [LOG2E, LOG2E] + widths[1])
         biases = by_row([bias_ref[c, 2 * p + e] for e in range(2) for c in range(4)]) * scales
-        s_ref[...] = mm_nt(jnp.concatenate([qp * lo16, qp * hi16], axis=0), kp)
-        sf_ref[...] = mm_nt(qp, jnp.concatenate([kgp * lo16, kgp * hi16], axis=0))
+        s_ref[slot] = mm_nt(jnp.concatenate([qp * lo16, qp * hi16], axis=0), kp)
+        sf_ref[slot] = mm_nt(qp, jnp.concatenate([kgp * lo16, kgp * hi16], axis=0))
         a, b = rich_sums(qp, kp, rq_ref[:, cols], rk_ref[:, cols], scales, biases)
-        a_ref[...] = a
-        b_ref[...] = b
+        a_ref[slot] = a
+        b_ref[slot] = b
+
+    def weights(p, slot):
+        widths = widths_of(p)
         for r in range(0, TILE, CH):
             rs = slice(r, r + CH)
-            far = sf_ref[rs, :] * (0.125 * LOG2E)
+            far = sf_ref[slot, rs, :] * (0.125 * LOG2E)
             tops = []
             held = []
             for e in range(2):
                 base = 4 * e
-                part = [a_ref[rs, base + c : base + c + 1] for c in range(4)]
-                line = [b_ref[base + c : base + c + 1, :] for c in range(4)]
+                part = [a_ref[slot, rs, base + c : base + c + 1] for c in range(4)]
+                line = [b_ref[slot, base + c : base + c + 1, :] for c in range(4)]
                 u0 = (part[0] + line[0]) * ox_ref[rs, :]
                 u1 = (part[1] + line[1]) * oy_ref[rs, :]
                 e0 = jnp.exp2(jnp.minimum(u0, -u0))
                 e1 = jnp.exp2(jnp.minimum(u1, -u1))
-                f0 = 1.0 + e0
-                f1 = 1.0 + e1
-                rr = 1.0 / (f0 * f1)
+                r0 = 1.0 / (1.0 + e0)
+                r1 = 1.0 / (1.0 + e1)
                 gx = (widths[e][0] * dx_ref[rs, :] - part[2]) - line[2]
                 gy = (widths[e][1] * dy_ref[rs, :] - part[3]) - line[3]
-                s = s_ref[e * TILE + r : e * TILE + r + CH, :] * (0.125 * LOG2E)
+                s = s_ref[slot, e * TILE + r : e * TILE + r + CH, :] * (0.125 * LOG2E)
                 s = s + jnp.minimum(u0, 0.0) + jnp.minimum(u1, 0.0) - gx * gx - gy * gy
                 top = jnp.maximum(jnp.maximum(s[:, 0:128], s[:, 128:256]), s[:, 256:384])
                 here = low if e == 0 else ~low
                 top = jnp.maximum(top, jnp.where(here, far, -3e38))
                 tops.append(jnp.max(top, axis=1, keepdims=True))
-                g0 = jnp.where(u0 >= 0.0, e0, 1.0) * ox_ref[rs, :] * (f1 * rr)
-                g1 = jnp.where(u1 >= 0.0, e1, 1.0) * oy_ref[rs, :] * (f0 * rr)
+                g0 = jnp.where(u0 >= 0.0, e0, 1.0) * (ox_ref[rs, :] * r0)
+                g1 = jnp.where(u1 >= 0.0, e1, 1.0) * (oy_ref[rs, :] * r1)
                 g0_ref[0, 2 * p + e, rs, :] = g0.astype(BF16)
                 g1_ref[0, 2 * p + e, rs, :] = g1.astype(BF16)
-                held.append((s, rr))
+                held.append((s, r0 * r1))
             pfar = jnp.exp2(far - jnp.where(low, tops[0], tops[1]))
             invs = []
             for e in range(2):
@@ -269,12 +275,26 @@
                 invs.append(inv)
                 pn_ref[0, 2 * p + e, rs, :] = (pe * inv).astype(BF16)
             pf_ref[0, p, rs, :] = (pfar * jnp.where(low, invs[0], invs[1])).astype(BF16)
+
+    def context(p):
+        cols = pl.ds(pl.multiple_of(p * 128, 128), 128)
+        vp = vp_ref[rows, cols]
+        vgp = vg_ref[0, :, cols]
         ctx = mm(pn_ref[0, 2 * p], vp * lo16) + mm(pn_ref[0, 2 * p + 1], vp * hi16)
         ctx = ctx + mm(pf_ref[0, p], jnp.concatenate([vgp * lo16, vgp * hi16], axis=0))
         ctx_ref[:, cols] = ctx.astype(BF16)
+
+    def group(index, carry):
+        first = index * UNROLL
+        for u in range(UNROLL):
+            scores(first + u, u)
+        for u in range(UNROLL):
+            weights(first + u, u)
+        for u in range(UNROLL):
+            context(first + u)
         return carry
 
-    lax.fori_loop(0, pairs, one_pair, 0)
+    lax.fori_loop(0, pairs // UNROLL, group, 0)
 
 
 def attn_forward(q, k, v, before, after, every_glob, owner, w_qkv, norms, coords, units, lengths, offset, rich):
@@ -335,8 +355,8 @@
         scratch_shapes=[
             pltpu.VMEM((TILE, SPAN), F32), pltpu.VMEM((TILE, SPAN), F32),
             pltpu.VMEM((TILE, SPAN), F32), pltpu.VMEM((TILE, SPAN), F32),
-            pltpu.VMEM((2 * TILE, SPAN), F32), pltpu.VMEM((TILE, 128), F32),
-            pltpu.VMEM((TILE, 8), F32), pltpu.VMEM((8, SPAN), F32),
+            pltpu.VMEM((UNROLL, 2 * TILE, SPAN), F32), pltpu.VMEM((UNROLL, TILE, 128), F32),
+            pltpu.VMEM((UNROLL, TILE, 8), F32), pltpu.VMEM((UNROLL, 8, SPAN), F32),
         ],
         compiler_params=pltpu.CompilerParams(vmem_limit_bytes=VMEM_LIMIT),
         cost_estimate=cost(65.0),
@@ -349,7 +369,7 @@
                q_ref, dc_ref, ctx_ref, k_ref, v_ref, kg_ref, vg_ref, coords_ref, rq_ref, rk_ref,
                pn_ref, pf_ref, g0_ref, g1_ref,
                dq_ref, dk_ref, dv_ref, dkg_ref, dvg_ref, vec_ref,
-               dx_ref, dy_ref, dp_ref, dpf_ref, ds_ref, dsf_ref, a_ref, b_ref, dqr_ref, db_ref,
+               dx_ref, dy_ref, dp_ref, dpf_ref, ds_ref, dsf_ref, a_ref, b_ref, dqr_ref, db_ref, db_now,
                *, pairs, first_pair, tiles, per_block, edge):
     step = pl.program_id(0)
     t = step * (tiles - 1) if edge else step + 1
@@ -374,8 +394,6 @@
 
     geometry_into(coords_ref, offset_ref[0, 0] // 128 + t - 1, None, (None, None, dx_ref, dy_ref))
     lo16, hi16 = half_masks(BF16)
-    lane = lax.broadcasted_iota(jnp.int32, (CH, 128), 1)
-    low = lane < 64
     low64 = lax.broadcasted_iota(jnp.int32, (64, 128), 1) < 64
     lane8 = lax.broadcasted_iota(jnp.int32, (4, 128), 1)
     lane1 = lax.broadcasted_iota(jnp.int32, (1, 128), 1)
@@ -407,66 +425,72 @@
         vec_ref[p, 8:9, :] += line
         return extra
 
-    def one_pair(p, carry):
+    low_rows = lax.broadcasted_iota(jnp.int32, (BACK_CH, 128), 1) < 64
+
+    def fold(full):
+        return jnp.sum(full.reshape(full.shape[0] // 8, 8, full.shape[1]), axis=0)
+
+    def pair_parts(p):
         cols = pl.ds(pl.multiple_of(p * 128, 128), 128)
         head = 2 * (p + first_pair)
+        squares = [[theta_ref[i, head + e] * theta_ref[i, head + e] for i in range(2)] for e in range(2)]
+        halves = [jnp.where(lane1 < 64, squares[0][i], squares[1][i]) for i in range(2)]
+        return cols, head, halves
+
+    def products(p, slot):
+        cols, head, _ = pair_parts(p)
         qp = q_ref[:, cols]
         dcp = dc_ref[:, cols]
         kp = k_ref[rows, cols]
-        vp = v_ref[rows, cols]
-        kgp = kg_ref[0, :, cols]
         vgp = vg_ref[0, :, cols]
-        kg2 = jnp.concatenate([kgp * lo16, kgp * hi16], axis=0)
-        vg2 = jnp.concatenate([vgp * lo16, vgp * hi16], axis=0)
-        dp_ref[...] = mm_nt(jnp.concatenate([dcp * lo16, dcp * hi16], axis=0), vp)
-        dpf_ref[...] = mm_nt(dcp, vg2)
+        dp_ref[slot] = mm_nt(jnp.concatenate([dcp * lo16, dcp * hi16], axis=0), v_ref[rows, cols])
+        dpf_ref[slot] = mm_nt(dcp, jnp.concatenate([vgp * lo16, vgp * hi16], axis=0))
         biases = by_row([bias_ref[c, head + e] for e in range(2) for c in range(4)])
         a, b = rich_sums(qp, kp, rq_ref[:, cols], rk_ref[:, cols], None, biases)
-        a_ref[...] = a
-        b_ref[...] = b
-        squares = [[theta_ref[i, head + e] * theta_ref[i, head + e] for i in range(2)] for e in range(2)]
-        halves = [jnp.where(lane1 < 64, squares[0][i], squares[1][i]) for i in range(2)]
+        a_ref[slot] = a
+        b_ref[slot] = b
+
+    def elements(p, slot):
+        cols, head, halves = pair_parts(p)
         lines = [rq_ref[0:1, cols], rq_ref[1:2, cols], rq_ref[2:3, cols] * halves[0], rq_ref[3:4, cols] * halves[1]]
         col_sums = [[jnp.zeros((8, SPAN), F32) for _ in range(4)] for _ in range(2)]
         thetas = [[jnp.zeros((8, 128), F32) for _ in range(2)] for _ in range(2)]
         query_sums = [jnp.zeros((8, 128), F32) for _ in range(4)]
-        for r in range(0, TILE, CH):
-            rs = slice(r, r + CH)
+        for r in range(0, TILE, BACK_CH):
+            rs = slice(r, r + BACK_CH)
             prod = dc_ref[rs, cols].astype(F32) * ctx_ref[rs, cols].astype(F32)
             row_sums = []
             dots = []
             for e in range(2):
-                here = low if e == 0 else ~low
+                here = low_rows if e == 0 else ~low_rows
                 base = 4 * e
                 dot = jnp.sum(jnp.where(here, prod, 0.0), axis=1, keepdims=True)
                 dots.append(dot)
-                es = slice(e * TILE + r, e * TILE + r + CH)
-                ds = pn_ref[0, 2 * p + e, rs, :].astype(F32) * (dp_ref[es, :] - dot)
-                ds_ref[es, :] = ds.astype(BF16)
+                es = slice(e * TILE + r, e * TILE + r + BACK_CH)
+                ds = pn_ref[0, 2 * p + e, rs, :].astype(F32) * (dp_ref[slot, es, :] - dot)
+                ds_ref[slot, es, :] = ds.astype(BF16)
                 t0 = ds * g0_ref[0, 2 * p + e, rs, :].astype(F32)
                 t1 = ds * g1_ref[0, 2 * p + e, rs, :].astype(F32)
-                gx = (dx_ref[rs, :] - a_ref[rs, base + 2 : base + 3]) - b_ref[base + 2 : base + 3, :]
-                gy = (dy_ref[rs, :] - a_ref[rs, base + 3 : base + 4]) - b_ref[base + 3 : base + 4, :]
+                gx = (dx_ref[rs, :] - a_ref[slot, rs, base + 2 : base + 3]) - b_ref[slot, base + 2 : base + 3, :]
+                gy = (dy_ref[rs, :] - a_ref[slot, rs, base + 3 : base + 4]) - b_ref[slot, base + 3 : base + 4, :]
                 tx = ds * gx
                 ty = ds * gy
                 for i, full in enumerate((tx * gx, ty * gy)):
-                    part = full[:, 0:128] + full[:, 128:256] + full[:, 256:384]
-                    thetas[e][i] = thetas[e][i] + (part[0:8] + part[8:16])
+                    thetas[e][i] = thetas[e][i] + fold(full[:, 0:128] + full[:, 128:256] + full[:, 256:384])
                 sums = []
                 for c, full in enumerate((t0, t1, tx, ty)):
-                    col_sums[e][c] = col_sums[e][c] + (full[0:8] + full[8:16])
+                    col_sums[e][c] = col_sums[e][c] + fold(full)
                     sums.append(jnp.sum(full[:, 0:128] + full[:, 128:256] + full[:, 256:384], axis=1, keepdims=True))
                 row_sums.append(sums)
-            dsf = pf_ref[0, p, rs, :].astype(F32) * (dpf_ref[rs, :] - jnp.where(low, dots[0], dots[1]))
-            dsf_ref[rs, :] = dsf.astype(BF16)
+            dsf = pf_ref[0, p, rs, :].astype(F32) * (dpf_ref[slot, rs, :] - jnp.where(low_rows, dots[0], dots[1]))
+            dsf_ref[slot, rs, :] = dsf.astype(BF16)
             qf = q_ref[rs, cols].astype(F32)
-            dqr = jnp.zeros((CH, 128), F32)
+            dqr = jnp.zeros((BACK_CH, 128), F32)
             for c in range(4):
-                da = jnp.where(low, row_sums[0][c], row_sums[1][c])
+                da = jnp.where(low_rows, row_sums[0][c], row_sums[1][c])
                 dqr = dqr + da * lines[c]
-                part = da * qf
-                query_sums[c] = query_sums[c] + (part[0:8] + part[8:16])
-            dqr_ref[rs, :] = dqr
+                query_sums[c] = query_sums[c] + fold(da * qf)
+            dqr_ref[slot, rs, :] = dqr
         folded = jnp.concatenate([jnp.sum(query_sums[c], axis=0, keepdims=True) for c in range(4)], axis=0)
         scale4 = jnp.concatenate([jnp.ones((2, 128), F32), halves[0], halves[1]], axis=0)
         vec_ref[p, 0:4, :] += folded * scale4
@@ -476,12 +500,21 @@
                 total = jnp.sum(jnp.sum(thetas[e][i], axis=0, keepdims=True), axis=1, keepdims=True)
                 line = jnp.where(lane1 == 8 + 2 * e + i, total * (-theta_ref[i, head + e]), line)
         vec_ref[p, 8:9, :] += line
-        packed = jnp.concatenate([jnp.sum(col_sums[e][c], axis=0, keepdims=True) for e in range(2) for c in range(4)], axis=0)
-        dq = mm(ds_ref[0:TILE, :], kp * lo16) + mm(ds_ref[TILE : 2 * TILE, :], kp * hi16) + mm(dsf_ref[...], kg2)
-        dq_ref[:, cols] = (dq * 0.125 + dqr_ref[...]).astype(BF16)
+        db_now[slot] = jnp.concatenate([jnp.sum(col_sums[e][c], axis=0, keepdims=True) for e in range(2) for c in range(4)], axis=0)
+
+    def results(p, slot):
+        cols, head, _ = pair_parts(p)
+        qp = q_ref[:, cols]
+        dcp = dc_ref[:, cols]
+        kp = k_ref[rows, cols]
+        kgp = kg_ref[0, :, cols]
+        packed = db_now[slot]
+        dq = mm(ds_ref[slot, 0:TILE, :], kp * lo16) + mm(ds_ref[slot, TILE : 2 * TILE, :], kp * hi16)
+        dq = dq + mm(dsf_ref[slot], jnp.concatenate([kgp * lo16, kgp * hi16], axis=0))
+        dq_ref[:, cols] = (dq * 0.125 + dqr_ref[slot]).astype(BF16)
         qT = jnp.transpose(qp)
         dcT = jnp.transpose(dcp)
-        dk = mm(jnp.concatenate([qT * lo16c, qT * hi16c], axis=1), ds_ref[...]) * 0.125
+        dk = mm(jnp.concatenate([qT * lo16c, qT * hi16c], axis=1), ds_ref[slot]) * 0.125
         dv = mm(dcT * lo16c, pn_ref[0, 2 * p]) + mm(dcT * hi16c, pn_ref[0, 2 * p + 1])
         if edge:
             dk_ref[0, cols, :] = dk + rich_key_parts(p, cols, packed, kp, rows)
@@ -490,13 +523,19 @@
             dk_ref[cols, out_rows] += dk
             dv_ref[cols, out_rows] += dv
             db_ref[p, :, out_rows] += packed
-        dkg2 = mm(jnp.transpose(dsf_ref[...]), qp) * 0.125
+        dkg2 = mm(jnp.transpose(dsf_ref[slot]), qp) * 0.125
         dvg2 = mm(jnp.transpose(pf_ref[0, p]), dcp)
         dkg_ref[0, :, cols] += jnp.where(low64, dkg2[0:64], dkg2[64:128])
         dvg_ref[0, :, cols] += jnp.where(low64, dvg2[0:64], dvg2[64:128])
+
+    def group(index, carry):
+        first = index * BACK_UNROLL
+        for stage in (products, elements, results):
+            for u in range(BACK_UNROLL):
+                stage(first + u, u)
         return carry
 
-    lax.fori_loop(0, pairs, one_pair, 0)
+    lax.fori_loop(0, pairs // BACK_UNROLL, group, 0)
 
     if not edge:
 
@@ -563,10 +602,11 @@
         ],
         scratch_shapes=[
             pltpu.VMEM((TILE, SPAN), F32), pltpu.VMEM((TILE, SPAN), F32),
-            pltpu.VMEM((2 * TILE, SPAN), F32), pltpu.VMEM((TILE, 128), F32),
-            pltpu.VMEM((2 * TILE, SPAN), BF16), pltpu.VMEM((TILE, 128), BF16),
-            pltpu.VMEM((TILE, 8), F32), pltpu.VMEM((8, SPAN), F32),
-            pltpu.VMEM((TILE, 128), F32), pltpu.VMEM((pairs, 8, rows), F32),
+            pltpu.VMEM((BACK_UNROLL, 2 * TILE, SPAN), F32), pltpu.VMEM((BACK_UNROLL, TILE, 128), F32),
+            pltpu.VMEM((BACK_UNROLL, 2 * TILE, SPAN), BF16), pltpu.VMEM((BACK_UNROLL, TILE, 128), BF16),
+            pltpu.VMEM((BACK_UNROLL, TILE, 8), F32), pltpu.VMEM((BACK_UNROLL, 8, SPAN), F32),
+            pltpu.VMEM((BACK_UNROLL, TILE, 128), F32), pltpu.VMEM((pairs, 8, rows), F32),
+            pltpu.VMEM((BACK_UNROLL, 8, SPAN), F32),
         ],
         compiler_params=pltpu.CompilerParams(vmem_limit_bytes=VMEM_LIMIT),
         cost_estimate=cost(8.2 * steps * pairs / 6),
@@ -574,22 +614,23 @@
     )(offset, rich_bias, rich_theta, q, dctx, ctx, k_pad, v_pad, kg, vg, coords, rich_query, rich_key, *kept)
 
 
-FF_CHUNK = 384
+FF_CHUNK = 512
 ROW_CHUNK = 256
 
-def normal_tail(values):
-    z = jnp.abs(values) * math.sqrt(0.5)
-    t = 1.0 / (1.0 + 0.5 * z)
-    poly = jnp.full_like(t, 0.17087277)
-    for coef in (-0.82215223, 1.48851587, -1.13520398, 0.27886807, -0.18628806, 0.09678418, 0.37409196, 1.00002368, -1.26551223):
+TAIL_SLOPE = 0.35
+TAIL = (0.0987331438, 0.0987265523, 0.092954664, 0.0773361877, 0.0814717893, -0.00727472285, 0.100604539, -0.0425525649)
+
+
+def gelu_pair(values):
+    t = 1.0 / (1.0 + (TAIL_SLOPE * math.sqrt(0.5)) * jnp.abs(values))
+    poly = TAIL[-1] * t + TAIL[-2]
+    for coef in TAIL[-3::-1]:
         poly = poly * t + coef
-    return 0.5 * t * jnp.exp(poly - z * z)
-
-def gelu_pair(values):
-    tail = normal_tail(values)
+    bell = jnp.exp2((values * values) * (-0.5 * LOG2E))
+    tail = t * poly * bell
     phi = jnp.where(values >= 0.0, 1.0 - tail, tail)
-    density = jnp.exp(-0.5 * values * values) * (1.0 / math.sqrt(2.0 * math.pi))
-    return values * phi, phi + values * density
+    return values * phi, phi + (values * bell) * (1.0 / math.sqrt(2.0 * math.pi))
+
 
 def ffn_kernel(tok_ref, ctx_ref, ct_ref, wo_ref, wu_ref, wd_ref, norms_ref,
                out_ref, dmid_ref, dctx_ref, wog_ref, wug_ref, wdg_ref, vec_ref,
@@ -610,15 +651,26 @@
             acc_ref[rs, :] = jnp.zeros_like(mid)
             dh_ref[rs, :] = jnp.zeros_like(mid)
 
-    for r in range(0, rows, ROW_CHUNK):
-        rs = slice(r, r + ROW_CHUNK)
-        pre = mm(h2_ref[rs, :], wu_ref[...])
-        dact = mm_nt(ct_ref[rs, :], wd_ref[...])
+    def second(rs):
+        acc_ref[rs, :] += mm(act_ref[rs, :], wd_ref[...])
+        dh_ref[rs, :] += mm_nt(dpre_ref[rs, :], wu_ref[...])
+
+    spans = [slice(r, r + ROW_CHUNK) for r in range(0, rows, ROW_CHUNK)]
+
+    def first(rs):
+        return mm(h2_ref[rs, :], wu_ref[...]), mm_nt(ct_ref[rs, :], wd_ref[...])
+
+    ahead = first(spans[0])
+    for index, rs in enumerate(spans):
+        pre, dact = ahead
+        if index + 1 < len(spans):
+            ahead = first(spans[index + 1])
         act, slope = gelu_pair(pre)
         act_ref[rs, :] = act.astype(BF16)
         dpre_ref[rs, :] = (dact * slope).astype(BF16)
-        acc_ref[rs, :] += mm(act_ref[rs, :], wd_ref[...])
-        dh_ref[rs, :] += mm_nt(dpre_ref[rs, :], wu_ref[...])
+        if index > 0:
+            second(spans[index - 1])
+    second(spans[-1])
     wug_ref[...] = mm(h2t_ref[...], dpre_ref[...]).astype(BF16)
     wdg_ref[...] = mm_tn(act_ref[...], ct_ref[...]).astype(BF16)
 

time: 407 us -> 377 us (0.926)
  Pallas kernels: 261 us -> 211 us
  waiting for transfers between devices: 38.2 us -> 58.4 us
    pallas_call x3, Pallas kernels: 82.6 us -> 54.9 us  [attn_backward(): pl.pallas_call(partial(bwd_kernel, pairs=pairs, first_pair=first_pair, ti...]
    pallas_call x1, Pallas kernels: 75.1 us -> 53.8 us  [attn_forward(): pl.pallas_call(partial(fwd_kernel, pairs=pairs, per_block=per_block), gri...]
    ppermute x4, waiting for transfers between devices: 1.1 us -> 9.91 us  [halve_step(): return add_low(kept, lax.ppermute(send, axis, swap_on(axis, 1 << bit)))]
    ppermute x18, waiting for transfers between devices: 31.1 us -> 39.9 us  [exchange_sum(): lax.ppermute(send, axis, swap_on(axis, step * stride)).astype(F32)]
  transfers between devices with their start and end apart: 45 -> 45, of which waited for: 18 -> 21; matrix products, arithmetic and copies ran while one was open for 7% -> 7% of each run, Pallas kernels for 31% -> 26%
where the time goes in v3:
time: 377 us; the launch traced here: 370 us
  Pallas kernels  211 us (56%)
  waiting for transfers between devices  58.4 us (15%)
  starting transfers between devices  55.3 us (15%)
  local copies, waits for them, and re-layouts  24.1 us (6%)
  other arithmetic  19.2 us (5%)
    pallas_call x1, Pallas kernels, feed_forward(): pl.pallas_call(partial(ffn_kernel, rows=rows), grid=(steps,), in_specs=[w...  61.5 us
    pallas_call x3, Pallas kernels, attn_backward(): pl.pallas_call(partial(bwd_kernel, pairs=pairs, first_pair=first_pair, ti...  54.9 us
    pallas_call x1, Pallas kernels, attn_forward(): pl.pallas_call(partial(fwd_kernel, pairs=pairs, per_block=per_block), gri...  53.8 us
    ppermute x18, waiting for transfers between devices, exchange_sum(): lax.ppermute(send, axis, swap_on(axis, step * stride)).astype(F32)  39.9 us
    pallas_call x2, Pallas kernels, qkv_backward(): pl.pallas_call(partial(qkv_back_kernel, half=half, final=final, pairs=pai...  32.5 us
    ppermute x18, starting transfers between devices, exchange_sum(): lax.ppermute(send, axis, swap_on(axis, step * stride)).astype(F32)  23.8 us
    ppermute x9, starting transfers between devices, exchange_all(): lax.ppermute(piece, axis, swap_on(axis, step))  10.7 us
    convert_element_type x10, other arithmetic, add_low(): return (kept.astype(F32) + received.astype(F32)).astype(BF16)  10.3 us
  transfers between devices with their start and end apart: 45, of which 21 were waited for; matrix products, arithmetic and copies ran while one was open for 7% of the time, Pallas kernels for 26%

profile of v3, /device:TPU:0, one launch (start us, length us, event | category | flops | bytes accessed | tf_op | source)
XLA Modules:
  0.0 369.8 jit_solution(15173807492803877334)
XLA Ops:
  3.5 3.0 collective-permute-start.1
  11.7 4.7 %collective-permute-start.5 = (bf16[64,768]{1,0:T(8,128)(2,1)S(1)}, bf16[64,768]{1,0:T(8,128)(2,1)S(1)}, u32[]{:S(2)}, u32[]{:S(2)}) collective-permute-start(bf16[64,768]{1,0:T(8,128)(2,1)S(1)} %pad_maximum_fusion.9), channel_id=1, source_target_pairs={{0,6},{1,7},{2,4},{3,5},{4,2},{5,3},{6,0},{7,1},{8,14},{9,15},{10,... | collective-permute-start | bytes 294920 | tf_op jit(solution)/shard_map/ppermute | solution.py:938
  17.1 8.2 %project_tokens.1 = (bf16[1024,768]{1,0:T(8,128)(2,1)}, bf16[1024,768]{1,0:T(8,128)(2,1)}, bf16[1024,768]{1,0:T(8,128)(2,1)}, bf16[768,1024]{1,0:T(8,128)(2,1)}) custom-call(bf16[1024,768]{1,0:T(8,128)(2,1)} %bitcast.249, bf16[768,2304]{1,0:T(8,128)(2,1)} %refs_2_.3, f32[4,768]{1,0:T(4,128)} %pad_maximum_fusion.10.norms_ref.refs_19_), custom_call_target="tpu_custom_call" | custom-call | flops 8000000000 | tf_op jit(solution)/shard_map/project_tokens/pallas_call | solution.py:152
  26.3 53.8 %attn_forward.1 = (bf16[1024,768]{1,0:T(8,128)(2,1)}, bf16[8,12,128,384]{3,2,1,0:T(8,128)(2,1)}, bf16[8,6,128,128]{3,2,1,0:T(8,128)(2,1)}, bf16[8,12,128,384]{3,...) custom-call(s32[1,4]{1,0:T(1,128)} %units_ref.1, ...), custom_call_target="tpu_custom_call" | custom-call | flops 65000001536 | tf_op jit(solution)/shard_map/attn_forward/pallas_call | solution.py:321
  80.1 61.5 %feed_forward.1 = (bf16[1024,768]{1,0:T(8,128)(2,1)}, f32[1024,768]{1,0:T(8,128)}, bf16[1024,768]{1,0:T(8,128)(2,1)}, bf16[768,768]{1,0:T(8,128)(2,1)}, bf16[768...) custom-call(bf16[1024,768]{1,0:T(8,128)(2,1)} %bitcast.250, ...), custom_call_target="tpu_custom_call" | custom-call | flops 60000002048 | tf_op jit(solution)/shard_map/feed_forward/pallas_call | solution.py:703
  142.7 3.4 dynamic-slice_bitcast_fusion.1
  148.9 15.8 %attn_backward_edge.1 = (bf16[256,768]{1,0:T(8,128)(2,1)}, f32[2,768,384]{2,1,0:T(8,128)}, f32[2,768,384]{2,1,0:T(8,128)}, f32[2,64,768]{2,1,0:T(8,128)}, f32[2,64,768]{2,1,0:T(8,128)}, /*index=5*/f32[6,16,128]{2,1,0:T(8,128)}) custom-call(s32[1,1]{1,0:T(1,128)} %bitcast.1.offset_ref, f32[4,12]{1,0:T(4,128)} %bias_ref.7, f32[2,12]{1,0:T(2,128)} %theta_ref.7, ...), custom_call_target="tpu_custom_call" | custom-call | flops 16400000000 | tf_op jit(solution)/shard_map/attn_backward_edge/pallas_call | solution.py:584
  167.5 2.3 collective-permute-start.9
  172.4 2.2 fusion
  174.6 2.6 fusion.1
  180.1 2.0 collective-permute-start.12
  184.8 19.4 %attn_backward_mid.2 = (bf16[768,384]{1,0:T(8,128)(2,1)}, f32[384,1024]{1,0:T(8,128)}, f32[384,1024]{1,0:T(8,128)}, f32[2,64,384]{2,1,0:T(8,128)}, f32[2,64,384]{2,1,0:T(8,128)}, /*index=5*/f32[3,16,128]{2,1,0:T(8,128)}) custom-call(s32[1,1]{1,0:T(1,128)} %bitcast.1.offset_ref, f32[4,12]{1,0:T(4,128)} %bias_ref.7, f32[2,12]{1,0:T(2,128)} %theta_ref.7, ...), custom_call_target="tpu_custom_call" | custom-call | flops 24600000512 | tf_op jit(solution)/shard_map/attn_backward_mid/pallas_call | solution.py:584
  204.3 7.4 %collective-permute-done.12 = bf16[2,4,216,384]{3,2,0,1:T(8,128)(2,1)} collective-permute-done((bf16[2,4,216,384]{3,2,0,1:T(8,128)(2,1)}, bf16[2,4,216,384]{3,2,0,1:T(8,128)(2,1)}, u32[]{:S(2)}, u32[]{:S(2)}) %collective-permute-start.12) | collective-permute-done | bytes 1327136 | tf_op jit(solution)/shard_map/ppermute | solution.py:912
  213.3 2.2 collective-permute-done.11
  219.7 13.9 %qkv_backward.2 = (bf16[768,1152]{1,0:T(8,128)(2,1)}, f32[1024,768]{1,0:T(8,128)}, f32[128,768]{1,0:T(8,128)}) custom-call(bf16[768,1024]{1,0:T(8,128)(2,1)} %get-tuple-element.102.refs_0_, bf16[2,64,768]{2,1,0:T(8,128)(2,1)} %get-tuple-element.103.refs_1_, bf16[768,2304]{1,0:T(8,128)(2,1)} %refs_2_.3, bf16[256,768]{1,0:T(8,128)(2,1)} %get-tuple-element.121.refs_3_, ...), custom_call_target="tpu_custom_call" | custom-call | flops 8000000000 | tf_op jit(solution)/shard_map/qkv_backward/pallas_call | solution.py:870
  237.7 2.4 collective-permute-start.16
  240.1 2.6 collective-permute-start.18
  242.7 19.7 %attn_backward_mid.3 = (bf16[768,384]{1,0:T(8,128)(2,1)}, f32[384,1024]{1,0:T(8,128)}, f32[384,1024]{1,0:T(8,128)}, f32[2,64,384]{2,1,0:T(8,128)}, f32[2,64,384]{2,1,0:T(8,128)}, /*index=5*/f32[3,16,128]{2,1,0:T(8,128)}) custom-call(s32[1,1]{1,0:T(1,128)} %bitcast.1.offset_ref, f32[4,12]{1,0:T(4,128)} %bias_ref.7, f32[2,12]{1,0:T(2,128)} %theta_ref.7, ...), custom_call_target="tpu_custom_call" | custom-call | flops 24600000512 | tf_op jit(solution)/shard_map/attn_backward_mid/pallas_call | solution.py:584
  262.4 8.9 %collective-permute-done.17 = bf16[216,768]{1,0:T(8,128)(2,1)S(1)} collective-permute-done((bf16[216,768]{1,0:T(8,128)(2,1)S(1)}, bf16[216,768]{1,0:T(8,128)(2,1)S(1)}, u32[]{:S(2)}, u32[]{:S(2)}) %collective-permute-start.17) | collective-permute-done | bytes 331808 | tf_op jit(solution)/shard_map/ppermute | solution.py:920
  273.5 18.7 %qkv_backward.3 = (bf16[768,1152]{1,0:T(8,128)(2,1)}, bf16[768,128]{1,0:T(8,128)(2,1)}, bf16[1024,768]{1,0:T(8,128)(2,1)}, bf16[256,768]{1,0:T(8,128)(2,1)}) custom-call(bf16[768,1024]{1,0:T(8,128)(2,1)} %get-tuple-element.102.refs_0_, bf16[2,64,768]{2,1,0:T(8,128)(2,1)} %get-tuple-element.103.refs_1_, bf16[768,2304]{1,0:T(8,128)(2,1)} %refs_2_.3, ...), custom_call_target="tpu_custom_call" | custom-call | flops 15000000512 | tf_op jit(solution)/shard_map/qkv_backward/pallas_call | solution.py:870
  297.0 4.6 %collective-permute-done.26 = bf16[4,24,1152]{2,1,0:T(8,128)(2,1)S(1)} collective-permute-done((bf16[4,24,1152]{2,1,0:T(8,128)(2,1)S(1)}, bf16[4,24,1152]{2,1,0:T(8,128)(2,1)S(1)}, u32[]{:S(2)}, u32[]{:S(2)}) %collective-permute-start.26) | collective-permute-done | bytes 221216 | tf_op jit(solution)/shard_map/ppermute | solution.py:920
  301.7 4.7 %collective-permute-done.28 = bf16[4,24,1152]{2,1,0:T(8,128)(2,1)S(1)} collective-permute-done((bf16[4,24,1152]{2,1,0:T(8,128)(2,1)S(1)}, bf16[4,24,1152]{2,1,0:T(8,128)(2,1)S(1)}, u32[]{:S(2)}, u32[]{:S(2)}) %collective-permute-start.28) | collective-permute-done | bytes 221216 | tf_op jit(solution)/shard_map/ppermute | solution.py:920
  306.3 2.6 collective-permute-start.22
  309.1 2.0 collective-permute-start.29
  312.3 3.0 collective-permute-start.31
  318.3 2.1 collective-permute-done.30
  320.4 3.4 collective-permute-done.23
  324.5 2.2 collective-permute-start.34
  335.7 5.2 %collective-permute-done.36 = bf16[4,24,1280]{2,1,0:T(8,128)(2,1)S(1)} collective-permute-done((bf16[4,24,1280]{2,1,0:T(8,128)(2,1)S(1)}, bf16[4,24,1280]{2,1,0:T(8,128)(2,1)S(1)}, u32[]{:S(2)}, u32[]{:S(2)}) %collective-permute-start.36) | collective-permute-done | bytes 245792 | tf_op jit(solution)/shard_map/ppermute | solution.py:920
  340.9 5.6 %collective-permute-done.38 = bf16[4,24,1280]{2,1,0:T(8,128)(2,1)S(1)} collective-permute-done((bf16[4,24,1280]{2,1,0:T(8,128)(2,1)S(1)}, bf16[4,24,1280]{2,1,0:T(8,128)(2,1)S(1)}, u32[]{:S(2)}, u32[]{:S(2)}) %collective-permute-start.38) | collective-permute-done | bytes 245792 | tf_op jit(solution)/shard_map/ppermute | solution.py:920
  348.0 2.3 collective-permute-start.39
  352.7 3.6 collective-permute-done.41
  (199 shorter events, 72.1 us)
Async XLA Ops:
  0.6 10.2 %collective-permute-start = (bf16[32,768]{1,0:T(8,128)(2,1)}, bf16[32,768]{1,0:T(8,128)(2,1)S(1)}, u32[]{:S(2)}, u32[]{:S(2)}) collective-permute-start(bf16[32,768]{1,0:T(8,128)(2,1)} %bitcast.229), channel_id=1, source_target_pairs={{0,1},{1,0},{2,3},{3,2},{4,5},{5,4},{6,7},{7,6},{8,9},{9,8},{10,11... | collective-permute-start | bytes 147464 | tf_op jit(solution)/shard_map/ppermute | solution.py:931
  2.2 9.5 %collective-permute-start.2 = (bf16[128,768]{1,0:T(8,128)(2,1)S(1)}, bf16[128,768]{1,0:T(8,128)(2,1)S(1)}, u32[]{:S(2)}, u32[]{:S(2)}) collective-permute-start(bf16[128,768]{1,0:T(8,128)(2,1)S(1)} %get-tuple-element.210), channel_id=1, source_target_pairs={{1,0},{2,1},{3,2},{4,3},{5,4},{6,5},{7,6},{9,8},{10,9},{11,10},{12... | collective-permute-start | bytes 589832 | tf_op jit(solution)/shard_map/ppermute | solution.py:994
  3.5 8.2 %collective-permute-start.1 = (bf16[128,768]{1,0:T(8,128)(2,1)S(1)}, bf16[128,768]{1,0:T(8,128)(2,1)S(1)}, u32[]{:S(2)}, u32[]{:S(2)}) collective-permute-start(bf16[128,768]{1,0:T(8,128)(2,1)S(1)} %get-tuple-element.211), channel_id=1, source_target_pairs={{0,1},{1,2},{2,3},{3,4},{4,5},{5,6},{6,7},{8,9},{9,10},{10,11},{11... | collective-permute-start | bytes 589832 | tf_op jit(solution)/shard_map/ppermute | solution.py:993
  11.7 13.5 %collective-permute-start.5 = (bf16[64,768]{1,0:T(8,128)(2,1)S(1)}, bf16[64,768]{1,0:T(8,128)(2,1)S(1)}, u32[]{:S(2)}, u32[]{:S(2)}) collective-permute-start(bf16[64,768]{1,0:T(8,128)(2,1)S(1)} %pad_maximum_fusion.9), channel_id=1, source_target_pairs={{0,6},{1,7},{2,4},{3,5},{4,2},{5,3},{6,0},{7,1},{8,14},{9,15},{10,... | collective-permute-start | bytes 294920 | tf_op jit(solution)/shard_map/ppermute | solution.py:938
  16.5 8.8 %collective-permute-start.4 = (bf16[64,768]{1,0:T(8,128)(2,1)S(1)}, bf16[64,768]{1,0:T(8,128)(2,1)S(1)}, u32[]{:S(2)}, u32[]{:S(2)}) collective-permute-start(bf16[64,768]{1,0:T(8,128)(2,1)S(1)} %pad_maximum_fusion.9), channel_id=1, source_target_pairs={{0,4},{1,5},{2,6},{3,7},{4,0},{5,1},{6,2},{7,3},{8,12},{9,13},{10,... | collective-permute-start | bytes 294920 | tf_op jit(solution)/shard_map/ppermute | solution.py:938
  16.5 8.8 %collective-permute-start.3 = (bf16[64,768]{1,0:T(8,128)(2,1)S(1)}, bf16[64,768]{1,0:T(8,128)(2,1)S(1)}, u32[]{:S(2)}, u32[]{:S(2)}) collective-permute-start(bf16[64,768]{1,0:T(8,128)(2,1)S(1)} %pad_maximum_fusion.9), channel_id=1, source_target_pairs={{0,2},{1,3},{2,0},{3,1},{4,6},{5,7},{6,4},{7,5},{8,10},{9,11},{10,... | collective-permute-start | bytes 294920 | tf_op jit(solution)/shard_map/ppermute | solution.py:938
  147.7 23.3 %collective-permute-start.6 = (bf16[4,96,3072]{2,1,0:T(8,128)(2,1)}, bf16[4,96,3072]{2,1,0:T(8,128)(2,1)}, u32[]{:S(2)}, u32[]{:S(2)}) collective-permute-start(bf16[4,96,3072]{2,1,0:T(8,128)(2,1)} %dynamic-slice_bitcast_fusion.1), channel_id=1, source_target_pairs={{0,1},{1,0},{2,3},{3,2},{4,5},{5,4},{6,7},{7,6},{8,9},{9,8},{10,11... | collective-permute-start | bytes 7077896 | tf_op jit(solution)/shard_map/ppermute | solution.py:900
  148.2 22.9 %collective-permute-start.7 = (bf16[4,384,768]{2,1,0:T(8,128)(2,1)}, bf16[4,384,768]{2,1,0:T(8,128)(2,1)}, u32[]{:S(2)}, u32[]{:S(2)}) collective-permute-start(bf16[4,384,768]{2,1,0:T(8,128)(2,1)} %dynamic-slice_bitcast_fusion), channel_id=1, source_target_pairs={{0,1},{1,0},{2,3},{3,2},{4,5},{5,4},{6,7},{7,6},{8,9},{9,8},{10,11... | collective-permute-start | bytes 7077896 | tf_op jit(solution)/shard_map/ppermute | solution.py:900
  148.4 22.6 %collective-permute-start.8 = (bf16[4,96,768]{2,1,0:T(8,128)(2,1)S(1)}, bf16[4,96,768]{2,1,0:T(8,128)(2,1)}, u32[]{:S(2)}, u32[]{:S(2)}) collective-permute-start(bf16[4,96,768]{2,1,0:T(8,128)(2,1)S(1)} %dynamic-slice_bitcast_fusion.8), channel_id=1, source_target_pairs={{0,1},{1,0},{2,3},{3,2},{4,5},{5,4},{6,7},{7,6},{8,9},{9,8},{10,11... | collective-permute-start | bytes 1769480 | tf_op jit(solution)/shard_map/ppermute | solution.py:900
  167.5 11.3 %collective-permute-start.9 = (bf16[2,768,128]{2,1,0:T(8,128)(2,1)S(1)}, bf16[2,768,128]{2,1,0:T(8,128)(2,1)S(1)}, u32[]{:S(2)}, u32[]{:S(2)}) collective-permute-start(bf16[2,768,128]{2,1,0:T(8,128)(2,1)S(1)} %pad_maximum_fusion.5), channel_id=1, source_target_pairs={{0,1},{1,2},{2,3},{3,4},{4,5},{5,6},{6,7},{8,9},{9,10},{10,11},{11... | collective-permute-start | bytes 1179656 | tf_op jit(solution)/shard_map/ppermute | solution.py:1020
  169.8 9.0 %collective-permute-start.10 = (bf16[2,768,128]{2,1,0:T(8,128)(2,1)S(1)}, bf16[2,768,128]{2,1,0:T(8,128)(2,1)S(1)}, u32[]{:S(2)}, u32[]{:S(2)}) collective-permute-start(bf16[2,768,128]{2,1,0:T(8,128)(2,1)S(1)} %pad_maximum_fusion.6), channel_id=1, source_target_pairs={{1,0},{2,1},{3,2},{4,3},{5,4},{6,5},{7,6},{9,8},{10,9},{11,10},{12... | collective-permute-start | bytes 1179656 | tf_op jit(solution)/shard_map/ppermute | solution.py:1020
  180.1 31.6 %collective-permute-start.12 = (bf16[2,4,216,384]{3,2,0,1:T(8,128)(2,1)}, bf16[2,4,216,384]{3,2,0,1:T(8,128)(2,1)}, u32[]{:S(2)}, u32[]{:S(2)}) collective-permute-start(bf16[2,4,216,384]{3,2,0,1:T(8,128)(2,1)} %dynamic-slice_bitcast_fusion.2), channel_id=1, source_target_pairs={{0,16},{8,24},{16,0},{24,8},{1,17},{9,25},{17,1},{25,9},{2,18},{10... | collective-permute-start | bytes 3981320 | tf_op jit(solution)/shard_map/ppermute | solution.py:912
  183.3 32.2 %collective-permute-start.11 = (bf16[2,4,216,384]{3,2,1,0:T(8,128)(2,1)}, bf16[2,4,216,384]{3,2,1,0:T(8,128)(2,1)}, u32[]{:S(2)}, u32[]{:S(2)}) collective-permute-start(bf16[2,4,216,384]{3,2,1,0:T(8,128)(2,1)} %dynamic-slice_bitcast_fusion.3), channel_id=1, source_target_pairs={{0,8},{8,0},{16,24},{24,16},{1,9},{9,1},{17,25},{25,17},{2,10},{10... | collective-permute-start | bytes 3981320 | tf_op jit(solution)/shard_map/ppermute | solution.py:912
  217.4 17.6 %collective-permute-start.14 = (bf16[4,216,384]{2,1,0:T(8,128)(2,1)S(1)}, bf16[4,216,384]{2,1,0:T(8,128)(2,1)S(1)}, u32[]{:S(2)}, u32[]{:S(2)}) collective-permute-start(bf16[4,216,384]{2,1,0:T(8,128)(2,1)S(1)} %dynamic-slice_bitcast_fusion.6), channel_id=1, source_target_pairs={{0,8},{8,0},{16,24},{24,16},{1,9},{9,1},{17,25},{25,17},{2,10},{10... | collective-permute-start | bytes 1990664 | tf_op jit(solution)/shard_map/ppermute | solution.py:912
  218.9 16.6 %collective-permute-start.13 = (bf16[4,216,384]{2,1,0:T(8,128)(2,1)S(1)}, bf16[4,216,384]{2,1,0:T(8,128)(2,1)S(1)}, u32[]{:S(2)}, u32[]{:S(2)}) collective-permute-start(bf16[4,216,384]{2,1,0:T(8,128)(2,1)S(1)} %dynamic-slice_bitcast_fusion.7), channel_id=1, source_target_pairs={{0,16},{8,24},{16,0},{24,8},{1,17},{9,25},{17,1},{25,9},{2,18},{10... | collective-permute-start | bytes 1990664 | tf_op jit(solution)/shard_map/ppermute | solution.py:912
  237.7 24.6 %collective-permute-start.16 = (bf16[216,768]{1,0:T(8,128)(2,1)S(1)}, bf16[216,768]{1,0:T(8,128)(2,1)S(1)}, u32[]{:S(2)}, u32[]{:S(2)}) collective-permute-start(bf16[216,768]{1,0:T(8,128)(2,1)S(1)} %get-tuple-element.212), channel_id=1, source_target_pairs={{0,2},{1,3},{2,0},{3,1},{4,6},{5,7},{6,4},{7,5},{8,10},{9,11},{10,... | collective-permute-start | bytes 995336 | tf_op jit(solution)/shard_map/ppermute | solution.py:920
  240.1 22.3 %collective-permute-start.18 = (bf16[216,768]{1,0:T(8,128)(2,1)S(1)}, bf16[216,768]{1,0:T(8,128)(2,1)S(1)}, u32[]{:S(2)}, u32[]{:S(2)}) collective-permute-start(bf16[216,768]{1,0:T(8,128)(2,1)S(1)} %get-tuple-element.213), channel_id=1, source_target_pairs={{0,6},{1,7},{2,4},{3,5},{4,2},{5,3},{6,0},{7,1},{8,14},{9,15},{10,... | collective-permute-start | bytes 995336 | tf_op jit(solution)/shard_map/ppermute | solution.py:920
  242.7 28.6 %collective-permute-start.17 = (bf16[216,768]{1,0:T(8,128)(2,1)S(1)}, bf16[216,768]{1,0:T(8,128)(2,1)S(1)}, u32[]{:S(2)}, u32[]{:S(2)}) collective-permute-start(bf16[216,768]{1,0:T(8,128)(2,1)S(1)} %get-tuple-element.214), channel_id=1, source_target_pairs={{0,4},{1,5},{2,6},{3,7},{4,0},{5,1},{6,2},{7,3},{8,12},{9,13},{10,... | collective-permute-start | bytes 995336 | tf_op jit(solution)/shard_map/ppermute | solution.py:920
  271.4 49.0 %collective-permute-start.25 = (bf16[216,768]{1,0:T(8,128)(2,1)S(1)}, bf16[216,768]{1,0:T(8,128)(2,1)S(1)}, u32[]{:S(2)}, u32[]{:S(2)}) collective-permute-start(bf16[216,768]{1,0:T(8,128)(2,1)S(1)} %fusion.12), channel_id=1, source_target_pairs={{0,24},{8,16},{16,8},{24,0},{1,25},{9,17},{17,9},{25,1},{2,26},{10... | collective-permute-start | bytes 995336 | tf_op jit(solution)/shard_map/ppermute | solution.py:926
  272.3 48.1 %collective-permute-start.24 = (bf16[216,768]{1,0:T(8,128)(2,1)S(1)}, bf16[216,768]{1,0:T(8,128)(2,1)S(1)}, u32[]{:S(2)}, u32[]{:S(2)}) collective-permute-start(bf16[216,768]{1,0:T(8,128)(2,1)S(1)} %fusion.12), channel_id=1, source_target_pairs={{0,16},{8,24},{16,0},{24,8},{1,17},{9,25},{17,1},{25,9},{2,18},{10... | collective-permute-start | bytes 995336 | tf_op jit(solution)/shard_map/ppermute | solution.py:926
  293.4 8.3 %collective-permute-start.26 = (bf16[4,24,1152]{2,1,0:T(8,128)(2,1)S(1)}, bf16[4,24,1152]{2,1,0:T(8,128)(2,1)S(1)}, u32[]{:S(2)}, u32[]{:S(2)}) collective-permute-start(bf16[4,24,1152]{2,1,0:T(8,128)(2,1)S(1)} %get-tuple-element.222), channel_id=1, source_target_pairs={{0,8},{8,0},{16,24},{24,16},{1,9},{9,1},{17,25},{25,17},{2,10},{10... | collective-permute-start | bytes 663560 | tf_op jit(solution)/shard_map/ppermute | solution.py:920
  294.9 11.4 %collective-permute-start.28 = (bf16[4,24,1152]{2,1,0:T(8,128)(2,1)S(1)}, bf16[4,24,1152]{2,1,0:T(8,128)(2,1)S(1)}, u32[]{:S(2)}, u32[]{:S(2)}) collective-permute-start(bf16[4,24,1152]{2,1,0:T(8,128)(2,1)S(1)} %get-tuple-element.223), channel_id=1, source_target_pairs={{0,24},{8,16},{16,8},{24,0},{1,25},{9,17},{17,9},{25,1},{2,26},{10... | collective-permute-start | bytes 663560 | tf_op jit(solution)/shard_map/ppermute | solution.py:920
  295.7 13.3 %collective-permute-start.27 = (bf16[4,24,1152]{2,1,0:T(8,128)(2,1)S(1)}, bf16[4,24,1152]{2,1,0:T(8,128)(2,1)S(1)}, u32[]{:S(2)}, u32[]{:S(2)}) collective-permute-start(bf16[4,24,1152]{2,1,0:T(8,128)(2,1)S(1)} %get-tuple-element.224), channel_id=1, source_target_pairs={{0,16},{8,24},{16,0},{24,8},{1,17},{9,25},{17,1},{25,9},{2,18},{10... | collective-permute-start | bytes 663560 | tf_op jit(solution)/shard_map/ppermute | solution.py:920
  301.7 7.5 %collective-permute-start.20 = (bf16[32,768]{1,0:T(8,128)(2,1)S(1)}, bf16[32,768]{1,0:T(8,128)(2,1)S(1)}, u32[]{:S(2)}, u32[]{:S(2)}) collective-permute-start(bf16[32,768]{1,0:T(8,128)(2,1)S(1)} %get-tuple-element.231), channel_id=1, source_target_pairs={{0,2},{1,3},{2,0},{3,1},{4,6},{5,7},{6,4},{7,5},{8,10},{9,11},{10,... | collective-permute-start | bytes 147464 | tf_op jit(solution)/shard_map/ppermute | solution.py:920
  309.0 6.3 %collective-permute-start.21 = (bf16[32,768]{1,0:T(8,128)(2,1)S(1)}, bf16[32,768]{1,0:T(8,128)(2,1)S(1)}, u32[]{:S(2)}, u32[]{:S(2)}) collective-permute-start(bf16[32,768]{1,0:T(8,128)(2,1)S(1)} %get-tuple-element.233), channel_id=1, source_target_pairs={{0,4},{1,5},{2,6},{3,7},{4,0},{5,1},{6,2},{7,3},{8,12},{9,13},{10,... | collective-permute-start | bytes 147464 | tf_op jit(solution)/shard_map/ppermute | solution.py:920
  309.1 7.1 %collective-permute-start.29 = (bf16[24,1152]{1,0:T(8,128)(2,1)S(1)}, bf16[24,1152]{1,0:T(8,128)(2,1)S(1)}, u32[]{:S(2)}, u32[]{:S(2)}) collective-permute-start(bf16[24,1152]{1,0:T(8,128)(2,1)S(1)} %get-tuple-element.228), channel_id=1, source_target_pairs={{0,2},{1,3},{2,0},{3,1},{4,6},{5,7},{6,4},{7,5},{8,10},{9,11},{10,... | collective-permute-start | bytes 165896 | tf_op jit(solution)/shard_map/ppermute | solution.py:920
  316.2 7.5 %collective-permute-start.23 = (bf16[216,768]{1,0:T(8,128)(2,1)S(1)}, bf16[216,768]{1,0:T(8,128)(2,1)S(1)}, u32[]{:S(2)}, u32[]{:S(2)}) collective-permute-start(bf16[216,768]{1,0:T(8,128)(2,1)S(1)} %fusion.12), channel_id=1, source_target_pairs={{0,8},{8,0},{16,24},{24,16},{1,9},{9,1},{17,25},{25,17},{2,10},{10... | collective-permute-start | bytes 995336 | tf_op jit(solution)/shard_map/ppermute | solution.py:926
  324.5 7.1 %collective-permute-start.34 = (bf16[24,1152]{1,0:T(8,128)(2,1)S(1)}, bf16[24,1152]{1,0:T(8,128)(2,1)S(1)}, u32[]{:S(2)}, u32[]{:S(2)}) collective-permute-start(bf16[24,1152]{1,0:T(8,128)(2,1)S(1)} %fusion.32), channel_id=1, source_target_pairs={{0,24},{8,16},{16,8},{24,0},{1,25},{9,17},{17,9},{25,1},{2,26},{10... | collective-permute-start | bytes 165896 | tf_op jit(solution)/shard_map/ppermute | solution.py:926
  332.1 8.8 %collective-permute-start.36 = (bf16[4,24,1280]{2,1,0:T(8,128)(2,1)S(1)}, bf16[4,24,1280]{2,1,0:T(8,128)(2,1)S(1)}, u32[]{:S(2)}, u32[]{:S(2)}) collective-permute-start(bf16[4,24,1280]{2,1,0:T(8,128)(2,1)S(1)} %get-tuple-element.219), channel_id=1, source_target_pairs={{0,8},{8,0},{16,24},{24,16},{1,9},{9,1},{17,25},{25,17},{2,10},{10... | collective-permute-start | bytes 737288 | tf_op jit(solution)/shard_map/ppermute | solution.py:920
  333.6 12.9 %collective-permute-start.38 = (bf16[4,24,1280]{2,1,0:T(8,128)(2,1)S(1)}, bf16[4,24,1280]{2,1,0:T(8,128)(2,1)S(1)}, u32[]{:S(2)}, u32[]{:S(2)}) collective-permute-start(bf16[4,24,1280]{2,1,0:T(8,128)(2,1)S(1)} %get-tuple-element.220), channel_id=1, source_target_pairs={{0,24},{8,16},{16,8},{24,0},{1,25},{9,17},{17,9},{25,1},{2,26},{10... | collective-permute-start | bytes 737288 | tf_op jit(solution)/shard_map/ppermute | solution.py:920
  334.8 13.0 %collective-permute-start.37 = (bf16[4,24,1280]{2,1,0:T(8,128)(2,1)S(1)}, bf16[4,24,1280]{2,1,0:T(8,128)(2,1)S(1)}, u32[]{:S(2)}, u32[]{:S(2)}) collective-permute-start(bf16[4,24,1280]{2,1,0:T(8,128)(2,1)S(1)} %get-tuple-element.221), channel_id=1, source_target_pairs={{0,16},{8,24},{16,0},{24,8},{1,17},{9,25},{17,1},{25,9},{2,18},{10... | collective-permute-start | bytes 737288 | tf_op jit(solution)/shard_map/ppermute | solution.py:920
  350.3 6.0 %collective-permute-start.41 = (bf16[24,1280]{1,0:T(8,128)(2,1)S(1)}, bf16[24,1280]{1,0:T(8,128)(2,1)S(1)}, u32[]{:S(2)}, u32[]{:S(2)}) collective-permute-start(bf16[24,1280]{1,0:T(8,128)(2,1)S(1)} %get-tuple-element.226), channel_id=1, source_target_pairs={{0,6},{1,7},{2,4},{3,5},{4,2},{5,3},{6,0},{7,1},{8,14},{9,15},{10,... | collective-permute-start | bytes 184328 | tf_op jit(solution)/shard_map/ppermute | solution.py:920
  (31 other events, 162.5 us)
